TPU v7x, 32 devices: a whole 2x2x4 slice. The times are simulated.
32 devices in a mesh: section: 2 (over core), dp: 4 (over z), tensor: 4 (over y, x).
Axes of the slice: x: 2, y: 2, z: 4, core: 2. Of those that a mesh axis runs over, the one named last changes fastest.
Arguments:
- inputs: bfloat16 [2, 4096, 1536], P(None, ('dp', 'tensor')), may hold values from -6 to 6
- cotangent: float32 [2, 4096, 1536], P(None, ('dp', 'tensor')), may hold values from -6 to 6
- segments: int32 [2, 4, 1024], P(None, 'dp'), may hold values from 0 to 3, never falling along the last dimension, each value on 1 to 896 neighbouring positions
- routes: int32 [2, 2, 4096, 4], P('section', None, ('dp', 'tensor')), may hold values from 0 to 7, all different within a row; in each aligned block of 256 rows (0 to 255, 256 to 511, ..., all dimensions but the last counted through in order) at most 145 rows name the same one
- route_gates: float32 [2, 2, 4096, 4], P('section', None, ('dp', 'tensor')), may hold values from 0.1 to 0.4
- attn_gain: float32 [2, 1536], P('section'), may hold values from 0.5 to 1.5
- w_query: bfloat16 [2, 1536, 1536], P('section', None, 'tensor'), may hold values from -0.15625 to 0.15625
- key_weight: bfloat16 [2, 1536, 256], P('section'), may hold values from -0.15625 to 0.15625
- value_weight: bfloat16 [2, 1536, 256], P('section'), may hold values from -0.15625 to 0.15625
- w_out: bfloat16 [2, 1536, 1536], P('section', 'tensor'), may hold values from -0.625 to 0.625
- mixer_gain: float32 [2, 1536], P('section'), may hold values from 0.5 to 1.5
- w_gate: bfloat16 [2, 8, 1536, 768], P('section', 'dp', None, 'tensor'), may hold values from -0.15625 to 0.15625
- w_up: bfloat16 [2, 8, 1536, 768], P('section', 'dp', None, 'tensor'), may hold values from -0.15625 to 0.15625
- w_down: bfloat16 [2, 8, 768, 1536], P('section', 'dp', 'tensor'), may hold values from -0.4375 to 0.4375
Outputs:
- layer_outputs: bfloat16 [2, 2, 4096, 1536], P('section', None, ('dp', 'tensor'))
- input_grads: float32 [2, 2, 4096, 1536], P('section', None, ('dp', 'tensor'))
- grad_attn_gain: float32 [2, 1536], P('section')
- grad_w_query: float32 [2, 1536, 1536], P('section', None, 'tensor')
- grad_w_key: float32 [2, 1536, 256], P('section')
- grad_w_value: float32 [2, 1536, 256], P('section')
- grad_w_out: float32 [2, 1536, 1536], P('section', 'tensor')
- grad_mixer_gain: float32 [2, 1536], P('section')
- grad_w_gate: float32 [2, 8, 1536, 768], P('section', 'dp', None, 'tensor')
- grad_w_up: float32 [2, 8, 1536, 768], P('section', 'dp', None, 'tensor')
- grad_w_down: float32 [2, 8, 768, 1536], P('section', 'dp', 'tensor')
Inputs may be any that keep to these rules, and one draw needn't show every extreme that they name: `routes`: each row names 4 different experts. In every aligned block of 256 rows (one device's rows of one layer and micro-batch) no expert is named more than 145 times, and in some blocks one is named exactly 145 times. `segments`: along each sequence the numbers start at 0, never fall and rise by one at each new document; each sequence has 4 documents, the longest of exactly 896 tokens.
All inputs are finite; a program needn't handle non-finite values.
Results may differ from a plain program's by a relative error of at most 0.03.
Values may be sent and summed in bfloat16 or wider, within the bound.
A program may use at most 384 MiB of HBM per device.

v0:
```python
import jax
import jax.numpy as jnp
from jax import lax
from jax.sharding import PartitionSpec as P

S, D, T = "section", "dp", "tensor"
ST = (T, S)
HEADS = 12
GROUPS = 2
HEAD = 128
EPSILON = 1e-06
BF = jnp.bfloat16
F32 = jnp.float32


def dot(a, b, ca, cb):
    return lax.dot_general(a, b, ((ca, cb), ((), ())), preferred_element_type=F32)


def partner(values):
    return lax.ppermute(values, S, [(0, 1), (1, 0)])


def both(first, own):
    other = partner(own)
    return jnp.where(first, own, other), jnp.where(first, other, own)


def halves(first, own):
    keep = jnp.where(first, own[0], own[1])
    got = partner(jnp.where(first, own[1], own[0]))
    return jnp.where(first, keep, got), jnp.where(first, got, keep)


def join(first, zero, one):
    keep = jnp.where(first, zero, one)
    got = partner(jnp.where(first, one, zero))
    return jnp.stack([jnp.where(first, keep, got), jnp.where(first, got, keep)])


def rope_tables(places):
    half = HEAD // 2
    rates = 10000.0 ** (-jnp.arange(half, dtype=F32) * 2.0 / HEAD)
    angles = places[:, None] * rates[None, :]
    cosine, sine = jnp.cos(angles), jnp.sin(angles)
    return jnp.concatenate([cosine, cosine], 1)[:, None], jnp.concatenate([-sine, sine], 1)[:, None]


def rotate(values, cosine, sine):
    half = HEAD // 2
    turned = jnp.concatenate([values[..., half:], values[..., :half]], -1)
    return values * cosine + turned * sine


def inverse_rms(values):
    return lax.rsqrt(jnp.mean(values * values, -1, keepdims=True) + EPSILON)


def norm_back(grad, values, gain):
    r = inverse_rms(values)
    n = values * r
    m = grad * gain
    return r * (m - n * jnp.mean(m * n, -1, keepdims=True)), jnp.sum(grad * n, 0)


def scores_of(queries, keys, allowed):
    scores = dot(queries, keys, (2,), (1,)) * HEAD ** (-0.5)
    return jnp.where(allowed[None], scores, -1e30)


def attend(queries, keys, values, allowed):
    outs, logs = [], []
    per = HEADS // GROUPS
    for g in range(GROUPS):
        scores = scores_of(queries[g * per : (g + 1) * per], keys[:, g], allowed)
        peak = jnp.max(scores, -1, keepdims=True)
        raised = jnp.exp(scores - peak)
        total = jnp.sum(raised, -1, keepdims=True)
        probs = (raised / total).astype(BF)
        outs.append(dot(probs, values[:, g], (2,), (0,)).astype(BF))
        logs.append(peak + jnp.log(total))
    return jnp.concatenate(outs), jnp.concatenate(logs)


def attend_back(queries, keys, values, allowed, logs, grad_out):
    per = HEADS // GROUPS
    scale = HEAD ** (-0.5)
    gq, gk, gv = [], [], []
    for g in range(GROUPS):
        part = slice(g * per, (g + 1) * per)
        q, go = queries[part], grad_out[part]
        soft = jnp.exp(scores_of(q, keys[:, g], allowed) - logs[part])
        grad_probs = dot(go, values[:, g], (2,), (1,))
        inner = jnp.sum(soft * grad_probs, -1, keepdims=True)
        gs = (soft * (grad_probs - inner)).astype(BF)
        gq.append(dot(gs, keys[:, g], (2,), (0,)) * scale)
        gk.append(dot(gs, q, (0, 1), (0, 1)) * scale)
        gv.append(dot(soft.astype(BF), go, (0, 1), (0, 1)))
    return jnp.concatenate(gq), jnp.stack(gk, 1), jnp.stack(gv, 1)


def layer_forward(x, p, c, last):
    rows, width = x.shape
    xf = x.astype(F32)
    normed = (xf * inverse_rms(xf) * p["ga"]).astype(BF)
    kv = dot(normed, p["kv"], (1,), (0,)).reshape(rows, 2 * GROUPS, HEAD)
    keys = rotate(kv[:, :GROUPS], *c["rope"])
    kv = jnp.concatenate([keys, kv[:, GROUPS:]], 1).astype(BF)
    kv = lax.all_gather(kv.reshape(rows, -1), T, axis=0, tiled=True).reshape(-1, 2 * GROUPS, HEAD)
    keys, values = kv[:, :GROUPS], kv[:, GROUPS:]
    queries = dot(normed, p["wq"], (1,), (1,)).reshape(rows, HEADS, HEAD)
    queries = rotate(queries, *c["rope"]).astype(BF).transpose(1, 0, 2)
    attended, logs = attend(queries, keys, values, c["allowed"])
    flat = attended.transpose(1, 0, 2).reshape(rows, HEADS * HEAD)
    hidden = xf + dot(flat, p["wo"], (1,), (0,))
    mixer = (hidden * inverse_rms(hidden) * p["gm"]).astype(BF)
    tokens = lax.all_gather(mixer, D, axis=0, tiled=True)
    gate = dot(tokens, p["wg"], (1,), (3,))
    up = dot(tokens, p["wu"], (1,), (3,))
    act = (jax.nn.silu(gate) * up * p["share"]).astype(BF)
    part = dot(act, p["wd"], (1, 2, 3), (0, 1, 2)).astype(BF)
    y = hidden + lax.psum_scatter(part, D, scatter_dimension=0, tiled=True).astype(F32)
    kept = dict(
        xf=xf, normed=normed, keys=keys, values=values, queries=queries, logs=logs, flat=flat,
        hidden=hidden, tokens=tokens, gate=gate, up=up, act=act,
    )
    return y.astype(BF), kept


def layer_backward(grad, grad_all, k, p, c):
    rows, width = grad.shape
    gate, up, share = k["gate"], k["up"], p["share"]
    grad_act = dot(grad_all, p["wd"], (1,), (3,)) * share
    gw_down = dot(k["act"], grad_all, (0,), (0,)).astype(BF)
    sig = jax.nn.sigmoid(gate)
    grad_gate = (grad_act * up * sig * (1.0 + gate * (1.0 - sig))).astype(BF)
    grad_up = (grad_act * gate * sig).astype(BF)
    mixed = dot(grad_gate, p["wg"], (1, 2, 3), (0, 1, 2)) + dot(grad_up, p["wu"], (1, 2, 3), (0, 1, 2))
    gw_gate = dot(grad_gate, k["tokens"], (0,), (0,)).astype(BF)
    gw_up = dot(grad_up, k["tokens"], (0,), (0,)).astype(BF)
    grad_mixer = lax.psum_scatter(mixed.astype(BF), D, scatter_dimension=0, tiled=True).astype(F32)
    more, g_gm = norm_back(grad_mixer, k["hidden"], p["gm"])
    grad_hidden = grad + more
    gao = grad_hidden.astype(BF)
    gw_out = dot(k["flat"], gao, (0,), (0,)).astype(BF)
    ga = dot(gao, p["wo"], (1,), (1,)).astype(BF).reshape(rows, HEADS, HEAD).transpose(1, 0, 2)
    gq, gk, gv = attend_back(k["queries"], k["keys"], k["values"], c["allowed"], k["logs"], ga)
    gkv = jnp.concatenate([gk, gv], 1).astype(BF).reshape(-1, 2 * GROUPS * HEAD)
    gkv = lax.psum_scatter(gkv, T, scatter_dimension=0, tiled=True).astype(F32)
    gkv = gkv.reshape(rows, 2 * GROUPS, HEAD)
    cosine, sine = c["rope"]
    gkv = jnp.concatenate([rotate(gkv[:, :GROUPS], cosine, -sine), gkv[:, GROUPS:]], 1)
    gkv = gkv.astype(BF).reshape(rows, -1)
    gql = rotate(gq.transpose(1, 0, 2), cosine, -sine).astype(BF).reshape(rows, p["wq"].shape[0], -1)
    grad_normed = dot(gql, p["wq"], (1, 2), (0, 2)) + dot(gkv, p["kv"], (1,), (1,))
    gw_q = dot(k["normed"], gql, (0,), (0,)).transpose(1, 0, 2).astype(BF)
    gw_kv = dot(k["normed"], gkv, (0,), (0,))
    more, g_ga = norm_back(grad_normed, k["xf"], p["ga"])
    grads = dict(wd=gw_down, wg=gw_gate, wu=gw_up, wo=gw_out, wq=gw_q, kv=gw_kv, gm=g_gm, ga=g_ga)
    return grad_hidden + more, grads


def on_device(
    inputs, cotangent, segments, routes, route_gates, attn_gain, w_query, key_weight,
    value_weight, w_out, mixer_gain, w_gate, w_up, w_down,
):
    section = lax.axis_index(S)
    first = section == 0
    at = lax.axis_index(T)
    group = lax.axis_size(T)
    rows, width = inputs.shape[1:]
    length = segments.shape[2]
    here = w_gate.shape[1]
    hidden = w_gate.shape[3]
    experts = lax.axis_size(D) * here
    pick = lambda a: jnp.where(first, a[0], a[1])
    x0 = pick(inputs)
    grad1 = pick(cotangent)
    segment = pick(segments)[0]

    named = routes[0][..., None] == jnp.arange(experts, dtype=jnp.int32)
    shares = jnp.sum(jnp.where(named, route_gates[0][..., None], 0.0), 2)
    keep = jnp.where(first, shares[0], shares[1])
    got = partner(jnp.where(first, shares[1], shares[0]))
    shares = jnp.stack([jnp.where(first, keep, got), jnp.where(first, got, keep)], 1)
    shares = lax.all_gather(shares, D, axis=0, tiled=True)
    shares = lax.dynamic_slice_in_dim(shares, lax.axis_index(D) * here, here, 2)

    queries_at = at * rows + jnp.arange(rows)
    mine = lax.dynamic_slice_in_dim(segment, at * rows, rows, 0)
    allowed = (jnp.arange(length)[None] <= queries_at[:, None]) & (mine[:, None] == segment[None])
    c = dict(rope=rope_tables(queries_at.astype(F32)), allowed=allowed)

    gather = lambda a: lax.all_gather(a, ST, axis=0, tiled=False)
    wq = halves(first, w_query[0].reshape(2, width // 2, -1))
    wo = halves(first, w_out[0].reshape(2, -1, width))
    g, u = (w[0].transpose(0, 2, 1) for w in (w_gate, w_up))
    ffn = halves(first, jnp.stack([g, u, w_down[0]], 1))
    kv = both(first, jnp.concatenate([key_weight[0], value_weight[0]], 1))
    ga = both(first, attn_gain)
    gm = both(first, mixer_gain)
    params = []
    for l in range(2):
        f = gather(ffn[l]).reshape(group, here, 3, hidden, width)
        q = gather(wq[l]).reshape(group, width, -1)
        o = gather(wo[l]).reshape(-1, width)
        share = shares[:, l]
        params.append(
            dict(
                wq=q, wo=o, kv=kv[l], ga=ga[l], gm=gm[l], wg=f[:, :, 0], wu=f[:, :, 1], wd=f[:, :, 2],
                share=share[:, None, :, None],
            )
        )
    y0, k0 = layer_forward(x0, params[0], c, False)
    y1, k1 = layer_forward(y0, params[1], c, True)
    spread = lambda a: lax.all_gather(a.astype(BF), D, axis=0, tiled=True)
    gx1, w1 = layer_backward(grad1, spread(grad1), k1, params[1], c)
    gb = gx1.astype(BF)
    gx0, w0 = layer_backward(gb.astype(F32), spread(gb), k0, params[0], c)

    def swap(zero, one):
        keep = jnp.where(first, zero, one)
        got = partner(jnp.where(first, one, zero))
        return jnp.stack([jnp.where(first, keep, got), jnp.where(first, got, keep)])

    outs = swap(y0, y1)
    input_grads = swap(gx0.astype(BF), gx1.astype(BF)).astype(F32)
    scatter = lambda a: lax.psum_scatter(a, ST, scatter_dimension=0, tiled=True)
    reduced = []
    for w in (w0, w1):
        f = jnp.stack([w["wg"], w["wu"], w["wd"]], 2)
        f = scatter(f.reshape(group * here, 3, hidden, width)).reshape(3, hidden, width)
        q = scatter(w["wq"].reshape(group * 2, width // 2, -1)).reshape(width // 2, -1)
        o = scatter(w["wo"].reshape(group * 2, -1, width)).reshape(-1, width)
        reduced.append((f, q, o))
    f, q, o = (join(first, a, b) for a, b in zip(*reduced))
    q, o = lax.psum((q.reshape(w_query.shape[1:]), o.reshape(w_out.shape[1:])), D)
    small = [jnp.where(first, w0[n], w1[n]) + partner(jnp.where(first, w1[n], w0[n])) for n in ("kv", "ga", "gm")]
    kv, ga, gm = lax.psum(tuple(small), (D, T))
    f = f.astype(F32)
    half = kv.shape[1] // 2
    return (
        outs[None], input_grads[None], ga.reshape(1, -1), q.astype(F32)[None], kv[None, :, :half],
        kv[None, :, half:], o.astype(F32)[None], gm.reshape(1, -1), f[:, 0].transpose(0, 2, 1)[None],
        f[:, 1].transpose(0, 2, 1)[None], f[:, 2][None],
    )


def solution(mesh):
    rows, layer, cols = P(None, (D, T), None), P(S, None, (D, T), None), P(S, D, None, T)
    in_specs = (
        rows, rows, P(None, D, None), layer, layer, P(S, None), P(S, None, T), P(S, None, None),
        P(S, None, None), P(S, T, None), P(S, None), cols, cols, P(S, D, T, None),
    )
    out_specs = (
        layer, layer, P(S, None), P(S, None, T), P(S, None, None), P(S, None, None), P(S, T, None),
        P(S, None), cols, cols, P(S, D, T, None),
    )
    return jax.shard_map(on_device, mesh=mesh, in_specs=in_specs, out_specs=out_specs, check_vma=False)
```

profile of v0, /device:TPU:0, one launch (start us, length us, event | category | flops | bytes accessed | tf_op | source)
XLA Modules:
  0.0 1832.9 jit_solution(14881300873281172044)
XLA Ops:
  31.7 23.3 %all-gather.31.cloned.1.call-done = bf16[6144,384]{1,0:T(8,128)(2,1)} async-done(((bf16[768,384]{1,0:T(8,128)(2,1)}), bf16[6144,384]{1,0:T(8,128)(2,1)}) %all-gather.31.cloned.1.call-update) | async-done | bytes 4718608 | tf_op jit(solution)/shard_map/all_gather | solution.py:194
  66.8 17.1 all-gather.19.cloned.1.call-done
  94.7 30.5 %all-gather.33.cloned.1.call-done = bf16[1536,1536]{1,0:T(8,128)(2,1)} async-done(((bf16[192,1536]{1,0:T(8,128)(2,1)}), bf16[1536,1536]{1,0:T(8,128)(2,1)}) %all-gather.33.cloned.1.call-update) | async-done | bytes 4718608 | tf_op jit(solution)/shard_map/all_gather | solution.py:194
  140.2 14.2 all_gather.65
  155.0 40.0 %all-gather.21.cloned.1.call-done = bf16[1024,1536]{1,0:T(8,128)(2,1)} async-done(((bf16[256,1536]{1,0:T(8,128)(2,1)}), bf16[1024,1536]{1,0:T(8,128)(2,1)}) %all-gather.21.cloned.1.call-update) | async-done | bytes 3145744 | tf_op jit(solution)/shard_map/all_gather | solution.py:117
  195.1 79.8 %all-gather.35.cloned.1.call-done = bf16[24,192,1536]{2,1,0:T(8,128)(2,1)} async-done(((bf16[3,192,1536]{2,1,0:T(8,128)(2,1)}), bf16[24,192,1536]{2,1,0:T(8,128)(2,1)}) %all-gather.35.cloned.1.call-update) | async-done | bytes 14155792 | tf_op jit(solution)/shard_map/all_gather | solution.py:194
  274.9 10.0 fusion.11
  284.9 10.0 multiply_convert_fusion.9
  304.2 59.6 %reduce-scatter.13.cloned.1.call-done = bf16[256,1536]{1,0:T(8,128)(2,1)} async-done(((bf16[1024,1536]{1,0:T(8,128)(2,1)}), bf16[256,1536]{1,0:T(8,128)(2,1)}) %reduce-scatter.13.cloned.1.call-update) | async-done | bytes 786448 | tf_op jit(solution)/shard_map/reduce_scatter | solution.py:122
  373.5 31.8 %all-gather.37.cloned.1.call-done = bf16[6144,384]{1,0:T(8,128)(2,1)} async-done(((bf16[768,384]{1,0:T(8,128)(2,1)}), bf16[6144,384]{1,0:T(8,128)(2,1)}) %all-gather.37.cloned.1.call-update) | async-done | bytes 4718608 | tf_op jit(solution)/shard_map/all_gather | solution.py:194
  417.1 17.1 all-gather.23.cloned.1.call-done
  445.1 30.0 %all-gather.39.cloned.1.call-done = bf16[1536,1536]{1,0:T(8,128)(2,1)} async-done(((bf16[192,1536]{1,0:T(8,128)(2,1)}), bf16[1536,1536]{1,0:T(8,128)(2,1)}) %all-gather.39.cloned.1.call-update) | async-done | bytes 4718608 | tf_op jit(solution)/shard_map/all_gather | solution.py:194
  480.7 59.9 %all-gather.27.cloned.1.call-done = bf16[1024,1536]{1,0:T(8,128)(2,1)} async-done(((bf16[256,1536]{1,0:T(8,128)(2,1)}), bf16[1024,1536]{1,0:T(8,128)(2,1)}) %all-gather.27.cloned.1.call-update) | async-done | bytes 3145744 | tf_op jit(solution)/shard_map/all_gather | solution.py:216
  540.6 79.9 %all-gather.41.cloned.1.call-done = bf16[24,192,1536]{2,1,0:T(8,128)(2,1)} async-done(((bf16[3,192,1536]{2,1,0:T(8,128)(2,1)}), bf16[24,192,1536]{2,1,0:T(8,128)(2,1)}) %all-gather.41.cloned.1.call-update) | async-done | bytes 14155792 | tf_op jit(solution)/shard_map/all_gather | solution.py:194
  620.5 9.9 fusion.17
  630.4 55.7 %all-gather.25.cloned.1.call-done = bf16[1024,1536]{1,0:T(8,128)(2,1)} async-done(((bf16[256,1536]{1,0:T(8,128)(2,1)}), bf16[1024,1536]{1,0:T(8,128)(2,1)}) %all-gather.25.cloned.1.call-update) | async-done | bytes 3145744 | tf_op jit(solution)/shard_map/all_gather | solution.py:117
  686.1 10.0 fusion.16
  696.1 14.0 multiply_convert_fusion.6
  725.3 58.4 %reduce-scatter.17.cloned.1.call-done = bf16[256,1536]{1,0:T(8,128)(2,1)} async-done(((bf16[1024,1536]{1,0:T(8,128)(2,1)}), bf16[256,1536]{1,0:T(8,128)(2,1)}) %reduce-scatter.17.cloned.1.call-update) | async-done | bytes 786448 | tf_op jit(solution)/shard_map/reduce_scatter | solution.py:141
  820.9 22.2 %reduce-scatter.19.cloned.1.call-done = bf16[256,512]{0,1:T(8,128)(2,1)} async-done(((bf16[1024,512]{0,1:T(8,128)(2,1)}), bf16[256,512]{0,1:T(8,128)(2,1)}) %reduce-scatter.19.cloned.1.call-update) | async-done | bytes 262160 | tf_op jit(solution)/shard_map/reduce_scatter | solution.py:149
  854.6 63.6 %all-gather.29.cloned.1.call-done = bf16[1024,1536]{1,0:T(8,128)(2,1)} async-done(((bf16[256,1536]{1,0:T(8,128)(2,1)}), bf16[1024,1536]{1,0:T(8,128)(2,1)}) %all-gather.29.cloned.1.call-update) | async-done | bytes 3145744 | tf_op jit(solution)/shard_map/all_gather | solution.py:216
  918.2 11.9 multiply_convert_fusion.2
  949.1 58.4 %reduce-scatter.21.cloned.1.call-done = bf16[256,1536]{1,0:T(8,128)(2,1)} async-done(((bf16[1024,1536]{1,0:T(8,128)(2,1)}), bf16[256,1536]{1,0:T(8,128)(2,1)}) %reduce-scatter.21.cloned.1.call-update) | async-done | bytes 786448 | tf_op jit(solution)/shard_map/reduce_scatter | solution.py:141
  1152.9 32.0 %reduce-scatter.31.cloned.1.call-done = bf16[1,192,1536]{2,1,0:T(8,128)(2,1)} async-done(((bf16[8,192,1536]{2,1,0:T(8,128)(2,1)}), bf16[1,192,1536]{2,1,0:T(8,128)(2,1)}) %reduce-scatter.31.cloned.1.call-update) | async-done | bytes 589840 | tf_op jit(solution)/shard_map/reduce_scatter | solution.py:228
  1184.9 57.6 %reduce-scatter.29.cloned.1.call-done = bf16[1,192,1536]{2,1,0:T(8,128)(2,1)} async-done(((bf16[8,192,1536]{2,1,0:T(8,128)(2,1)}), bf16[1,192,1536]{2,1,0:T(8,128)(2,1)}) %reduce-scatter.29.cloned.1.call-update) | async-done | bytes 589840 | tf_op jit(solution)/shard_map/reduce_scatter | solution.py:228
  1244.4 55.4 %reduce-scatter.27.cloned.1.call-done = bf16[1,768,384]{2,1,0:T(8,128)(2,1)} async-done(((bf16[8,768,384]{2,1,0:T(8,128)(2,1)}), bf16[1,768,384]{2,1,0:T(8,128)(2,1)}) %reduce-scatter.27.cloned.1.call-update) | async-done | bytes 589840 | tf_op jit(solution)/shard_map/reduce_scatter | solution.py:228
  1299.8 57.7 %reduce-scatter.25.cloned.1.call-done = bf16[1,768,384]{2,1,0:T(8,128)(2,1)} async-done(((bf16[8,768,384]{2,1,0:T(8,128)(2,1)}), bf16[1,768,384]{2,1,0:T(8,128)(2,1)}) %reduce-scatter.25.cloned.1.call-update) | async-done | bytes 589840 | tf_op jit(solution)/shard_map/reduce_scatter | solution.py:228
  1366.2 95.7 %reduce-scatter.35.cloned.1.call-done = bf16[1,3,192,1536]{3,2,1,0:T(8,128)(2,1)} async-done(((bf16[8,3,192,1536]{3,2,1,0:T(8,128)(2,1)}), bf16[1,3,192,1536]{3,2,1,0:T(8,128)(2,1)}) %reduce-scatter.35.cloned.1.call-update) | async-done | bytes 1769488 | tf_op jit(solution)/shard_map/reduce_scatter | solution.py:228
  1461.9 104.2 %reduce-scatter.33.cloned.1.call-done = bf16[1,3,192,1536]{3,2,1,0:T(8,128)(2,1)} async-done(((bf16[8,3,192,1536]{3,2,1,0:T(8,128)(2,1)}), bf16[1,3,192,1536]{3,2,1,0:T(8,128)(2,1)}) %reduce-scatter.33.cloned.1.call-update) | async-done | bytes 1769488 | tf_op jit(solution)/shard_map/reduce_scatter | solution.py:228
  1569.1 77.4 %all-reduce = (f32[1,1536]{1,0:T(1,128)}, f32[1,1536]{1,0:T(1,128)}) all-reduce(f32[1,1536]{1,0:T(1,128)S(1)} %reshape.523, f32[1,1536]{1,0:T(1,128)S(1)} %reshape.530), channel_id=1, replica_groups=mesh['section'=2,'dp'=4,'tensor'=4] {'dp','tensor'}, use_global_device_ids=true, to_apply=%region_29.30 | all-reduce | flops 3072 | bytes 24576 | tf_op jit(solution)/shard_map/psum | solution.py:239
  1649.6 69.7 %all-reduce.5.cloned.1.call-done = f32[1536,512]{1,0:T(8,128)} async-done(((f32[1536,512]{1,0:T(8,128)}), f32[1536,512]{1,0:T(8,128)}) %all-reduce.5.cloned.1.call-update) | async-done | bytes 3145744 | tf_op jit(solution)/shard_map/psum | solution.py:239
  1723.1 94.3 %all-reduce.7.cloned.1.call-done = (bf16[1,1536,384]{2,1,0:T(8,128)(2,1)}, bf16[1,384,1536]{2,1,0:T(8,128)(2,1)}) async-done(((bf16[1,1536,384]{2,1,0:T(8,128)(2,1)}, bf16[1,384,1536]{2,1,0:T(8,128)(2,1)}), (bf16[1,1536,384]{2,1,0:T(8,128)(2,1)}, bf16[1,384,1536]{2,1,0:T(8,128)(2,1)})) %all-reduce.7.cloned.1.call-update) | async-done | bytes 2359312 | tf_op jit(solution)/shard_map/psum | solution.py:237
  (516 shorter events, 365.2 us)
Async XLA Ops:
  7.2 47.7 %all-gather.31.cloned.1.call-start = ((), (), s32[]{:S(2)}) async-start(), calls=%async_computation.31 | async-start | bytes 5308416 | tf_op jit(solution)/shard_map/all_gather | solution.py:194
  13.3 70.6 %all-gather.19.cloned.1.call-start = ((), (), s32[]{:S(2)}) async-start(), calls=%async_computation.12 | async-start | bytes 1310720 | tf_op jit(solution)/shard_map/all_gather | solution.py:109
  25.4 99.9 %all-gather.33.cloned.1.call-start = ((), (), s32[]{:S(2)}) async-start(), calls=%async_computation.32 | async-start | bytes 5308416 | tf_op jit(solution)/shard_map/all_gather | solution.py:194
  29.1 166.0 %all-gather.21.cloned.1.call-start = ((), (), s32[]{:S(2)}) async-start(), calls=%async_computation.13 | async-start | bytes 3932160 | tf_op jit(solution)/shard_map/all_gather | solution.py:117
  130.5 144.4 %all-gather.35.cloned.1.call-start = ((), (), s32[]{:S(2)}) async-start(), calls=%async_computation.33 | async-start | bytes 15925248 | tf_op jit(solution)/shard_map/all_gather | solution.py:194
  138.8 225.0 %reduce-scatter.13.cloned.1.call-start = ((), (), s32[]{:S(2)}) async-start(), calls=%async_computation.14 | async-start | bytes 3932160 | tf_op jit(solution)/shard_map/reduce_scatter | solution.py:122
  303.4 101.8 %all-gather.37.cloned.1.call-start = ((), (), s32[]{:S(2)}) async-start(), calls=%async_computation.34 | async-start | bytes 5308416 | tf_op jit(solution)/shard_map/all_gather | solution.py:194
  304.2 130.0 %all-gather.23.cloned.1.call-start = ((), (), s32[]{:S(2)}) async-start(), calls=%async_computation.15 | async-start | bytes 1310720 | tf_op jit(solution)/shard_map/all_gather | solution.py:109
  368.8 106.3 %all-gather.39.cloned.1.call-start = ((), (), s32[]{:S(2)}) async-start(), calls=%async_computation.35 | async-start | bytes 5308416 | tf_op jit(solution)/shard_map/all_gather | solution.py:194
  369.5 171.1 %all-gather.27.cloned.1.call-start = ((), (), s32[]{:S(2)}) async-start(), calls=%async_computation.18 | async-start | bytes 3932160 | tf_op jit(solution)/shard_map/all_gather | solution.py:216
  372.5 248.1 %all-gather.41.cloned.1.call-start = ((), (), s32[]{:S(2)}) async-start(), calls=%async_computation.36 | async-start | bytes 15925248 | tf_op jit(solution)/shard_map/all_gather | solution.py:194
  373.2 312.8 %all-gather.25.cloned.1.call-start = ((), (), s32[]{:S(2)}) async-start(), calls=%async_computation.16 | async-start | bytes 3932160 | tf_op jit(solution)/shard_map/all_gather | solution.py:117
  480.2 303.4 %reduce-scatter.17.cloned.1.call-start = ((), (), s32[]{:S(2)}) async-start(), calls=%async_computation.19 | async-start | bytes 3932160 | tf_op jit(solution)/shard_map/reduce_scatter | solution.py:141
  724.6 118.5 %reduce-scatter.19.cloned.1.call-start = ((), (), s32[]{:S(2)}) async-start(), calls=%async_computation.20 | async-start | bytes 1310720 | tf_op jit(solution)/shard_map/reduce_scatter | solution.py:149
  815.2 102.9 %all-gather.29.cloned.1.call-start = ((), (), s32[]{:S(2)}) async-start(), calls=%async_computation.21 | async-start | bytes 3932160 | tf_op jit(solution)/shard_map/all_gather | solution.py:216
  854.5 153.0 %reduce-scatter.21.cloned.1.call-start = ((), (), s32[]{:S(2)}) async-start(), calls=%async_computation.22 | async-start | bytes 3932160 | tf_op jit(solution)/shard_map/reduce_scatter | solution.py:141
  948.4 173.4 %reduce-scatter.23.cloned.1.call-start = ((), (), s32[]{:S(2)}) async-start(), calls=%async_computation.23 | async-start | bytes 1310720 | tf_op jit(solution)/shard_map/reduce_scatter | solution.py:149
  1037.1 92.1 %reduce-scatter.15.cloned.1.call-start = ((), (), s32[]{:S(2)}) async-start(), calls=%async_computation.17 | async-start | bytes 3932160 | tf_op jit(solution)/shard_map/reduce_scatter | solution.py:122
  1046.5 138.4 %reduce-scatter.31.cloned.1.call-start = ((), (), s32[]{:S(2)}) async-start(), calls=%async_computation.28 | async-start | bytes 5308416 | tf_op jit(solution)/shard_map/reduce_scatter | solution.py:228
  1051.7 190.8 %reduce-scatter.29.cloned.1.call-start = ((), (), s32[]{:S(2)}) async-start(), calls=%async_computation.27 | async-start | bytes 5308416 | tf_op jit(solution)/shard_map/reduce_scatter | solution.py:228
  1056.9 243.0 %reduce-scatter.27.cloned.1.call-start = ((), (), s32[]{:S(2)}) async-start(), calls=%async_computation.25 | async-start | bytes 5308416 | tf_op jit(solution)/shard_map/reduce_scatter | solution.py:228
  1061.7 295.9 %reduce-scatter.25.cloned.1.call-start = ((), (), s32[]{:S(2)}) async-start(), calls=%async_computation.24 | async-start | bytes 5308416 | tf_op jit(solution)/shard_map/reduce_scatter | solution.py:228
  1072.4 389.5 %reduce-scatter.35.cloned.1.call-start = ((), (), s32[]{:S(2)}) async-start(), calls=%async_computation.30 | async-start | bytes 15925248 | tf_op jit(solution)/shard_map/reduce_scatter | solution.py:228
  1097.2 468.9 %reduce-scatter.33.cloned.1.call-start = ((), (), s32[]{:S(2)}) async-start(), calls=%async_computation.29 | async-start | bytes 15925248 | tf_op jit(solution)/shard_map/reduce_scatter | solution.py:228
  1121.8 597.5 %all-reduce.5.cloned.1.call-start = ((), (), s32[]{:S(2)}) async-start(), calls=%async_computation.26 | async-start | bytes 6291456 | tf_op jit(solution)/shard_map/psum | solution.py:239
  1129.2 9.4 collective-permute-start.11
  1137.4 431.6 %collective-permute-start.13 = (f32[1536]{0:T(1024)S(1)}, f32[1536]{0:T(1024)S(1)}, u32[]{:S(2)}, u32[]{:S(2)}) collective-permute-start(f32[1536]{0:T(1024)S(1)} %broadcast_select_fusion.21), channel_id=1, source_target_pairs={{0,16},{16,0},{1,17},{17,1},{2,18},{18,2},{3,19},{19,3},{4,20},{20... | collective-permute-start | bytes 18440 | tf_op jit(solution)/shard_map/ppermute | solution.py:21
  1145.8 671.6 %all-reduce.7.cloned.1.call-start = ((), (), s32[]{:S(2)}) async-start(), calls=%async_computation.37 | async-start | bytes 4718592 | tf_op jit(solution)/shard_map/psum | solution.py:237
  1152.1 417.0 %collective-permute-start.9 = (f32[1536]{0:T(1024)S(1)}, f32[1536]{0:T(1024)S(1)}, u32[]{:S(2)}, u32[]{:S(2)}) collective-permute-start(f32[1536]{0:T(1024)S(1)} %broadcast_select_fusion.22), channel_id=1, source_target_pairs={{0,16},{16,0},{1,17},{17,1},{2,18},{18,2},{3,19},{19,3},{4,20},{20... | collective-permute-start | bytes 18440 | tf_op jit(solution)/shard_map/ppermute | solution.py:21
  1244.4 119.4 %collective-permute-start.12 = (bf16[192,1536]{1,0:T(8,128)(2,1)}, bf16[192,1536]{1,0:T(8,128)(2,1)}, u32[]{:S(2)}, u32[]{:S(2)}) collective-permute-start(bf16[192,1536]{1,0:T(8,128)(2,1)} %select_bitcast_fusion.6), channel_id=1, source_target_pairs={{0,16},{16,0},{1,17},{17,1},{2,18},{18,2},{3,19},{19,3},{4,20},{20... | collective-permute-start | bytes 1769480 | tf_op jit(solution)/shard_map/ppermute | solution.py:21
  1362.1 284.4 %collective-permute-start.8 = (bf16[256,1536]{1,0:T(8,128)(2,1)}, bf16[256,1536]{1,0:T(8,128)(2,1)}, u32[]{:S(2)}, u32[]{:S(2)}) collective-permute-start(bf16[256,1536]{1,0:T(8,128)(2,1)} %get-tuple-element.27), channel_id=1, source_target_pairs={{0,16},{16,0},{1,17},{17,1},{2,18},{18,2},{3,19},{19,3},{4,20},{20... | collective-permute-start | bytes 2359304 | tf_op jit(solution)/shard_map/ppermute | solution.py:21
  1569.0 253.1 %collective-permute-start.14 = (bf16[3,192,1536]{2,1,0:T(8,128)(2,1)}, bf16[3,192,1536]{2,1,0:T(8,128)(2,1)S(1)}, u32[]{:S(2)}, u32[]{:S(2)}) collective-permute-start(bf16[3,192,1536]{2,1,0:T(8,128)(2,1)} %select_bitcast_fusion), channel_id=1, source_target_pairs={{0,16},{16,0},{1,17},{17,1},{2,18},{18,2},{3,19},{19,3},{4,20},{20... | collective-permute-start | bytes 5308424 | tf_op jit(solution)/shard_map/ppermute | solution.py:21
  (135 other events, 2718.1 us)
Sparse Core Ops, SparseCore 0:
  13.4 41.5 all-gather.30
  57.3 26.4 all-gather.18
  86.3 38.9 all-gather.32
  130.6 64.4 all-gather.20
  197.4 77.4 all-gather.34
  303.6 60.2 reduce-scatter.12
  366.3 38.9 all-gather.36
  407.7 26.5 all-gather.22
  436.1 38.9 all-gather.38
  477.1 63.4 all-gather.26
  543.1 77.4 all-gather.40
  622.5 63.4 all-gather.24
  724.7 58.8 reduce-scatter.16
  815.4 27.7 reduce-scatter.18
  854.6 63.4 all-gather.28
  948.6 58.8 reduce-scatter.20
  1037.2 27.7 reduce-scatter.22
  1067.2 60.2 reduce-scatter.14
  1130.9 53.9 reduce-scatter.30
  1188.6 53.8 reduce-scatter.28
  1245.9 53.8 reduce-scatter.26
  1303.7 53.8 reduce-scatter.24
  1361.2 100.7 reduce-scatter.34
  1465.4 100.7 reduce-scatter.32
  1571.7 147.5 all-reduce.4
  1722.3 95.0 all-reduce.6
where the time goes:
time: 1840 us; the launch traced here: 1830 us
  waiting for transfers between devices  1310 us (71%)
  matrix products  259 us (14%)
  other arithmetic  93.9 us (5%)
  blocking collectives  91.7 us (5%)
  local copies, waits for them, and re-layouts  54.2 us (3%)
    reduce_scatter x6, waiting for transfers between devices, on_device(): scatter = lambda a: lax.psum_scatter(a, ST, scatter_dimension=0, tiled=True)  403 us
    all_gather x6, waiting for transfers between devices, on_device(): gather = lambda a: lax.all_gather(a, ST, axis=0, tiled=False)  275 us
    dot_general x60, matrix products, dot(): lax.dot_general(a, b, ((ca, cb), ((), ())), preferred_element_type=F32)  259 us
    all_gather x2, waiting for transfers between devices, on_device(): spread = lambda a: lax.all_gather(a.astype(BF), D, axis=0, tiled=True)  124 us
    reduce_scatter x2, waiting for transfers between devices, layer_backward(): lax.psum_scatter(mixed.astype(BF), D, scatter_dimension=0, tiled=True)  117 us
    all_gather x2, waiting for transfers between devices, layer_forward(): tokens = lax.all_gather(mixer, D, axis=0, tiled=True)  95.7 us
    psum x1, waiting for transfers between devices, on_device(): lax.psum((q.reshape(w_query.shape[1:]), o.reshape(w_out.shape[1:])), D)  94.3 us
    psum x1, blocking collectives, on_device(): kv, ga, gm = lax.psum(tuple(small), (D, T))  77.4 us
  transfers between devices with their start and end apart: 41, of which 31 were waited for; matrix products, arithmetic and copies ran while one was open for 12% of the time, Pallas kernels for 0%

commit v1 on v0

v1 whole, which is shorter than its diff:
```python
import functools
import jax
import jax.numpy as jnp
from jax import lax
from jax.experimental import pallas as pl
from jax.experimental.pallas import tpu as pltpu
from jax.sharding import PartitionSpec as P

S, D, T = "section", "dp", "tensor"
HEADS = 12
GROUPS = 2
HEAD = 128
EPSILON = 1e-06
BF = jnp.bfloat16
F32 = jnp.float32


def dot(a, b, ca, cb):
    return lax.dot_general(a, b, ((ca, cb), ((), ())), preferred_element_type=F32)


def low(values):
    return lax.reduce_precision(values.astype(F32), 8, 7).astype(BF)


def partner(values):
    return lax.ppermute(values, S, [(0, 1), (1, 0)])


def both(first, own):
    other = partner(own)
    return jnp.where(first, own, other), jnp.where(first, other, own)


def swap(first, zero, one):
    keep = jnp.where(first, zero, one)
    got = partner(jnp.where(first, one, zero))
    return jnp.where(first, keep, got), jnp.where(first, got, keep)


def hop(values, bit):
    return lax.ppermute(values, T, [(i, i ^ bit) for i in range(lax.axis_size(T))])


def spread(piece, after):
    a, b = piece
    if after is not None:
        a, b, _ = lax.optimization_barrier((a, b, after))
    ax, by = hop(a, 1), hop(b, 2)
    ay = hop(jnp.stack([a, ax]), 2)
    bx = hop(jnp.stack([b, by]), 1)
    return [a, ax, ay[0], ay[1]], [b, bx[0], by, bx[1]], (ay, bx)


def add(*values):
    return low(sum(v.astype(F32) for v in values))


def reduce_spread(a, b):
    ra = hop(jnp.stack([a[1], a[3]]), 1)
    rb = hop(jnp.stack([b[2], b[3]]), 2)
    own_a = hop(add(a[2], ra[1]), 2)
    own_b = hop(add(b[1], rb[1]), 1)
    return add(a[0], ra[0], own_a), add(b[0], rb[0], own_b)


def sum_spread(a, b):
    a, b = add(a, hop(a, 1)), add(b, hop(b, 2))
    return add(a, hop(a, 2)), add(b, hop(b, 1))


def rope_tables(places):
    half = HEAD // 2
    rates = 10000.0 ** (-jnp.arange(half, dtype=F32) * 2.0 / HEAD)
    angles = places[:, None] * rates[None, :]
    cosine, sine = jnp.cos(angles), jnp.sin(angles)
    return jnp.concatenate([cosine, cosine], 1), jnp.concatenate([-sine, sine], 1)


def rotate(values, cosine, sine):
    half = HEAD // 2
    turned = jnp.concatenate([values[..., half:], values[..., :half]], -1)
    return values * cosine + turned * sine


def inverse_rms(values):
    return lax.rsqrt(jnp.mean(values * values, -1, keepdims=True) + EPSILON)


def norm_back(grad, values, gain):
    r = inverse_rms(values)
    n = values * r
    m = grad * gain
    return r * (m - n * jnp.mean(m * n, -1, keepdims=True)), jnp.sum(grad * n, 0)


MESH = pl.DeviceIdType.MESH
SMALL = 4
SUB = 4
VMEM_LIMIT = 48 * 1024 * 1024


def expert_kernel(n, forward, backward, *refs):
    refs = list(refs)
    take = lambda count: [refs.pop(0) for _ in range(count)]
    x, mine, other, share = take(4)
    grads_in = take(1)[0] if forward and backward else None
    saved = take(4) if not forward else None
    y = take(1)[0]
    outs = take(4) if not backward else None
    part_out = take(1)[0] if forward and backward else None
    gw_out = take(1)[0] if backward else None
    tok, part, got, w, gate, up, act = take(7)
    second = take(1)[0] if backward else None
    stage = take(1)[0] if backward else None
    tok_send, tok_recv, part_send, part_recv, w_sem, io_sem, save_sem = refs
    rows, width = x.shape
    sub = rows // SUB
    me = lax.axis_index(D)

    small = mine.shape[3]
    for i in range(3):
        for h, pieces in enumerate((mine, other)):
            for p in range(2):
                for r in range(4):
                    at = ((h * 2 + p) * 4 + r) * small
                    pltpu.make_async_copy(pieces.at[p, r, i], w.at[i, pl.ds(at, small)], w_sem.at[i]).start()
    loads = []
    if saved is not None:
        loads = [pltpu.make_async_copy(a, o, io_sem.at[i]) for i, (a, o) in enumerate(zip(saved, (gate, up, act, second)))]
    elif backward:
        loads = [pltpu.make_async_copy(grads_in, second, io_sem.at[0])]
    for load in loads:
        load.start()
    barrier = pltpu.get_barrier_semaphore()
    for step in (-1, 1):
        @pl.when((me + step >= 0) & (me + step < n))
        def _():
            pl.semaphore_signal(barrier, inc=1, device_id={D: me + step}, device_id_type=MESH)
    tok[me] = x[...]
    pl.semaphore_wait(barrier, jnp.where((me == 0) | (me == n - 1), 1, 2))

    def move(b, to, side):
        return pltpu.make_async_remote_copy(
            src_ref=tok.at[b], dst_ref=tok.at[b], send_sem=tok_send.at[side, b], recv_sem=tok_recv.at[b],
            device_id={D: to}, device_id_type=MESH,
        )

    def pass_sum(b, s, to, slot):
        at = pl.ds(pl.multiple_of(s * sub, sub), sub)
        return pltpu.make_async_remote_copy(
            src_ref=part.at[b, at], dst_ref=got.at[slot, at], send_sem=part_send.at[b, s],
            recv_sem=part_recv.at[slot, s], device_id={D: to}, device_id_type=MESH,
        )

    def right(b, s):
        return pass_sum(b, s, me + 1, b)

    def left(b, s):
        return pass_sum(b, s, me - 1, jnp.where(b == me - 1, n, b))

    def arrived(b, s, slot):
        pass_sum(b, s, me, slot).wait_recv()

    chunk = 256
    steps = width // chunk

    def chunked(body):
        def step(c, carry):
            body(pl.ds(pl.multiple_of(c * chunk, chunk), chunk), c)
            return carry
        lax.fori_loop(0, steps, step, 0)

    def run(b):
        values = tok.at[b]

        def scale(c):
            s = share[c * 2 // steps, b]
            return jnp.concatenate([s, s], 1)

        if forward:
            def ahead(cols, c):
                gt = dot(values[...], w[0, cols], (1,), (1,))
                u = dot(values[...], w[1, cols], (1,), (1,))
                gate[b, :, cols] = gt.astype(BF)
                up[b, :, cols] = u.astype(BF)
                act[b, :, cols] = (gt * jax.nn.sigmoid(gt) * u * scale(c)).astype(BF)

            chunked(ahead)

            def down(cols, c):
                part[b, :, cols] = dot(act[b], w[2, :, cols], (1,), (0,)).astype(BF)

            chunked(down)
            if not backward:
                for i, (a, o) in enumerate(zip((tok, act, gate, up), outs)):
                    pltpu.make_async_copy(a.at[b], o.at[b], save_sem.at[i, b]).start()
            else:
                save = pltpu.make_async_copy(part.at[b], part_out.at[b], save_sem.at[0, b])
                save.start()
                save.wait()
        if backward:
            source = second.at[b] if forward else values

            def back(cols, c):
                da = dot(source[...], w[2, cols], (1,), (1,)) * scale(c)
                gt, u = gate[b, :, cols].astype(F32), up[b, :, cols].astype(F32)
                sig = jax.nn.sigmoid(gt)
                gate[b, :, cols] = (da * u * sig * (1.0 + gt * (1.0 - sig))).astype(BF)
                up[b, :, cols] = (da * gt * sig).astype(BF)

            chunked(back)

            def mix(cols, c):
                total = dot(gate[b], w[0, :, cols], (1,), (0,)) + dot(up[b], w[1, :, cols], (1,), (0,))
                part[b, :, cols] = total.astype(BF)

            chunked(mix)

    def turn(i, carry):
        d = (i + 1) // 2
        b = me + jnp.where(i % 2 == 1, d, -d)

        @pl.when((b >= 0) & (b < n))
        def _():
            @pl.when(i > 0)
            def _():
                move(b, me, 0).wait_recv()

            @pl.when((me < n - 1) & (b <= me))
            def _():
                move(b, me + 1, 0).start()

            @pl.when((me > 0) & (b >= me))
            def _():
                move(b, me - 1, 1).start()

            @pl.when(i == 0)
            def _():
                for k in range(3):
                    pltpu.make_async_copy(w.at[k], w.at[k], w_sem.at[k]).wait()
                for load in loads:
                    load.wait()

            run(b)

            @pl.when((b > me) & (me == 0))
            def _():
                for s in range(SUB):
                    right(b, s).start()

            @pl.when((b < me) & (me == n - 1))
            def _():
                for s in range(SUB):
                    left(b, s).start()

        return carry

    lax.fori_loop(0, 2 * n - 1, turn, 0)

    piece = 256
    slices = width // piece
    total = 3 * slices

    def save_slice(k, slot):
        at = pl.ds(pl.multiple_of(k % slices * piece, piece), piece)
        return pltpu.make_async_copy(stage.at[slot], gw_out.at[k // slices, at], save_sem.at[1, slot])

    def weight_slice(k):
        slot = k % 2
        at = pl.ds(pl.multiple_of(k % slices * piece, piece), piece)

        @pl.when(k >= 2)
        def _():
            save_slice(k - 2, slot).wait()

        tokens, grads = (tok, second) if forward else (second, tok)
        for i, (a, v) in enumerate(((gate, tokens), (up, tokens), (act, grads))):
            @pl.when(k // slices == i)
            def _():
                lhs = jnp.concatenate([a[b, :, at] for b in range(n)], 0)
                for c in range(2):
                    cols = pl.ds(c * (width // 2), width // 2)
                    rhs = jnp.concatenate([v[b, :, cols] for b in range(n)], 0)
                    stage[slot, :, cols] = dot(lhs, rhs, (0,), (0,)).astype(BF)

        save_slice(k, slot).start()

    def add_rows(b, s, slot):
        at = pl.ds(pl.multiple_of(s * sub, sub), sub)
        part[b, at] = (part[b, at].astype(F32) + got[slot, at].astype(F32)).astype(BF)

    count = (n - 1) * SUB

    def relay(t, carry):
        q, s = 1 + t // SUB, t % SUB

        @pl.when((me > 0) & (q > me))
        def _():
            arrived(q, s, q)
            add_rows(q, s, q)
            right(q, s).start()

        @pl.when((me < n - 1) & (n - 1 - q < me))
        def _():
            b = n - 1 - q
            arrived(b, s, b)
            add_rows(b, s, b)
            left(b, s).start()

        if backward:
            def some(k, carry):
                weight_slice(k)
                return carry
            lax.fori_loop(t * total // count, (t + 1) * total // count, some, 0)
        return carry

    lax.fori_loop(0, count, relay, 0)
    y[...] = part[me].astype(F32)

    @pl.when(me > 0)
    def _():
        for s in range(SUB):
            arrived(me, s, me)
        y[...] += got[me].astype(F32)

    @pl.when(me < n - 1)
    def _():
        for s in range(SUB):
            arrived(me, s, n)
        y[...] += got[n].astype(F32)

    if backward:
        for k in (total - 2, total - 1):
            save_slice(k, k % 2).wait()
    for b in range(n):
        if not backward:
            for i, (a, o) in enumerate(zip((tok, act, gate, up), outs)):
                pltpu.make_async_copy(a.at[b], o.at[b], save_sem.at[i, b]).wait()

        @pl.when((me < n - 1) & (b <= me))
        def _():
            move(b, me + 1, 0).wait_send()

        @pl.when((me > 0) & (b >= me))
        def _():
            move(b, me - 1, 1).wait_send()

        @pl.when(b > me)
        def _():
            for s in range(SUB):
                right(b, s).wait_send()

        @pl.when(b < me)
        def _():
            for s in range(SUB):
                left(b, s).wait_send()


def experts(n, forward, backward, x, mine, other, share, *more):
    rows, width = x.shape
    hidden = mine.shape[3] * 16
    shape = lambda *dims: jax.ShapeDtypeStruct(dims, BF)
    whole, wide = shape(n, rows, width), shape(n, rows, hidden)
    out = [jax.ShapeDtypeStruct((rows, width), F32)]
    out += [] if backward else [whole, wide, wide, wide]
    out += [whole] if forward and backward else []
    out += [shape(3, hidden, width)] if backward else []
    room = lambda *dims: pltpu.VMEM(dims, BF)
    scratch = [room(n, rows, width), room(n, rows, width), room(n + 1, rows, width), room(3, hidden, width)]
    scratch += [room(n, rows, hidden)] * 3
    scratch += [room(n, rows, width), room(2, 256, width)] if backward else []
    dma = pltpu.SemaphoreType.DMA
    scratch += [dma((2, n)), dma((n,)), dma((n, SUB)), dma((n + 1, SUB)), dma((3,)), dma((4,)), dma((4, n))]
    vmem, far = pl.BlockSpec(memory_space=pltpu.VMEM), pl.BlockSpec(memory_space=pl.ANY)
    return pl.pallas_call(
        functools.partial(expert_kernel, n, forward, backward),
        out_shape=out,
        in_specs=[vmem, far, far, vmem] + [far] * len(more),
        out_specs=[vmem] + [far] * (len(out) - 1),
        scratch_shapes=scratch,
        compiler_params=pltpu.CompilerParams(
            collective_id=forward + 2 * backward, has_side_effects=True, vmem_limit_bytes=VMEM_LIMIT
        ),
        cost_estimate=pl.CostEstimate(flops=80 * 10**9, bytes_accessed=10**8, transcendentals=0),
    )(x, mine, other, share, *more)


def turn_head(values, cosine, sine):
    return values * cosine + pltpu.roll(values, HEAD // 2, 1) * sine


def head_group(i):
    own = i // 3
    return jnp.where(lax.axis_index(T) < 2, own, 1 - own)


def lanes(start, size=HEAD):
    return pl.ds(pl.multiple_of(start, HEAD), size)


def loop(count, body):
    def step(i, carry):
        body(i)
        return carry
    lax.fori_loop(0, count, step, 0)


def attend_kernel(x, normed, kv, bias, cosine, sine, wq, wo, gain, hidden, mixer, queries, flat, logs):
    pair = 2 * HEAD

    def heads(i):
        both = dot(normed[...], wq[lanes(i * pair, pair)], (1,), (1,))
        g = head_group(i)
        keys, values = kv[:, lanes(g * HEAD)], kv[:, lanes((GROUPS + g) * HEAD)]
        for j in range(2):
            at = lanes(i * pair + j * HEAD)
            q = turn_head(both[:, j * HEAD : (j + 1) * HEAD], cosine[...], sine[...]).astype(BF)
            queries[:, at] = q
            scores = dot(q, keys, (1,), (1,)) * HEAD ** (-0.5) + bias[...]
            peak = jnp.max(scores, 1, keepdims=True)
            raised = jnp.exp(scores - peak)
            total = jnp.sum(raised, 1, keepdims=True)
            probs = (raised * (1.0 / total)).astype(BF)
            flat[:, at] = dot(probs, values, (1,), (0,)).astype(BF)
            logs[:, at] = jnp.broadcast_to(peak + jnp.log(total), q.shape)

    loop(HEADS // 2, heads)

    def out(i):
        cols = lanes(i * pair, pair)
        hidden[:, cols] = x[:, cols].astype(F32) + dot(flat[...], wo[:, cols], (1,), (0,))

    loop(x.shape[1] // pair, out)
    h = hidden[...]
    mixer[...] = (h * inverse_rms(h) * gain[...]).astype(BF)


def attend_back_kernel(
    grad, grad_mixer, hidden, gain, wo, queries, kv, logs, bias, flat, cosine, sine,
    grad_hidden, gql, gkv, gwo, grad_gain, gao, ga, acc,
):
    pair = 2 * HEAD
    scale = HEAD ** (-0.5)
    h = hidden[...]
    r = inverse_rms(h)
    n = h * r
    grad_gain[...] = jnp.sum(grad_mixer[...] * n, 0, keepdims=True)
    m = grad_mixer[...] * gain[...]
    total = grad[...] + r * (m - n * jnp.mean(m * n, -1, keepdims=True))
    grad_hidden[...] = total
    gao[...] = total.astype(BF)
    acc[...] = jnp.zeros_like(acc)

    def heads(i):
        rows = lanes(i * pair, pair)
        ga[...] = dot(gao[...], wo[rows], (1,), (1,)).astype(BF)
        gwo[rows] = dot(flat[:, rows], gao[...], (0,), (0,)).astype(BF)
        g = head_group(i)
        key_at, value_at = lanes(g * HEAD), lanes((GROUPS + g) * HEAD)
        keys, values = kv[:, key_at], kv[:, value_at]
        for j in range(2):
            at = lanes(i * pair + j * HEAD)
            q, go = queries[:, at], ga[:, j * HEAD : (j + 1) * HEAD]
            scores = dot(q, keys, (1,), (1,)) * scale + bias[...]
            soft = jnp.exp(scores - logs[:, at][:, :1])
            grad_probs = dot(go, values, (1,), (1,))
            inner = jnp.sum(soft * grad_probs, 1, keepdims=True)
            gs = (soft * (grad_probs - inner)).astype(BF)
            gq = dot(gs, keys, (1,), (0,)) * scale
            gql[:, at] = turn_head(gq, cosine[...], -sine[...]).astype(BF)
            acc[:, key_at] += dot(gs, q, (0,), (0,)) * scale
            acc[:, value_at] += dot(soft.astype(BF), go, (0,), (0,))

    loop(HEADS // 2, heads)
    gkv[...] = acc[...].astype(BF)


def local_call(body, flops, out, scratch, *operands):
    return pl.pallas_call(
        body,
        out_shape=[jax.ShapeDtypeStruct(*o) for o in out],
        scratch_shapes=[pltpu.VMEM(*s) for s in scratch],
        compiler_params=pltpu.CompilerParams(vmem_limit_bytes=VMEM_LIMIT),
        cost_estimate=pl.CostEstimate(flops=flops, bytes_accessed=2 * 10**7, transcendentals=0),
    )(*operands)


def attention_forward(x, p, c):
    rows, width = x.shape
    xf = x.astype(F32)
    normed = low(xf * inverse_rms(xf) * p["ga"])
    kv = dot(normed, p["kv"], (1,), (0,)).reshape(rows, 2 * GROUPS, HEAD)
    cosine, sine = c["rope"]
    keys = rotate(kv[:, :GROUPS], cosine[:, None], sine[:, None])
    kv = low(jnp.concatenate([keys, kv[:, GROUPS:]], 1)).reshape(rows, -1)
    kv = jnp.concatenate([kv] + [hop(kv, r) for r in (1, 2, 3)])
    wide = (rows, HEADS * HEAD)
    hidden, mixer, queries, flat, logs = local_call(
        attend_kernel, 10**10, [((rows, width), F32), ((rows, width), BF), (wide, BF), (wide, BF), (wide, F32)], [],
        x, normed, kv, c["bias"], cosine, sine, p["wq"], p["wo"], p["gm"].reshape(1, -1),
    )
    kept = dict(x=x, normed=normed, kv=kv, queries=queries, logs=logs, flat=flat, hidden=hidden)
    return hidden, mixer, kept


def along(values):
    return lax.all_gather(low(values), D, axis=0, tiled=True)


def scatter_along(values):
    return lax.psum_scatter(low(values.reshape(-1, values.shape[-1])), D, scatter_dimension=0, tiled=True)


def weights_of(p):
    f = jnp.stack([p["mine"], p["other"]])
    return tuple(f[:, :, :, i].reshape(-1, f.shape[-1]) for i in range(3))


def share_of(p, hidden):
    return jnp.repeat(p["share"], hidden // 2, axis=1)


def mix_forward(mixer, p, n):
    if n <= SMALL:
        y, tokens, act, gate, up = experts(n, True, False, mixer, p["mine"], p["other"], p["wide"])
        return y, dict(tokens=tokens, act=act, gate=gate, up=up)
    wg, wu, wd = weights_of(p)
    tokens = along(mixer)
    gate, up = dot(tokens, wg, (1,), (1,)), dot(tokens, wu, (1,), (1,))
    act = low((jax.nn.silu(gate) * up * share_of(p, wd.shape[0])))
    y = scatter_along(dot(act, wd, (1,), (0,))).astype(F32)
    return y, dict(tokens=tokens, act=act, gate=low(gate), up=low(up))


def mix_backward(grad, k, p, n):
    if n <= SMALL:
        saved = (k["gate"], k["up"], k["act"], k["tokens"])
        return experts(n, False, True, grad, p["mine"], p["other"], p["wide"], *saved)
    wg, wu, wd = weights_of(p)
    grads = along(grad)
    da = dot(grads, wd, (1,), (1,)) * share_of(p, wd.shape[0])
    gate, up = k["gate"].astype(F32), k["up"].astype(F32)
    sig = jax.nn.sigmoid(gate)
    dg, du = low((da * up * sig * (1.0 + gate * (1.0 - sig)))), low((da * gate * sig))
    gm = scatter_along(dot(dg, wg, (1,), (0,)) + dot(du, wu, (1,), (0,))).astype(F32)
    flat = lambda v: v.reshape(-1, v.shape[-1])
    pairs = ((dg, k["tokens"]), (du, k["tokens"]), (k["act"], grads))
    return gm, jnp.stack([low(dot(flat(u), flat(v), (0,), (0,))) for u, v in pairs])


def mix_both(mixer, grad, p, n):
    if n <= SMALL:
        grads = along(grad).reshape(n, *grad.shape)
        gm, part, gw = experts(n, True, True, mixer, p["mine"], p["other"], p["wide"], grads)
        y = scatter_along(part).astype(F32)
        return y, gm, gw
    y, k = mix_forward(mixer, p, n)
    return (y,) + mix_backward(grad, k, p, n)


def expert_grads(gw):
    gw = gw.reshape(3, 2, 2, 4, -1, gw.shape[-1])
    gf = add(gw[:, 0], partner(gw[:, 1]))
    return reduce_spread(gf[:, 0].transpose(1, 0, 2, 3), gf[:, 1].transpose(1, 0, 2, 3))


def attention_backward(grad, grad_mixer, k, p, c, first):
    rows, width = grad.shape
    cosine, sine = c["rope"]
    wide, length = (rows, HEADS * HEAD), c["bias"].shape[1]
    grad_hidden, gql, gkv, gw_out, g_gm = local_call(
        attend_back_kernel, 2 * 10**10,
        [((rows, width), F32), (wide, BF), ((length, 2 * GROUPS * HEAD), BF), ((HEADS * HEAD, width), BF), ((1, width), F32)],
        [((rows, width), BF), ((rows, 2 * HEAD), BF), ((length, 2 * GROUPS * HEAD), F32)],
        grad, grad_mixer, k["hidden"], p["gm"].reshape(1, -1), p["wo"], k["queries"], k["kv"], k["logs"], c["bias"],
        k["flat"], cosine, sine,
    )
    gkv = gkv.reshape(4, rows, -1)
    gkv = gkv[0].astype(F32) + sum(hop(gkv[r], r).astype(F32) for r in (1, 2, 3))
    gkv = gkv.reshape(rows, 2 * GROUPS, HEAD)
    cosine, sine = cosine[:, None], sine[:, None]
    gkv = jnp.concatenate([rotate(gkv[:, :GROUPS], cosine, -sine), gkv[:, GROUPS:]], 1)
    gkv = low(gkv).reshape(rows, -1)
    grad_normed = dot(gql, p["wq"], (1,), (0,)) + dot(gkv, p["kv"], (1,), (1,))
    gw_q = low(dot(gql, k["normed"], (0,), (0,)))
    gw_kv = dot(gkv, k["normed"], (0,), (0,))
    more, g_ga = norm_back(grad_normed, k["x"].astype(F32), p["ga"])
    gat = add(jnp.where(first, gw_q, gw_out), partner(jnp.where(first, gw_out, gw_q)))
    gat = gat.reshape(4, 2, -1, width)
    gat = reduce_spread(gat[:, 0], gat[:, 1])
    gw_kv = gw_kv.reshape(2, -1, width)
    pad = jnp.zeros((31, width), F32)
    small = [low(jnp.concatenate([gw_kv[i], g[None], pad])) for i, g in enumerate((g_ga, g_gm[0]))]
    small = add(jnp.where(first, small[0], small[1]), partner(jnp.where(first, small[1], small[0])))
    small = small.reshape(2, -1, width)
    small = sum_spread(small[0], small[1])
    sums = lax.psum(jnp.concatenate(gat + small), D)
    return grad_hidden + more, sums


def on_device(
    inputs, cotangent, segments, routes, route_gates, attn_gain, w_query, key_weight,
    value_weight, w_out, mixer_gain, w_gate, w_up, w_down,
):
    section = lax.axis_index(S)
    first = section == 0
    at = lax.axis_index(T)
    rows, width = inputs.shape[1:]
    length = segments.shape[2]
    here = w_gate.shape[1]
    hidden = w_gate.shape[3]
    experts = lax.axis_size(D) * here
    mine = lambda a: lax.dynamic_index_in_dim(a, section, 0, False)
    theirs = lambda a: lax.dynamic_index_in_dim(a, 1 - section, 0, False)
    x0 = mine(inputs)
    grad1 = mine(cotangent)
    segment = mine(segments)[0]

    def halves(own):
        keep, got = mine(own), partner(theirs(own))
        return jnp.where(first, keep, got), jnp.where(first, got, keep)

    named = routes[0][..., None] == jnp.arange(experts, dtype=jnp.int32)
    shares = jnp.sum(jnp.where(named, route_gates[0][..., None], 0.0), 2)
    shares = jnp.stack(halves(shares), 1)
    shares = lax.all_gather(shares, D, axis=0, tiled=True)
    shares = lax.dynamic_slice_in_dim(shares, lax.axis_index(D) * here, here, 2)
    shares = jnp.where(first, shares, shares[:, :, ::-1])

    queries_at = at * rows + jnp.arange(rows)
    keys_at = jnp.concatenate([(at ^ r) * rows + jnp.arange(rows) for r in range(4)])
    key_segment = jnp.concatenate([lax.dynamic_slice_in_dim(segment, (at ^ r) * rows, rows, 0) for r in range(4)])
    allowed = (keys_at[None] <= queries_at[:, None]) & (key_segment[:rows, None] == key_segment[None])
    c = dict(rope=rope_tables(queries_at.astype(F32)), bias=jnp.where(allowed, 0.0, -1e30))

    attn = halves(jnp.stack([w_query[0].T, w_out[0]]).reshape(2, 2, -1, width))
    g, u = (w[0].transpose(0, 2, 1) for w in (w_gate, w_up))
    ffn = jnp.stack([g, u, w_down[0]], 1).reshape(here, 3, 2, -1, width).transpose(0, 2, 1, 3, 4)
    ffn = halves(ffn)
    kv = both(first, jnp.concatenate([key_weight[0], value_weight[0]], 1))
    ga = both(first, attn_gain)
    gm = both(first, mixer_gain)
    params = []
    after = None
    for l in range(2):
        a, b, after = spread(attn[l], after)
        got = jnp.concatenate([v for pair in zip(a, b) for v in pair])
        other = partner(got)
        q, o = jnp.where(first, got, other), jnp.where(first, other, got)
        a, b, after = spread(ffn[l], after)
        got = jnp.stack([jnp.stack(a), jnp.stack(b)])
        share = shares[:, l]
        wide = jnp.broadcast_to(share.T.reshape(here, -1, rows, 1), (here, share.shape[0] // rows, rows, HEAD))
        params.append(
            dict(wq=q, wo=o, kv=kv[l], ga=ga[l], gm=gm[l], mine=got, other=partner(got), share=share, wide=wide)
        )
    n = lax.axis_size(D)
    hidden0, mixer, k0 = attention_forward(x0, params[0], c)
    y, kept = mix_forward(mixer, params[0], n)
    y0 = low((hidden0 + y))
    hidden1, mixer, k1 = attention_forward(y0, params[1], c)
    y, gm, gw = mix_both(mixer, low(grad1), params[1], n)
    y1 = low((hidden1 + y))
    f1 = expert_grads(gw)
    gx1, s1 = attention_backward(grad1, gm, k1, params[1], c, first)
    gb = low(gx1)
    gm, gw = mix_backward(gb, kept, params[0], n)
    f0 = expert_grads(gw)
    gx0, s0 = attention_backward(gb.astype(F32), gm, k0, params[0], c, first)

    outs = jnp.stack(swap(first, y0, y1))
    input_grads = jnp.stack(swap(first, low(gx0), low(gx1))).astype(F32)
    f = jnp.stack(swap(first, jnp.concatenate(f0, 1), jnp.concatenate(f1, 1))).astype(F32)
    zero, one = swap(first, s0, s1)
    high = w_out.shape[1]
    q, o = zero[:high].astype(F32), one[:high].astype(F32)
    ka, vm = zero[high:].astype(F32), one[high:].astype(F32)
    few = GROUPS * HEAD
    return (
        outs[None], input_grads[None], ka[few : few + 1], q.T[None], ka[:few].T[None],
        vm[:few].T[None], o[None], vm[few : few + 1], f[:, 0].transpose(0, 2, 1)[None],
        f[:, 1].transpose(0, 2, 1)[None], f[:, 2][None],
    )


def solution(mesh):
    rows, layer, cols = P(None, (D, T), None), P(S, None, (D, T), None), P(S, D, None, T)
    in_specs = (
        rows, rows, P(None, D, None), layer, layer, P(S, None), P(S, None, T), P(S, None, None),
        P(S, None, None), P(S, T, None), P(S, None), cols, cols, P(S, D, T, None),
    )
    out_specs = (
        layer, layer, P(S, None), P(S, None, T), P(S, None, None), P(S, None, None), P(S, T, None),
        P(S, None), cols, cols, P(S, D, T, None),
    )
    return jax.shard_map(on_device, mesh=mesh, in_specs=in_specs, out_specs=out_specs, check_vma=False)
```

time: 1840 us -> 1240 us (0.67)
  waiting for transfers between devices: 1310 us -> 313 us
  Pallas kernels: 0 us -> 484 us
  matrix products: 259 us -> 26.9 us
  local copies, waits for them, and re-layouts: 54.2 us -> 151 us
  blocking collectives: 91.7 us -> 15.7 us
  other arithmetic: 93.9 us -> 167 us
  starting transfers between devices: 8.27 us -> 59.3 us
    reduce_scatter x12 -> x1, waiting for transfers between devices: 601 us -> 0.02 us  [scatter_along(): lax.psum_scatter(low(values.reshape(-1, values.shape[-1])), D, scatter_di...]
    all_gather x12 -> x1, waiting for transfers between devices: 529 us -> 0.01 us  [along(): return lax.all_gather(low(values), D, axis=0, tiled=True)]
    pallas_call x0 -> x7, Pallas kernels: none -> 484 us  [the longest x3 394 us: experts(): pl.pallas_call(functools.partial(expert_kernel, n, forward, backward), ou...]
    ppermute x0 -> x52, waiting for transfers between devices: none -> 245 us  [hop(): lax.ppermute(values, T, [(i, i ^ bit) for i in range(lax.axis_size(T))])]
    dot_general x60 -> x10, matrix products: 259 us -> 26.9 us  [dot(): lax.dot_general(a, b, ((ca, cb), ((), ())), preferred_element_type=F32)]
    psum x2 -> x1, waiting for transfers between devices: 164 us -> 67.9 us  [attention_backward(): sums = lax.psum(jnp.concatenate(gat + small), D)]
    psum x1 -> x0, blocking collectives: 77.4 us -> none  [on_device(): kv, ga, gm = lax.psum(tuple(small), (D, T))]
    convert_element_type x14 -> x39, other arithmetic: 15.6 us -> 77.9 us  [the longest x33 73.6 us: low(): return lax.reduce_precision(values.astype(F32), 8, 7).astype(BF)]
  transfers between devices with their start and end apart: 41 -> 75, of which waited for: 31 -> 27; matrix products, arithmetic and copies ran while one was open for 12% -> 25% of each run, Pallas kernels for 0% -> 27%
where the time goes in v1:
time: 1240 us; the launch traced here: 1230 us
  Pallas kernels  484 us (39%)
  waiting for transfers between devices  313 us (25%)
  other arithmetic  167 us (13%)
  local copies, waits for them, and re-layouts  151 us (12%)
  starting transfers between devices  59.3 us (5%)
  matrix products  26.9 us (2%)
  between operations  15.8 us (1%)
  blocking collectives  15.7 us (1%)
    pallas_call x3, Pallas kernels, experts(): pl.pallas_call(functools.partial(expert_kernel, n, forward, backward), ou...  394 us
    ppermute x52, waiting for transfers between devices, hop(): lax.ppermute(values, T, [(i, i ^ bit) for i in range(lax.axis_size(T))])  245 us
    pallas_call x4, Pallas kernels, local_call(): pl.pallas_call(body, out_shape=[jax.ShapeDtypeStruct(*o) for o in out], s...  89.5 us
    convert_element_type x33, other arithmetic, low(): return lax.reduce_precision(values.astype(F32), 8, 7).astype(BF)  73.6 us
    psum x1, waiting for transfers between devices, attention_backward(): sums = lax.psum(jnp.concatenate(gat + small), D)  67.9 us
    unnamed x304, local copies, waits for them, and re-layouts  59.4 us
    ppermute x52, starting transfers between devices, hop(): lax.ppermute(values, T, [(i, i ^ bit) for i in range(lax.axis_size(T))])  56.7 us
    dot_general x10, matrix products, dot(): lax.dot_general(a, b, ((ca, cb), ((), ())), preferred_element_type=F32)  26.9 us
  transfers between devices with their start and end apart: 75, of which 27 were waited for; matrix products, arithmetic and copies ran while one was open for 25% of the time, Pallas kernels for 27%

profile of v1, /device:TPU:0, one launch (start us, length us, event | category | flops | bytes accessed | tf_op | source)
XLA Modules:
  0.0 1232.2 jit_solution(15069067691626925900)
XLA Ops:
  27.0 15.7 %all_gather.6 = f32[1024,2,8]{0,2,1:T(8,128)S(1)} all-gather(f32[256,2,8]{0,2,1:T(8,128)S(1)} %pad_maximum_fusion.26), channel_id=1, replica_groups=mesh['section'=2,'dp'=4,'tensor'=4] {'dp'}, dimensions={0}, use_global_device_ids=true | all-gather | bytes 81920 | tf_op jit(solution)/shard_map/all_gather | solution.py:627
  75.6 18.4 %collective-permute-done.8 = bf16[2,192,1536]{2,1,0:T(8,128)(2,1)} collective-permute-done((bf16[2,192,1536]{2,1,0:T(8,128)(2,1)}, bf16[2,192,1536]{2,1,0:T(8,128)(2,1)}, u32[]{:S(2)}, u32[]{:S(2)}) %collective-permute-start.8) | collective-permute-done | bytes 1179680 | tf_op jit(solution)/shard_map/ppermute | solution.py:42
  107.9 13.3 %collective-permute-done.13 = bf16[3,96,1536]{2,1,0:T(8,128)(2,1)S(1)} collective-permute-done((bf16[3,96,1536]{2,1,0:T(8,128)(2,1)S(1)}, bf16[3,96,1536]{2,1,0:T(8,128)(2,1)S(1)}, u32[]{:S(2)}, u32[]{:S(2)}) %collective-permute-start.13) | collective-permute-done | bytes 884768 | tf_op jit(solution)/shard_map/ppermute | solution.py:42
  136.2 25.1 %collective-permute-done.14 = bf16[2,3,96,1536]{3,2,1,0:T(8,128)(2,1)S(1)} collective-permute-done((bf16[2,3,96,1536]{3,2,1,0:T(8,128)(2,1)S(1)}, bf16[2,3,96,1536]{3,2,1,0:T(8,128)(2,1)S(1)}, u32[]{:S(2)}, u32[]{:S(2)}) %collective-permute-start.14) | collective-permute-done | bytes 1769504 | tf_op jit(solution)/shard_map/ppermute | solution.py:42
  164.4 10.2 collective-permute-done.22
  184.8 16.2 %collective-permute-done.25 = bf16[2,192,1536]{2,1,0:T(8,128)(2,1)} collective-permute-done((bf16[2,192,1536]{2,1,0:T(8,128)(2,1)}, bf16[2,192,1536]{2,1,0:T(8,128)(2,1)}, u32[]{:S(2)}, u32[]{:S(2)}) %collective-permute-start.25) | collective-permute-done | bytes 1179680 | tf_op jit(solution)/shard_map/ppermute | solution.py:42
  215.0 6.9 collective-permute-done.27
  226.3 7.9 broadcast_select_fusion.4
  234.3 21.3 %shard_map.221 = (f32[256,1536]{1,0:T(8,128)}, bf16[256,1536]{1,0:T(8,128)(2,1)S(1)}, bf16[256,1536]{1,0:T(8,128)(2,1)S(1)}, bf16[256,1536]{1,0:T(8,128)(2,1)S(1)}, f32[256,1536]{1,0:T(8,128)}) custom-call(bf16[256,1536]{1,0:T(8,128)(2,1)S(1)} %get-tuple-element.137.x, bf16[256,1536]{1,0:T(8,128)(2,1)S(1)} %fusion.25.normed, ...), custom_call_target="tpu_custom_call" | custom-call | flops 10000000000 | bytes 20000000 | tf_op jit(solution)/shard_map/pallas_call | solution.py:480
  267.7 115.3 %shard_map.222 = (f32[256,1536]{1,0:T(8,128)S(1)}, bf16[4,256,1536]{2,1,0:T(8,128)(2,1)}, bf16[4,256,1536]{2,1,0:T(8,128)(2,1)}, bf16[4,256,1536]{2,1,0:T(8,128)(2,1)}, bf16[4,256,1536]{2,1,0:T(8,128)(2,1)}) custom-call(bf16[256,1536]{1,0:T(8,128)(2,1)S(1)} %get-tuple-element.48.refs_0_, bf16[2,4,3,96,1536]{4,3,2,1,0:T(8,128)(2,1)} %pad_maximum_fusion.refs_1_, ...), custom_call_target="tpu_custom_call" | custom-call | flops 80000000000 | bytes 100000000 | tf_op jit(solution)/shard_map/pallas_call | solution.py:376
  390.8 8.0 broadcast_select_fusion.2
  398.9 21.3 %shard_map.223 = (f32[256,1536]{1,0:T(8,128)}, bf16[256,1536]{1,0:T(8,128)(2,1)S(1)}, bf16[256,1536]{1,0:T(8,128)(2,1)S(1)}, bf16[256,1536]{1,0:T(8,128)(2,1)S(1)}, f32[256,1536]{1,0:T(8,128)}) custom-call(bf16[256,1536]{1,0:T(8,128)(2,1)S(1)} %get-tuple-element.135.x, bf16[256,1536]{1,0:T(8,128)(2,1)S(1)} %fusion.35.normed, ...), custom_call_target="tpu_custom_call" | custom-call | flops 10000000000 | bytes 20000000 | tf_op jit(solution)/shard_map/pallas_call | solution.py:480
  423.0 124.8 %shard_map.224 = (f32[256,1536]{1,0:T(8,128)S(1)}, bf16[4,256,1536]{2,1,0:T(8,128)(2,1)}, bf16[3,1536,1536]{2,1,0:T(8,128)(2,1)}) custom-call(bf16[256,1536]{1,0:T(8,128)(2,1)S(1)} %get-tuple-element.55.refs_0_, bf16[2,4,3,96,1536]{4,3,2,1,0:T(8,128)(2,1)} %pad_maximum_fusion.1.refs_1_, bf16[2,4,3,96,1536]{4,3,2,1,0:T(8,128)(2,1)} %collective-permute-done.31.refs_2_, ...), custom_call_target="tpu_custom_call" | custom-call | flops 80000000000 | bytes 100000000 | tf_op jit(solution)/shard_map/pallas_call | solution.py:376
  549.0 23.4 %shard_map.225 = (f32[256,1536]{1,0:T(8,128)}, bf16[256,1536]{1,0:T(8,128)(2,1)S(1)}, bf16[1024,512]{1,0:T(8,128)(2,1)S(1)}, bf16[1536,1536]{1,0:T(8,128)(2,1)}, f32[1,1536]{1,0:T(1,128)S(1)}) custom-call(f32[256,1536]{1,0:T(8,128)} %get-tuple-element.133.grad, f32[256,1536]{1,0:T(8,128)} %copy-done.28, f32[256,1536]{1,0:T(8,128)} %get-tuple-element.54.hidden, ...), custom_call_target="tpu_custom_call" | custom-call | flops 20000000000 | bytes 20000000 | tf_op jit(solution)/shard_map/pallas_call | solution.py:480
  578.3 8.3 fusion.110
  590.1 7.6 broadcast_select_fusion
  615.4 153.8 %shard_map.226 = (f32[256,1536]{1,0:T(8,128)S(1)}, bf16[3,1536,1536]{2,1,0:T(8,128)(2,1)}) custom-call(bf16[256,1536]{1,0:T(8,128)(2,1)S(1)} %get-tuple-element.127.refs_0_, bf16[2,4,3,96,1536]{4,3,2,1,0:T(8,128)(2,1)} %pad_maximum_fusion.refs_1_, bf16[2,4,3,96,1536]{4,3,2,1,0:T(8,128)(2,1)} %collective-permute-done.17.refs_2_, ...), custom_call_target="tpu_custom_call" | custom-call | flops 80000000000 | bytes 100000000 | tf_op jit(solution)/shard_map/pallas_call | solution.py:376
  770.4 10.7 fusion.109
  781.2 23.5 %shard_map.227 = (f32[256,1536]{1,0:T(8,128)}, bf16[256,1536]{1,0:T(8,128)(2,1)S(1)}, bf16[1024,512]{1,0:T(8,128)(2,1)S(1)}, bf16[1536,1536]{1,0:T(8,128)(2,1)}, f32[1,1536]{1,0:T(1,128)S(1)}) custom-call(f32[256,1536]{1,0:T(8,128)} %get-tuple-element.126.grad, f32[256,1536]{1,0:T(8,128)} %copy-done.27, f32[256,1536]{1,0:T(8,128)} %get-tuple-element.47.hidden, ...), custom_call_target="tpu_custom_call" | custom-call | flops 20000000000 | bytes 20000000 | tf_op jit(solution)/shard_map/pallas_call | solution.py:480
  845.8 10.4 collective-permute-done.46
  858.5 9.5 collective-permute-done.56
  871.2 7.7 collective-permute-done.47
  882.1 8.1 reduce-precision_convert_fusion
  896.7 7.9 reduce-precision_convert_fusion.2
  910.6 12.3 collective-permute-done.53
  980.6 10.5 fusion.1
  999.4 10.6 fusion.3
  1022.7 15.7 %collective-permute-done.67 = bf16[2,3,96,1536]{3,2,1,0:T(8,128)(2,1)} collective-permute-done((bf16[2,3,96,1536]{3,2,1,0:T(8,128)(2,1)}, bf16[2,3,96,1536]{3,2,1,0:T(8,128)(2,1)}, u32[]{:S(2)}, u32[]{:S(2)}) %collective-permute-start.67) | collective-permute-done | bytes 1769504 | tf_op jit(solution)/shard_map/ppermute | solution.py:42
  1043.7 32.6 %collective-permute-done.62 = bf16[2,3,96,1536]{3,2,1,0:T(8,128)(2,1)} collective-permute-done((bf16[2,3,96,1536]{3,2,1,0:T(8,128)(2,1)}, bf16[2,3,96,1536]{3,2,1,0:T(8,128)(2,1)}, u32[]{:S(2)}, u32[]{:S(2)}) %collective-permute-start.62) | collective-permute-done | bytes 1769504 | tf_op jit(solution)/shard_map/ppermute | solution.py:42
  1079.9 17.5 %collective-permute-done.68 = bf16[3,96,1536]{2,1,0:T(8,128)(2,1)S(1)} collective-permute-done((bf16[3,96,1536]{2,1,0:T(8,128)(2,1)S(1)}, bf16[3,96,1536]{2,1,0:T(8,128)(2,1)S(1)}, u32[]{:S(2)}, u32[]{:S(2)}) %collective-permute-start.68) | collective-permute-done | bytes 884768 | tf_op jit(solution)/shard_map/ppermute | solution.py:42
  1101.3 14.6 %collective-permute-done.63 = bf16[3,96,1536]{2,1,0:T(8,128)(2,1)S(1)} collective-permute-done((bf16[3,96,1536]{2,1,0:T(8,128)(2,1)S(1)}, bf16[3,96,1536]{2,1,0:T(8,128)(2,1)S(1)}, u32[]{:S(2)}, u32[]{:S(2)}) %collective-permute-start.63) | collective-permute-done | bytes 884768 | tf_op jit(solution)/shard_map/ppermute | solution.py:42
  1124.5 67.9 %all-reduce.3.cloned.1.call-done = (bf16[672,1536]{0,1:T(8,128)(2,1)}, bf16[672,1536]{0,1:T(8,128)(2,1)}) async-done(((bf16[672,1536]{0,1:T(8,128)(2,1)}, bf16[672,1536]{0,1:T(8,128)(2,1)}), (bf16[672,1536]{0,1:T(8,128)(2,1)}, bf16[672,1536]{0,1:T(8,128)(2,1)})) %all-reduce.3.cloned.1.call-update) | async-done | bytes 4128784 | tf_op jit(solution)/shard_map/psum | solution.py:598
  (629 shorter events, 359.4 us)
Async XLA Ops:
  7.2 414.9 %all-gather.2.cloned.1.call-start = ((), (), s32[]{:S(2)}) async-start(), calls=%async_computation.1 | async-start | bytes 3932160 | tf_op jit(solution)/shard_map/all_gather | solution.py:508
  14.5 57.4 %collective-permute-start.12 = (bf16[2,3,96,1536]{3,2,1,0:T(8,128)(2,1)}, bf16[2,3,96,1536]{3,2,1,0:T(8,128)(2,1)}, u32[]{:S(2)}, u32[]{:S(2)}) collective-permute-start(bf16[2,3,96,1536]{3,2,1,0:T(8,128)(2,1)} %dynamic-slice_bitcast_fusion), channel_id=1, source_target_pairs={{0,16},{16,0},{1,17},{17,1},{2,18},{18,2},{3,19},{19,3},{4,20},{20... | collective-permute-start | bytes 5308424 | tf_op jit(solution)/shard_map/ppermute | solution.py:27
  16.3 37.4 %collective-permute-start.1 = (bf16[1536,512]{1,0:T(8,128)(2,1)}, bf16[1536,512]{1,0:T(8,128)(2,1)}, u32[]{:S(2)}, u32[]{:S(2)}) collective-permute-start(bf16[1536,512]{1,0:T(8,128)(2,1)} %pad_maximum_fusion.13), channel_id=1, source_target_pairs={{0,16},{16,0},{1,17},{17,1},{2,18},{18,2},{3,19},{19,3},{4,20},{20... | collective-permute-start | bytes 4718600 | tf_op jit(solution)/shard_map/ppermute | solution.py:27
  20.1 936.5 %reduce-scatter.2.cloned.1.call-start = ((), (), s32[]{:S(2)}) async-start(), calls=%async_computation.2 | async-start | bytes 3932160 | tf_op jit(solution)/shard_map/reduce_scatter | solution.py:512
  69.8 34.0 %collective-permute-start.2 = (bf16[256,512]{1,0:T(8,128)(2,1)}, bf16[256,512]{1,0:T(8,128)(2,1)S(1)}, u32[]{:S(2)}, u32[]{:S(2)}) collective-permute-start(bf16[256,512]{1,0:T(8,128)(2,1)} %copy.184), channel_id=1, source_target_pairs={{0,1},{1,0},{2,3},{3,2},{4,5},{5,4},{6,7},{7,6},{8,9},{9,8},{10,11... | collective-permute-start | bytes 786440 | tf_op jit(solution)/shard_map/ppermute | solution.py:42
  70.3 37.5 %collective-permute-start.3 = (bf16[256,512]{1,0:T(8,128)(2,1)}, bf16[256,512]{1,0:T(8,128)(2,1)S(1)}, u32[]{:S(2)}, u32[]{:S(2)}) collective-permute-start(bf16[256,512]{1,0:T(8,128)(2,1)} %copy.184), channel_id=1, source_target_pairs={{0,2},{1,3},{2,0},{3,1},{4,6},{5,7},{6,4},{7,5},{8,10},{9,11},{10,... | collective-permute-start | bytes 786440 | tf_op jit(solution)/shard_map/ppermute | solution.py:42
  71.9 35.9 %collective-permute-start.4 = (bf16[256,512]{1,0:T(8,128)(2,1)}, bf16[256,512]{1,0:T(8,128)(2,1)S(1)}, u32[]{:S(2)}, u32[]{:S(2)}) collective-permute-start(bf16[256,512]{1,0:T(8,128)(2,1)} %copy.184), channel_id=1, source_target_pairs={{0,3},{1,2},{2,1},{3,0},{4,7},{5,6},{6,5},{7,4},{8,11},{9,10},{10,... | collective-permute-start | bytes 786440 | tf_op jit(solution)/shard_map/ppermute | solution.py:42
  121.4 40.0 %collective-permute-start.14 = (bf16[2,3,96,1536]{3,2,1,0:T(8,128)(2,1)S(1)}, bf16[2,3,96,1536]{3,2,1,0:T(8,128)(2,1)S(1)}, u32[]{:S(2)}, u32[]{:S(2)}) collective-permute-start(bf16[2,3,96,1536]{3,2,1,0:T(8,128)(2,1)S(1)} %pad_maximum_fusion.5), channel_id=1, source_target_pairs={{0,2},{1,3},{2,0},{3,1},{4,6},{5,7},{6,4},{7,5},{8,10},{9,11},{10,... | collective-permute-start | bytes 5308424 | tf_op jit(solution)/shard_map/ppermute | solution.py:42
  125.7 35.7 %collective-permute-start.16 = (bf16[2,3,96,1536]{3,2,1,0:T(8,128)(2,1)S(1)}, bf16[2,3,96,1536]{3,2,1,0:T(8,128)(2,1)S(1)}, u32[]{:S(2)}, u32[]{:S(2)}) collective-permute-start(bf16[2,3,96,1536]{3,2,1,0:T(8,128)(2,1)S(1)} %pad_maximum_fusion.6), channel_id=1, source_target_pairs={{0,1},{1,0},{2,3},{3,2},{4,5},{5,4},{6,7},{7,6},{8,9},{9,8},{10,11... | collective-permute-start | bytes 5308424 | tf_op jit(solution)/shard_map/ppermute | solution.py:42
  136.2 90.1 %collective-permute-start.10 = (bf16[1536,1536]{1,0:T(8,128)(2,1)}, bf16[1536,1536]{1,0:T(8,128)(2,1)}, u32[]{:S(2)}, u32[]{:S(2)}) collective-permute-start(bf16[1536,1536]{1,0:T(8,128)(2,1)} %fusion.85), channel_id=1, source_target_pairs={{0,16},{16,0},{1,17},{17,1},{2,18},{18,2},{3,19},{19,3},{4,20},{20... | collective-permute-start | bytes 14155784 | tf_op jit(solution)/shard_map/ppermute | solution.py:27
  182.2 85.1 %collective-permute-start.17 = (bf16[2,4,3,96,1536]{4,3,2,1,0:T(8,128)(2,1)}, bf16[2,4,3,96,1536]{4,3,2,1,0:T(8,128)(2,1)}, u32[]{:S(2)}, u32[]{:S(2)}) collective-permute-start(bf16[2,4,3,96,1536]{4,3,2,1,0:T(8,128)(2,1)} %pad_maximum_fusion.refs_1_), channel_id=1, source_target_pairs={{0,16},{16,0},{1,17},{17,1},{2,18},{18,2},{3,19},{19,3},{4,20},{20... | collective-permute-start | bytes 21233672 | tf_op jit(solution)/shard_map/ppermute | solution.py:27
  215.0 175.9 %collective-permute-start.26 = (bf16[1536,1536]{1,0:T(8,128)(2,1)}, bf16[1536,1536]{1,0:T(8,128)(2,1)}, u32[]{:S(2)}, u32[]{:S(2)}) collective-permute-start(bf16[1536,1536]{1,0:T(8,128)(2,1)} %fusion.81), channel_id=1, source_target_pairs={{0,16},{16,0},{1,17},{17,1},{2,18},{18,2},{3,19},{19,3},{4,20},{20... | collective-permute-start | bytes 14155784 | tf_op jit(solution)/shard_map/ppermute | solution.py:27
  222.8 35.7 %collective-permute-start.28 = (bf16[2,3,96,1536]{3,2,1,0:T(8,128)(2,1)S(1)}, bf16[2,3,96,1536]{3,2,1,0:T(8,128)(2,1)}, u32[]{:S(2)}, u32[]{:S(2)}) collective-permute-start(bf16[2,3,96,1536]{3,2,1,0:T(8,128)(2,1)S(1)} %pad_maximum_fusion.7), channel_id=1, source_target_pairs={{0,2},{1,3},{2,0},{3,1},{4,6},{5,7},{6,4},{7,5},{8,10},{9,11},{10,... | collective-permute-start | bytes 5308424 | tf_op jit(solution)/shard_map/ppermute | solution.py:42
  226.0 35.6 %collective-permute-start.30 = (bf16[2,3,96,1536]{3,2,1,0:T(8,128)(2,1)}, bf16[2,3,96,1536]{3,2,1,0:T(8,128)(2,1)}, u32[]{:S(2)}, u32[]{:S(2)}) collective-permute-start(bf16[2,3,96,1536]{3,2,1,0:T(8,128)(2,1)} %pad_maximum_fusion.8), channel_id=1, source_target_pairs={{0,1},{1,0},{2,3},{3,2},{4,5},{5,4},{6,7},{7,6},{8,9},{9,8},{10,11... | collective-permute-start | bytes 5308424 | tf_op jit(solution)/shard_map/ppermute | solution.py:42
  267.3 154.7 %collective-permute-start.31 = (bf16[2,4,3,96,1536]{4,3,2,1,0:T(8,128)(2,1)}, bf16[2,4,3,96,1536]{4,3,2,1,0:T(8,128)(2,1)}, u32[]{:S(2)}, u32[]{:S(2)}) collective-permute-start(bf16[2,4,3,96,1536]{4,3,2,1,0:T(8,128)(2,1)} %pad_maximum_fusion.1.refs_1_), channel_id=1, source_target_pairs={{0,16},{16,0},{1,17},{17,1},{2,18},{18,2},{3,19},{19,3},{4,20},{20... | collective-permute-start | bytes 21233672 | tf_op jit(solution)/shard_map/ppermute | solution.py:27
  590.1 390.5 %collective-permute-start.66 = (bf16[3,2,4,96,1536]{4,3,0,2,1:T(8,128)(2,1)}, bf16[3,2,4,96,1536]{4,3,0,2,1:T(8,128)(2,1)}, u32[]{:S(2)}, u32[]{:S(2)}) collective-permute-start(bf16[3,2,4,96,1536]{4,3,0,2,1:T(8,128)(2,1)} %bitcast.394), channel_id=1, source_target_pairs={{0,16},{16,0},{1,17},{17,1},{2,18},{18,2},{3,19},{19,3},{4,20},{20... | collective-permute-start | bytes 21233672 | tf_op jit(solution)/shard_map/ppermute | solution.py:27
  597.7 284.4 %collective-permute-start.50 = (bf16[1536,1536]{1,0:T(8,128)(2,1)}, bf16[1536,1536]{1,0:T(8,128)(2,1)}, u32[]{:S(2)}, u32[]{:S(2)}) collective-permute-start(bf16[1536,1536]{1,0:T(8,128)(2,1)} %get-tuple-element.252), channel_id=1, source_target_pairs={{0,16},{16,0},{1,17},{17,1},{2,18},{18,2},{3,19},{19,3},{4,20},{20... | collective-permute-start | bytes 14155784 | tf_op jit(solution)/shard_map/ppermute | solution.py:27
  599.6 592.8 %all-reduce.3.cloned.1.call-start = ((), (), s32[]{:S(2)}) async-start(), calls=%async_computation.3 | async-start | bytes 9437184 | tf_op jit(solution)/shard_map/psum | solution.py:598
  836.7 58.9 %collective-permute-start.40 = (bf16[1536,1536]{1,0:T(8,128)(2,1)}, bf16[1536,1536]{1,0:T(8,128)(2,1)}, u32[]{:S(2)}, u32[]{:S(2)}) collective-permute-start(bf16[1536,1536]{1,0:T(8,128)(2,1)} %get-tuple-element.254), channel_id=1, source_target_pairs={{0,16},{16,0},{1,17},{17,1},{2,18},{18,2},{3,19},{19,3},{4,20},{20... | collective-permute-start | bytes 14155784 | tf_op jit(solution)/shard_map/ppermute | solution.py:27
  895.6 42.3 %collective-permute-start.51 = (bf16[2,192,1536]{2,1,0:T(8,128)(2,1)}, bf16[2,192,1536]{2,1,0:T(8,128)(2,1)}, u32[]{:S(2)}, u32[]{:S(2)}) collective-permute-start(bf16[2,192,1536]{2,1,0:T(8,128)(2,1)} %pad_maximum_fusion.20), channel_id=1, source_target_pairs={{0,1},{1,0},{2,3},{3,2},{4,5},{5,4},{6,7},{7,6},{8,9},{9,8},{10,11... | collective-permute-start | bytes 3538952 | tf_op jit(solution)/shard_map/ppermute | solution.py:42
  909.1 90.3 %collective-permute-start.61 = (bf16[3,2,4,96,1536]{4,3,0,2,1:T(8,128)(2,1)}, bf16[3,2,4,96,1536]{4,3,0,2,1:T(8,128)(2,1)}, u32[]{:S(2)}, u32[]{:S(2)}) collective-permute-start(bf16[3,2,4,96,1536]{4,3,0,2,1:T(8,128)(2,1)} %bitcast.395), channel_id=1, source_target_pairs={{0,16},{16,0},{1,17},{17,1},{2,18},{18,2},{3,19},{19,3},{4,20},{20... | collective-permute-start | bytes 21233672 | tf_op jit(solution)/shard_map/ppermute | solution.py:27
  909.1 39.1 %collective-permute-start.43 = (bf16[2,192,1536]{2,1,0:T(8,128)(2,1)}, bf16[2,192,1536]{2,1,0:T(8,128)(2,1)}, u32[]{:S(2)}, u32[]{:S(2)}) collective-permute-start(bf16[2,192,1536]{2,1,0:T(8,128)(2,1)} %pad_maximum_fusion.19), channel_id=1, source_target_pairs={{0,2},{1,3},{2,0},{3,1},{4,6},{5,7},{6,4},{7,5},{8,10},{9,11},{10,... | collective-permute-start | bytes 3538952 | tf_op jit(solution)/shard_map/ppermute | solution.py:42
  964.4 157.6 %collective-permute-start.32 = (bf16[256,1536]{1,0:T(8,128)(2,1)}, bf16[256,1536]{1,0:T(8,128)(2,1)}, u32[]{:S(2)}, u32[]{:S(2)}) collective-permute-start(bf16[256,1536]{1,0:T(8,128)(2,1)} %get-tuple-element.130), channel_id=1, source_target_pairs={{0,16},{16,0},{1,17},{17,1},{2,18},{18,2},{3,19},{19,3},{4,20},{20... | collective-permute-start | bytes 2359304 | tf_op jit(solution)/shard_map/ppermute | solution.py:27
  996.6 41.7 %collective-permute-start.67 = (bf16[2,3,96,1536]{3,2,1,0:T(8,128)(2,1)}, bf16[2,3,96,1536]{3,2,1,0:T(8,128)(2,1)}, u32[]{:S(2)}, u32[]{:S(2)}) collective-permute-start(bf16[2,3,96,1536]{3,2,1,0:T(8,128)(2,1)} %pad_maximum_fusion.11), channel_id=1, source_target_pairs={{0,1},{1,0},{2,3},{3,2},{4,5},{5,4},{6,7},{7,6},{8,9},{9,8},{10,11... | collective-permute-start | bytes 5308424 | tf_op jit(solution)/shard_map/ppermute | solution.py:42
  998.9 41.8 %collective-permute-start.69 = (bf16[2,3,96,1536]{3,2,1,0:T(8,128)(2,1)}, bf16[2,3,96,1536]{3,2,1,0:T(8,128)(2,1)}, u32[]{:S(2)}, u32[]{:S(2)}) collective-permute-start(bf16[2,3,96,1536]{3,2,1,0:T(8,128)(2,1)} %stack.245), channel_id=1, source_target_pairs={{0,2},{1,3},{2,0},{3,1},{4,6},{5,7},{6,4},{7,5},{8,10},{9,11},{10,... | collective-permute-start | bytes 5308424 | tf_op jit(solution)/shard_map/ppermute | solution.py:42
  1015.4 60.9 %collective-permute-start.62 = (bf16[2,3,96,1536]{3,2,1,0:T(8,128)(2,1)}, bf16[2,3,96,1536]{3,2,1,0:T(8,128)(2,1)}, u32[]{:S(2)}, u32[]{:S(2)}) collective-permute-start(bf16[2,3,96,1536]{3,2,1,0:T(8,128)(2,1)} %pad_maximum_fusion.9), channel_id=1, source_target_pairs={{0,1},{1,0},{2,3},{3,2},{4,5},{5,4},{6,7},{7,6},{8,9},{9,8},{10,11... | collective-permute-start | bytes 5308424 | tf_op jit(solution)/shard_map/ppermute | solution.py:42
  1018.3 60.2 %collective-permute-start.64 = (bf16[2,3,96,1536]{3,2,1,0:T(8,128)(2,1)}, bf16[2,3,96,1536]{3,2,1,0:T(8,128)(2,1)S(1)}, u32[]{:S(2)}, u32[]{:S(2)}) collective-permute-start(bf16[2,3,96,1536]{3,2,1,0:T(8,128)(2,1)} %stack.244), channel_id=1, source_target_pairs={{0,2},{1,3},{2,0},{3,1},{4,6},{5,7},{6,4},{7,5},{8,10},{9,11},{10,... | collective-permute-start | bytes 5308424 | tf_op jit(solution)/shard_map/ppermute | solution.py:42
  1040.2 57.3 %collective-permute-start.68 = (bf16[3,96,1536]{2,1,0:T(8,128)(2,1)S(1)}, bf16[3,96,1536]{2,1,0:T(8,128)(2,1)S(1)}, u32[]{:S(2)}, u32[]{:S(2)}) collective-permute-start(bf16[3,96,1536]{2,1,0:T(8,128)(2,1)S(1)} %fusion.71), channel_id=1, source_target_pairs={{0,2},{1,3},{2,0},{3,1},{4,6},{5,7},{6,4},{7,5},{8,10},{9,11},{10,... | collective-permute-start | bytes 2654216 | tf_op jit(solution)/shard_map/ppermute | solution.py:42
  1042.5 56.7 %collective-permute-start.70 = (bf16[3,96,1536]{2,1,0:T(8,128)(2,1)S(1)}, bf16[3,96,1536]{2,1,0:T(8,128)(2,1)S(1)}, u32[]{:S(2)}, u32[]{:S(2)}) collective-permute-start(bf16[3,96,1536]{2,1,0:T(8,128)(2,1)S(1)} %fusion.72), channel_id=1, source_target_pairs={{0,1},{1,0},{2,3},{3,2},{4,5},{5,4},{6,7},{7,6},{8,9},{9,8},{10,11... | collective-permute-start | bytes 2654216 | tf_op jit(solution)/shard_map/ppermute | solution.py:42
  1077.7 38.3 %collective-permute-start.63 = (bf16[3,96,1536]{2,1,0:T(8,128)(2,1)S(1)}, bf16[3,96,1536]{2,1,0:T(8,128)(2,1)S(1)}, u32[]{:S(2)}, u32[]{:S(2)}) collective-permute-start(bf16[3,96,1536]{2,1,0:T(8,128)(2,1)S(1)} %fusion.69), channel_id=1, source_target_pairs={{0,2},{1,3},{2,0},{3,1},{4,6},{5,7},{6,4},{7,5},{8,10},{9,11},{10,... | collective-permute-start | bytes 2654216 | tf_op jit(solution)/shard_map/ppermute | solution.py:42
  1078.7 38.8 %collective-permute-start.65 = (bf16[3,96,1536]{2,1,0:T(8,128)(2,1)S(1)}, bf16[3,96,1536]{2,1,0:T(8,128)(2,1)S(1)}, u32[]{:S(2)}, u32[]{:S(2)}) collective-permute-start(bf16[3,96,1536]{2,1,0:T(8,128)(2,1)S(1)} %fusion.70), channel_id=1, source_target_pairs={{0,1},{1,0},{2,3},{3,2},{4,5},{5,4},{6,7},{7,6},{8,9},{9,8},{10,11... | collective-permute-start | bytes 2654216 | tf_op jit(solution)/shard_map/ppermute | solution.py:42
  1119.5 79.7 %collective-permute-start.71 = (bf16[3,192,1536]{2,1,0:T(8,128)(2,1)}, bf16[3,192,1536]{2,1,0:T(8,128)(2,1)}, u32[]{:S(2)}, u32[]{:S(2)}) collective-permute-start(bf16[3,192,1536]{2,1,0:T(8,128)(2,1)} %broadcast_select_fusion.10), channel_id=1, source_target_pairs={{0,16},{16,0},{1,17},{17,1},{2,18},{18,2},{3,19},{19,3},{4,20},{20... | collective-permute-start | bytes 5308424 | tf_op jit(solution)/shard_map/ppermute | solution.py:27
  (182 other events, 3853.5 us)
Sparse Core Ops, SparseCore 0:
  20.3 66.8 all-gather.1
  599.7 75.4 reduce-scatter.1
  1022.8 169.5 all-reduce.2

commit v2 on v1

--- a/solution.py
+++ b/solution.py
@@ -42,31 +42,34 @@
     return lax.ppermute(values, T, [(i, i ^ bit) for i in range(lax.axis_size(T))])
 
 
-def spread(piece, after):
-    a, b = piece
-    if after is not None:
-        a, b, _ = lax.optimization_barrier((a, b, after))
-    ax, by = hop(a, 1), hop(b, 2)
-    ay = hop(jnp.stack([a, ax]), 2)
-    bx = hop(jnp.stack([b, by]), 1)
-    return [a, ax, ay[0], ay[1]], [b, bx[0], by, bx[1]], (ay, bx)
+def after(values, *others):
+    return lax.optimization_barrier((values, others))[0]
+
+
+def line_gather(own):
+    n, me = lax.axis_size(D), lax.axis_index(D)
+    if n != SMALL:
+        return lax.all_gather(own, D, axis=0, tiled=True)
+    got = [own] + [lax.ppermute(own, D, [(i, i ^ r) for i in range(n)]) for r in range(1, n)]
+    got = jnp.stack(got)
+    return jnp.concatenate([lax.dynamic_index_in_dim(got, me ^ b, 0, False) for b in range(n)])
+
+
+def pieces_of(own):
+    return [own] + [hop(own, r) for r in (1, 2, 3)]
 
 
 def add(*values):
     return low(sum(v.astype(F32) for v in values))
 
 
-def reduce_spread(a, b):
-    ra = hop(jnp.stack([a[1], a[3]]), 1)
-    rb = hop(jnp.stack([b[2], b[3]]), 2)
-    own_a = hop(add(a[2], ra[1]), 2)
-    own_b = hop(add(b[1], rb[1]), 1)
-    return add(a[0], ra[0], own_a), add(b[0], rb[0], own_b)
-
-
-def sum_spread(a, b):
-    a, b = add(a, hop(a, 1)), add(b, hop(b, 2))
-    return add(a, hop(a, 2)), add(b, hop(b, 1))
+def summed(parts):
+    return add(parts[0], *(hop(parts[r], r) for r in (1, 2, 3)))
+
+
+def over_sections(keep, give):
+    got = partner(give)
+    return [add(keep[r], got[r]) for r in range(4)]
 
 
 def rope_tables(places):
@@ -103,13 +106,14 @@
 def expert_kernel(n, forward, backward, *refs):
     refs = list(refs)
     take = lambda count: [refs.pop(0) for _ in range(count)]
-    x, mine, other, share = take(4)
+    x, share = take(2)
+    pieces = take(8)
     grads_in = take(1)[0] if forward and backward else None
     saved = take(4) if not forward else None
     y = take(1)[0]
     outs = take(4) if not backward else None
     part_out = take(1)[0] if forward and backward else None
-    gw_out = take(1)[0] if backward else None
+    gw_outs = take(2) if backward else None
     tok, part, got, w, gate, up, act = take(7)
     second = take(1)[0] if backward else None
     stage = take(1)[0] if backward else None
@@ -118,13 +122,10 @@
     sub = rows // SUB
     me = lax.axis_index(D)
 
-    small = mine.shape[3]
+    small = pieces[0].shape[1]
     for i in range(3):
-        for h, pieces in enumerate((mine, other)):
-            for p in range(2):
-                for r in range(4):
-                    at = ((h * 2 + p) * 4 + r) * small
-                    pltpu.make_async_copy(pieces.at[p, r, i], w.at[i, pl.ds(at, small)], w_sem.at[i]).start()
+        for k, one in enumerate(pieces):
+            pltpu.make_async_copy(one.at[i], w.at[i, pl.ds(k * small, small)], w_sem.at[i]).start()
     loads = []
     if saved is not None:
         loads = [pltpu.make_async_copy(a, o, io_sem.at[i]) for i, (a, o) in enumerate(zip(saved, (gate, up, act, second)))]
@@ -258,21 +259,27 @@
 
     lax.fori_loop(0, 2 * n - 1, turn, 0)
 
-    piece = 256
+    piece = 2 * small
     slices = width // piece
     total = 3 * slices
 
-    def save_slice(k, slot):
-        at = pl.ds(pl.multiple_of(k % slices * piece, piece), piece)
-        return pltpu.make_async_copy(stage.at[slot], gw_out.at[k // slices, at], save_sem.at[1, slot])
+    def save_slice(k, slot, out=0):
+        unit = 2 * (k % (slices // 2))
+        return [
+            pltpu.make_async_copy(
+                stage.at[slot, pl.ds(v * small, small)], gw_outs[out].at[unit + v, k // slices], save_sem.at[1 + v, slot]
+            )
+            for v in range(2)
+        ]
 
     def weight_slice(k):
         slot = k % 2
-        at = pl.ds(pl.multiple_of(k % slices * piece, piece), piece)
+        at = pl.ds(pl.multiple_of(k % slices * piece, HEAD), piece)
 
         @pl.when(k >= 2)
         def _():
-            save_slice(k - 2, slot).wait()
+            for copy in save_slice(k - 2, slot):
+                copy.wait()
 
         tokens, grads = (tok, second) if forward else (second, tok)
         for i, (a, v) in enumerate(((gate, tokens), (up, tokens), (act, grads))):
@@ -284,7 +291,11 @@
                     rhs = jnp.concatenate([v[b, :, cols] for b in range(n)], 0)
                     stage[slot, :, cols] = dot(lhs, rhs, (0,), (0,)).astype(BF)
 
-        save_slice(k, slot).start()
+        for out in range(2):
+            @pl.when(k % slices // (slices // 2) == out)
+            def _():
+                for copy in save_slice(k, slot, out):
+                    copy.start()
 
     def add_rows(b, s, slot):
         at = pl.ds(pl.multiple_of(s * sub, sub), sub)
@@ -332,7 +343,8 @@
 
     if backward:
         for k in (total - 2, total - 1):
-            save_slice(k, k % 2).wait()
+            for copy in save_slice(k, k % 2):
+                copy.wait()
     for b in range(n):
         if not backward:
             for i, (a, o) in enumerate(zip((tok, act, gate, up), outs)):
@@ -357,33 +369,34 @@
                 left(b, s).wait_send()
 
 
-def experts(n, forward, backward, x, mine, other, share, *more):
+def experts(n, forward, backward, x, share, pieces, *more):
     rows, width = x.shape
-    hidden = mine.shape[3] * 16
+    small = pieces[0].shape[1]
+    hidden = small * 8
     shape = lambda *dims: jax.ShapeDtypeStruct(dims, BF)
     whole, wide = shape(n, rows, width), shape(n, rows, hidden)
     out = [jax.ShapeDtypeStruct((rows, width), F32)]
     out += [] if backward else [whole, wide, wide, wide]
     out += [whole] if forward and backward else []
-    out += [shape(3, hidden, width)] if backward else []
+    out += [shape(4, 3, small, width)] * 2 if backward else []
     room = lambda *dims: pltpu.VMEM(dims, BF)
     scratch = [room(n, rows, width), room(n, rows, width), room(n + 1, rows, width), room(3, hidden, width)]
     scratch += [room(n, rows, hidden)] * 3
-    scratch += [room(n, rows, width), room(2, 256, width)] if backward else []
+    scratch += [room(n, rows, width), room(2, 2 * small, width)] if backward else []
     dma = pltpu.SemaphoreType.DMA
     scratch += [dma((2, n)), dma((n,)), dma((n, SUB)), dma((n + 1, SUB)), dma((3,)), dma((4,)), dma((4, n))]
     vmem, far = pl.BlockSpec(memory_space=pltpu.VMEM), pl.BlockSpec(memory_space=pl.ANY)
     return pl.pallas_call(
         functools.partial(expert_kernel, n, forward, backward),
         out_shape=out,
-        in_specs=[vmem, far, far, vmem] + [far] * len(more),
+        in_specs=[vmem, vmem] + [far] * (8 + len(more)),
         out_specs=[vmem] + [far] * (len(out) - 1),
         scratch_shapes=scratch,
         compiler_params=pltpu.CompilerParams(
             collective_id=forward + 2 * backward, has_side_effects=True, vmem_limit_bytes=VMEM_LIMIT
         ),
-        cost_estimate=pl.CostEstimate(flops=80 * 10**9, bytes_accessed=10**8, transcendentals=0),
-    )(x, mine, other, share, *more)
+        cost_estimate=pl.CostEstimate(flops=4 * 10**11, bytes_accessed=10**8, transcendentals=0),
+    )(x, share, *pieces, *more)
 
 
 def turn_head(values, cosine, sine):
@@ -406,8 +419,28 @@
     lax.fori_loop(0, count, step, 0)
 
 
-def attend_kernel(x, normed, kv, bias, cosine, sine, wq, wo, gain, hidden, mixer, queries, flat, logs):
+def choose(mine, other, sem, *refs):
+    first = lax.axis_index(S) == 0
+    for i, (ref, low_first) in enumerate(refs):
+        a, b = (mine, other) if low_first else (other, mine)
+
+        @pl.when(first)
+        def _():
+            pltpu.make_async_copy(a, ref, sem.at[i]).start()
+
+        @pl.when(jnp.logical_not(first))
+        def _():
+            pltpu.make_async_copy(b, ref, sem.at[i]).start()
+
+    return [pltpu.make_async_copy(mine, ref, sem.at[i]) for i, (ref, _) in enumerate(refs)]
+
+
+def attend_kernel(
+    x, normed, kv, bias, cosine, sine, gain, mine, other, hidden, mixer, queries, flat, logs, wq, wo, sem
+):
     pair = 2 * HEAD
+    waits = choose(mine, other, sem, (wq, True), (wo, False))
+    waits[0].wait()
 
     def heads(i):
         both = dot(normed[...], wq[lanes(i * pair, pair)], (1,), (1,))
@@ -427,6 +460,8 @@
 
     loop(HEADS // 2, heads)
 
+    waits[1].wait()
+
     def out(i):
         cols = lanes(i * pair, pair)
         hidden[:, cols] = x[:, cols].astype(F32) + dot(flat[...], wo[:, cols], (1,), (0,))
@@ -437,10 +472,11 @@
 
 
 def attend_back_kernel(
-    grad, grad_mixer, hidden, gain, wo, queries, kv, logs, bias, flat, cosine, sine,
-    grad_hidden, gql, gkv, gwo, grad_gain, gao, ga, acc,
+    grad, grad_mixer, hidden, gain, queries, kv, logs, bias, flat, cosine, sine, mine, other,
+    grad_hidden, gql, gkv, gwo, grad_gain, gao, ga, acc, wo, sem,
 ):
     pair = 2 * HEAD
+    waits = choose(mine, other, sem, (wo, False))
     scale = HEAD ** (-0.5)
     h = hidden[...]
     r = inverse_rms(h)
@@ -451,6 +487,7 @@
     grad_hidden[...] = total
     gao[...] = total.astype(BF)
     acc[...] = jnp.zeros_like(acc)
+    waits[0].wait()
 
     def heads(i):
         rows = lanes(i * pair, pair)
@@ -480,25 +517,32 @@
     return pl.pallas_call(
         body,
         out_shape=[jax.ShapeDtypeStruct(*o) for o in out],
-        scratch_shapes=[pltpu.VMEM(*s) for s in scratch],
+        in_specs=[pl.BlockSpec(memory_space=pltpu.VMEM)] * (len(operands) - 2) + [pl.BlockSpec(memory_space=pl.ANY)] * 2,
+        scratch_shapes=[pltpu.VMEM(*s) for s in scratch] + [pltpu.SemaphoreType.DMA((2,))],
         compiler_params=pltpu.CompilerParams(vmem_limit_bytes=VMEM_LIMIT),
         cost_estimate=pl.CostEstimate(flops=flops, bytes_accessed=2 * 10**7, transcendentals=0),
     )(*operands)
 
 
-def attention_forward(x, p, c):
-    rows, width = x.shape
+def keys_and_values(x, p, c):
+    rows = x.shape[0]
     xf = x.astype(F32)
     normed = low(xf * inverse_rms(xf) * p["ga"])
     kv = dot(normed, p["kv"], (1,), (0,)).reshape(rows, 2 * GROUPS, HEAD)
     cosine, sine = c["rope"]
     keys = rotate(kv[:, :GROUPS], cosine[:, None], sine[:, None])
     kv = low(jnp.concatenate([keys, kv[:, GROUPS:]], 1)).reshape(rows, -1)
-    kv = jnp.concatenate([kv] + [hop(kv, r) for r in (1, 2, 3)])
+    return normed, jnp.concatenate(pieces_of(kv))
+
+
+def attention_forward(x, normed, kv, p, c):
+    rows, width = x.shape
+    cosine, sine = c["rope"]
     wide = (rows, HEADS * HEAD)
     hidden, mixer, queries, flat, logs = local_call(
-        attend_kernel, 10**10, [((rows, width), F32), ((rows, width), BF), (wide, BF), (wide, BF), (wide, F32)], [],
-        x, normed, kv, c["bias"], cosine, sine, p["wq"], p["wo"], p["gm"].reshape(1, -1),
+        attend_kernel, 10**11, [((rows, width), F32), ((rows, width), BF), (wide, BF), (wide, BF), (wide, F32)],
+        [(p["mine"].shape, BF)] * 2,
+        x, normed, kv, c["bias"], cosine, sine, p["gm"].reshape(1, -1), p["mine"], p["other"],
     )
     kept = dict(x=x, normed=normed, kv=kv, queries=queries, logs=logs, flat=flat, hidden=hidden)
     return hidden, mixer, kept
@@ -513,8 +557,8 @@
 
 
 def weights_of(p):
-    f = jnp.stack([p["mine"], p["other"]])
-    return tuple(f[:, :, :, i].reshape(-1, f.shape[-1]) for i in range(3))
+    f = jnp.stack(p["pieces"])
+    return tuple(f[:, i].reshape(-1, f.shape[-1]) for i in range(3))
 
 
 def share_of(p, hidden):
@@ -523,7 +567,7 @@
 
 def mix_forward(mixer, p, n):
     if n <= SMALL:
-        y, tokens, act, gate, up = experts(n, True, False, mixer, p["mine"], p["other"], p["wide"])
+        y, tokens, act, gate, up = experts(n, True, False, mixer, p["wide"], p["pieces"])
         return y, dict(tokens=tokens, act=act, gate=gate, up=up)
     wg, wu, wd = weights_of(p)
     tokens = along(mixer)
@@ -536,7 +580,7 @@
 def mix_backward(grad, k, p, n):
     if n <= SMALL:
         saved = (k["gate"], k["up"], k["act"], k["tokens"])
-        return experts(n, False, True, grad, p["mine"], p["other"], p["wide"], *saved)
+        return experts(n, False, True, grad, p["wide"], p["pieces"], *saved)
     wg, wu, wd = weights_of(p)
     grads = along(grad)
     da = dot(grads, wd, (1,), (1,)) * share_of(p, wd.shape[0])
@@ -546,23 +590,19 @@
     gm = scatter_along(dot(dg, wg, (1,), (0,)) + dot(du, wu, (1,), (0,))).astype(F32)
     flat = lambda v: v.reshape(-1, v.shape[-1])
     pairs = ((dg, k["tokens"]), (du, k["tokens"]), (k["act"], grads))
-    return gm, jnp.stack([low(dot(flat(u), flat(v), (0,), (0,))) for u, v in pairs])
+    gw = [low(dot(flat(u), flat(v), (0,), (0,))) for u, v in pairs]
+    gw = jnp.stack([g.reshape(8, -1, g.shape[-1]) for g in gw], 1)
+    return gm, gw[:4], gw[4:]
 
 
 def mix_both(mixer, grad, p, n):
     if n <= SMALL:
         grads = along(grad).reshape(n, *grad.shape)
-        gm, part, gw = experts(n, True, True, mixer, p["mine"], p["other"], p["wide"], grads)
+        gm, part, keep, give = experts(n, True, True, mixer, p["wide"], p["pieces"], grads)
         y = scatter_along(part).astype(F32)
-        return y, gm, gw
+        return y, gm, keep, give
     y, k = mix_forward(mixer, p, n)
     return (y,) + mix_backward(grad, k, p, n)
-
-
-def expert_grads(gw):
-    gw = gw.reshape(3, 2, 2, 4, -1, gw.shape[-1])
-    gf = add(gw[:, 0], partner(gw[:, 1]))
-    return reduce_spread(gf[:, 0].transpose(1, 0, 2, 3), gf[:, 1].transpose(1, 0, 2, 3))
 
 
 def attention_backward(grad, grad_mixer, k, p, c, first):
@@ -570,11 +610,11 @@
     cosine, sine = c["rope"]
     wide, length = (rows, HEADS * HEAD), c["bias"].shape[1]
     grad_hidden, gql, gkv, gw_out, g_gm = local_call(
-        attend_back_kernel, 2 * 10**10,
+        attend_back_kernel, 10**11,
         [((rows, width), F32), (wide, BF), ((length, 2 * GROUPS * HEAD), BF), ((HEADS * HEAD, width), BF), ((1, width), F32)],
-        [((rows, width), BF), ((rows, 2 * HEAD), BF), ((length, 2 * GROUPS * HEAD), F32)],
-        grad, grad_mixer, k["hidden"], p["gm"].reshape(1, -1), p["wo"], k["queries"], k["kv"], k["logs"], c["bias"],
-        k["flat"], cosine, sine,
+        [((rows, width), BF), ((rows, 2 * HEAD), BF), ((length, 2 * GROUPS * HEAD), F32), (p["mine"].shape, BF)],
+        grad, grad_mixer, k["hidden"], p["gm"].reshape(1, -1), k["queries"], k["kv"], k["logs"], c["bias"],
+        k["flat"], cosine, sine, p["mine"], p["other"],
     )
     gkv = gkv.reshape(4, rows, -1)
     gkv = gkv[0].astype(F32) + sum(hop(gkv[r], r).astype(F32) for r in (1, 2, 3))
@@ -582,21 +622,23 @@
     cosine, sine = cosine[:, None], sine[:, None]
     gkv = jnp.concatenate([rotate(gkv[:, :GROUPS], cosine, -sine), gkv[:, GROUPS:]], 1)
     gkv = low(gkv).reshape(rows, -1)
-    grad_normed = dot(gql, p["wq"], (1,), (0,)) + dot(gkv, p["kv"], (1,), (1,))
+    wq = jnp.where(first, p["mine"], p["other"])
+    grad_normed = dot(gql, wq, (1,), (0,)) + dot(gkv, p["kv"], (1,), (1,))
     gw_q = low(dot(gql, k["normed"], (0,), (0,)))
     gw_kv = dot(gkv, k["normed"], (0,), (0,))
     more, g_ga = norm_back(grad_normed, k["x"].astype(F32), p["ga"])
-    gat = add(jnp.where(first, gw_q, gw_out), partner(jnp.where(first, gw_out, gw_q)))
-    gat = gat.reshape(4, 2, -1, width)
-    gat = reduce_spread(gat[:, 0], gat[:, 1])
     gw_kv = gw_kv.reshape(2, -1, width)
-    pad = jnp.zeros((31, width), F32)
-    small = [low(jnp.concatenate([gw_kv[i], g[None], pad])) for i, g in enumerate((g_ga, g_gm[0]))]
-    small = add(jnp.where(first, small[0], small[1]), partner(jnp.where(first, small[1], small[0])))
-    small = small.reshape(2, -1, width)
-    small = sum_spread(small[0], small[1])
-    sums = lax.psum(jnp.concatenate(gat + small), D)
-    return grad_hidden + more, sums
+    at = lax.axis_index(T)
+    pad = jnp.zeros((63, width), F32)
+
+    def rows_of(main, i, gain):
+        less = low(jnp.concatenate([gw_kv[i], gain[None], pad])).reshape(4, -1, width)
+        less = jnp.stack([lax.dynamic_index_in_dim(less, at ^ r, 0, False) for r in range(4)])
+        return jnp.concatenate([main.reshape(4, -1, width), less], 1)
+
+    q, o = rows_of(gw_q, 0, g_ga), rows_of(gw_out, 1, g_gm[0])
+    parts = over_sections(jnp.where(first, q, o), jnp.where(first, o, q))
+    return grad_hidden + more, parts
 
 
 def on_device(
@@ -624,9 +666,14 @@
     named = routes[0][..., None] == jnp.arange(experts, dtype=jnp.int32)
     shares = jnp.sum(jnp.where(named, route_gates[0][..., None], 0.0), 2)
     shares = jnp.stack(halves(shares), 1)
-    shares = lax.all_gather(shares, D, axis=0, tiled=True)
-    shares = lax.dynamic_slice_in_dim(shares, lax.axis_index(D) * here, here, 2)
-    shares = jnp.where(first, shares, shares[:, :, ::-1])
+
+    shares = line_gather(shares)
+
+    def factors(own, l):
+        share = own[:, l]
+        share = lax.dynamic_slice_in_dim(share, lax.axis_index(D) * here, here, 1)
+        share = jnp.where(first, share, share[:, ::-1])
+        return jnp.broadcast_to(share.T.reshape(here, -1, rows, 1), (here, share.shape[0] // rows, rows, HEAD)), share
 
     queries_at = at * rows + jnp.arange(rows)
     keys_at = jnp.concatenate([(at ^ r) * rows + jnp.arange(rows) for r in range(4)])
@@ -634,48 +681,65 @@
     allowed = (keys_at[None] <= queries_at[:, None]) & (key_segment[:rows, None] == key_segment[None])
     c = dict(rope=rope_tables(queries_at.astype(F32)), bias=jnp.where(allowed, 0.0, -1e30))
 
-    attn = halves(jnp.stack([w_query[0].T, w_out[0]]).reshape(2, 2, -1, width))
+    attn = halves(jnp.stack([w_query[0].T, w_out[0]]))
     g, u = (w[0].transpose(0, 2, 1) for w in (w_gate, w_up))
-    ffn = jnp.stack([g, u, w_down[0]], 1).reshape(here, 3, 2, -1, width).transpose(0, 2, 1, 3, 4)
-    ffn = halves(ffn)
+    ffn = halves(jnp.stack([g, u, w_down[0]], 1))
     kv = both(first, jnp.concatenate([key_weight[0], value_weight[0]], 1))
     ga = both(first, attn_gain)
     gm = both(first, mixer_gain)
     params = []
-    after = None
+    last = None
+    small = [dict(kv=kv[l], ga=ga[l], gm=gm[l]) for l in range(2)]
+    ahead = keys_and_values(x0, small[0], c)
     for l in range(2):
-        a, b, after = spread(attn[l], after)
-        got = jnp.concatenate([v for pair in zip(a, b) for v in pair])
-        other = partner(got)
-        q, o = jnp.where(first, got, other), jnp.where(first, other, got)
-        a, b, after = spread(ffn[l], after)
-        got = jnp.stack([jnp.stack(a), jnp.stack(b)])
-        share = shares[:, l]
-        wide = jnp.broadcast_to(share.T.reshape(here, -1, rows, 1), (here, share.shape[0] // rows, rows, HEAD))
+        own = attn[l] if last is None else after(attn[l], last)
+        got = pieces_of(own)
+        if last is None:
+            ffn = after(ffn, got, ahead)
+        mine = jnp.concatenate(got)
+        wide, share = factors(shares, l)
+        got = pieces_of(ffn[l] if last is None else after(ffn[l], last))
+        last = got
         params.append(
-            dict(wq=q, wo=o, kv=kv[l], ga=ga[l], gm=gm[l], mine=got, other=partner(got), share=share, wide=wide)
+            dict(
+                small[l], mine=mine, other=partner(mine), share=share, wide=wide,
+                pieces=got + [partner(v) for v in got],
+            )
         )
     n = lax.axis_size(D)
-    hidden0, mixer, k0 = attention_forward(x0, params[0], c)
+    hidden0, mixer, k0 = attention_forward(x0, *ahead, params[0], c)
     y, kept = mix_forward(mixer, params[0], n)
     y0 = low((hidden0 + y))
-    hidden1, mixer, k1 = attention_forward(y0, params[1], c)
-    y, gm, gw = mix_both(mixer, low(grad1), params[1], n)
-    y1 = low((hidden1 + y))
-    f1 = expert_grads(gw)
-    gx1, s1 = attention_backward(grad1, gm, k1, params[1], c, first)
+    hidden1, mixer, k1 = attention_forward(y0, *keys_and_values(y0, params[1], c), params[1], c)
+    y, gm, keep, give = mix_both(mixer, low(grad1), params[1], n)
+    y1 = low(hidden1 + y)
+    parts = over_sections(keep, give)
+    gx1, more = attention_backward(grad1, gm, k1, params[1], c, first)
     gb = low(gx1)
-    gm, gw = mix_backward(gb, kept, params[0], n)
-    f0 = expert_grads(gw)
-    gx0, s0 = attention_backward(gb.astype(F32), gm, k0, params[0], c, first)
+    rows_f = 3 * hidden
+    both_parts = [jnp.concatenate([a.reshape(rows_f, width), b]) for a, b in zip(parts, more)]
+    gb, both_parts = lax.optimization_barrier((gb, both_parts))
+    got = summed(both_parts)
+    gm, keep, give = mix_backward(gb, kept, params[0], n)
+    gm, got, y1 = lax.optimization_barrier((gm, got, y1))
+    f1, s1 = got[:rows_f].reshape(3, hidden, width), lax.psum(got[rows_f:], D)
+    parts = over_sections(keep, give)
+    part_a = summed([v[:1] for v in parts])
+    gx0, more = attention_backward(gb.astype(F32), gm, k0, params[0], c, first)
+    s0 = summed(more)
+    part_b = summed(after([v[1:] for v in parts], s0))
+    f0 = jnp.concatenate([part_a, part_b])
+    s0 = lax.psum(after(s0, s1), D)
 
     outs = jnp.stack(swap(first, y0, y1))
     input_grads = jnp.stack(swap(first, low(gx0), low(gx1))).astype(F32)
-    f = jnp.stack(swap(first, jnp.concatenate(f0, 1), jnp.concatenate(f1, 1))).astype(F32)
+    f = jnp.stack(swap(first, f0, f1)).astype(F32)
     zero, one = swap(first, s0, s1)
     high = w_out.shape[1]
     q, o = zero[:high].astype(F32), one[:high].astype(F32)
-    ka, vm = zero[high:].astype(F32), one[high:].astype(F32)
+    less = jnp.stack(pieces_of(jnp.stack([zero[high:], one[high:]])))
+    less = jnp.concatenate([lax.dynamic_index_in_dim(less, at ^ i, 0, False) for i in range(4)], 1).astype(F32)
+    ka, vm = less[0], less[1]
     few = GROUPS * HEAD
     return (
         outs[None], input_grads[None], ka[few : few + 1], q.T[None], ka[:few].T[None],

time: 1240 us -> 1150 us (0.927)
  waiting for transfers between devices: 313 us -> 389 us
  local copies, waits for them, and re-layouts: 151 us -> 78.3 us
  other arithmetic: 167 us -> 112 us
  Pallas kernels: 484 us -> 451 us
  blocking collectives: 15.7 us -> 0 us
    reduce_scatter x1, waiting for transfers between devices: 0.02 us -> 44.7 us  [scatter_along(): lax.psum_scatter(low(values.reshape(-1, values.shape[-1])), D, scatter_di...]
    convert_element_type x33 -> x20, other arithmetic: 73.6 us -> 40.1 us  [low(): return lax.reduce_precision(values.astype(F32), 8, 7).astype(BF)]
    pallas_call x3, Pallas kernels: 394 us -> 361 us  [experts(): pl.pallas_call(functools.partial(expert_kernel, n, forward, backward), ou...]
    all_gather x1, waiting for transfers between devices: 0.01 us -> 30.3 us  [along(): return lax.all_gather(low(values), D, axis=0, tiled=True)]
    psum x1 -> x2, waiting for transfers between devices: 67.9 us -> 42.9 us  [the longest x1 42.9 us: on_device(): s0 = lax.psum(after(s0, s1), D)]
    another operation x22 -> x6, other arithmetic: 28.8 us -> 6.56 us  [the longest x2 2.58 us: on_device(): less = jnp.stack(pieces_of(jnp.stack([zero[high:], one[high:]])))]
    unnamed x304 -> x236, local copies, waits for them, and re-layouts: 59.4 us -> 38.3 us
    ppermute x52 -> x39, waiting for transfers between devices: 245 us -> 265 us  [hop(): lax.ppermute(values, T, [(i, i ^ bit) for i in range(lax.axis_size(T))])]
  transfers between devices with their start and end apart: 75 -> 70, of which waited for: 27 -> 27; matrix products, arithmetic and copies ran while one was open for 25% -> 15% of each run, Pallas kernels for 27% -> 26%
where the time goes in v2:
time: 1150 us; the launch traced here: 1140 us
  Pallas kernels  451 us (39%)
  waiting for transfers between devices  389 us (34%)
  other arithmetic  112 us (10%)
  local copies, waits for them, and re-layouts  78.3 us (7%)
  starting transfers between devices  63.4 us (6%)
  matrix products  26.4 us (2%)
  between operations  16 us (1%)
    pallas_call x3, Pallas kernels, experts(): pl.pallas_call(functools.partial(expert_kernel, n, forward, backward), ou...  361 us
    ppermute x39, waiting for transfers between devices, hop(): lax.ppermute(values, T, [(i, i ^ bit) for i in range(lax.axis_size(T))])  265 us
    pallas_call x4, Pallas kernels, local_call(): pl.pallas_call(body, out_shape=[jax.ShapeDtypeStruct(*o) for o in out], i...  90.4 us
    ppermute x39, starting transfers between devices, hop(): lax.ppermute(values, T, [(i, i ^ bit) for i in range(lax.axis_size(T))])  50.1 us
    reduce_scatter x1, waiting for transfers between devices, scatter_along(): lax.psum_scatter(low(values.reshape(-1, values.shape[-1])), D, scatter_di...  44.7 us
    psum x1, waiting for transfers between devices, on_device(): s0 = lax.psum(after(s0, s1), D)  42.9 us
    convert_element_type x20, other arithmetic, low(): return lax.reduce_precision(values.astype(F32), 8, 7).astype(BF)  40.1 us
    unnamed x236, local copies, waits for them, and re-layouts  38.3 us
  transfers between devices with their start and end apart: 70, of which 27 were waited for; matrix products, arithmetic and copies ran while one was open for 15% of the time, Pallas kernels for 26%

profile of v2, /device:TPU:0, one launch (start us, length us, event | category | flops | bytes accessed | tf_op | source)
XLA Modules:
  0.0 1136.7 jit_solution(11199873206995106980)
XLA Ops:
  40.0 18.4 %collective-permute-done.9 = bf16[384,1536]{1,0:T(8,128)(2,1)} collective-permute-done((bf16[384,1536]{1,0:T(8,128)(2,1)}, bf16[384,1536]{1,0:T(8,128)(2,1)}, u32[]{:S(2)}, u32[]{:S(2)}) %collective-permute-start.9) | collective-permute-done | bytes 1179680 | tf_op jit(solution)/shard_map/ppermute | solution.py:42
  60.3 23.3 %collective-permute-done.8 = bf16[384,1536]{1,0:T(8,128)(2,1)} collective-permute-done((bf16[384,1536]{1,0:T(8,128)(2,1)}, bf16[384,1536]{1,0:T(8,128)(2,1)}, u32[]{:S(2)}, u32[]{:S(2)}) %collective-permute-start.8) | collective-permute-done | bytes 1179680 | tf_op jit(solution)/shard_map/ppermute | solution.py:42
  85.6 5.3 pad_maximum_fusion.mine
  106.9 31.7 %collective-permute-done.16.refs_3_ = bf16[3,192,1536]{2,1,0:T(8,128)(2,1)} collective-permute-done((bf16[3,192,1536]{2,1,0:T(8,128)(2,1)S(1)}, bf16[3,192,1536]{2,1,0:T(8,128)(2,1)}, u32[]{:S(2)}, u32[]{:S(2)}) %collective-permute-start.16) | collective-permute-done | bytes 1769504 | tf_op jit(solution)/shard_map/ppermute | solution.py:42
  141.3 35.5 %collective-permute-done.17.refs_4_ = bf16[3,192,1536]{2,1,0:T(8,128)(2,1)} collective-permute-done((bf16[3,192,1536]{2,1,0:T(8,128)(2,1)S(1)}, bf16[3,192,1536]{2,1,0:T(8,128)(2,1)}, u32[]{:S(2)}, u32[]{:S(2)}) %collective-permute-start.17) | collective-permute-done | bytes 1769504 | tf_op jit(solution)/shard_map/ppermute | solution.py:42
  195.5 12.2 %collective-permute-done.26 = bf16[384,1536]{1,0:T(8,128)(2,1)} collective-permute-done((bf16[384,1536]{1,0:T(8,128)(2,1)}, bf16[384,1536]{1,0:T(8,128)(2,1)}, u32[]{:S(2)}, u32[]{:S(2)}) %collective-permute-start.26) | collective-permute-done | bytes 1179680 | tf_op jit(solution)/shard_map/ppermute | solution.py:42
  210.6 15.6 %collective-permute-done.27 = bf16[384,1536]{1,0:T(8,128)(2,1)} collective-permute-done((bf16[384,1536]{1,0:T(8,128)(2,1)}, bf16[384,1536]{1,0:T(8,128)(2,1)}, u32[]{:S(2)}, u32[]{:S(2)}) %collective-permute-start.27) | collective-permute-done | bytes 1179680 | tf_op jit(solution)/shard_map/ppermute | solution.py:42
  228.5 4.5 collective-permute-done.28
  235.9 20.8 %shard_map.221 = (f32[256,1536]{1,0:T(8,128)}, bf16[256,1536]{1,0:T(8,128)(2,1)S(1)}, bf16[256,1536]{1,0:T(8,128)(2,1)S(1)}, bf16[256,1536]{1,0:T(8,128)(2,1)S(1)}, f32[256,1536]{1,0:T(8,128)}) custom-call(bf16[256,1536]{1,0:T(8,128)(2,1)S(1)} %get-tuple-element.146.x, bf16[256,1536]{1,0:T(8,128)(2,1)S(1)} %fusion.29.normed, ...), custom_call_target="tpu_custom_call" | custom-call | flops 99999997952 | bytes 20000000 | tf_op jit(solution)/shard_map/pallas_call | solution.py:517
  262.3 113.9 %shard_map.222 = (f32[256,1536]{1,0:T(8,128)S(1)}, bf16[4,256,1536]{2,1,0:T(8,128)(2,1)}, bf16[4,256,1536]{2,1,0:T(8,128)(2,1)}, bf16[4,256,1536]{2,1,0:T(8,128)(2,1)}, bf16[4,256,1536]{2,1,0:T(8,128)(2,1)}) custom-call(bf16[256,1536]{1,0:T(8,128)(2,1)S(1)} %get-tuple-element.61.refs_0_, f32[2,4,256,128]{3,2,1,0:T(8,128)S(1)} %broadcast_in_dim.97.refs_1_, ...), custom_call_target="tpu_custom_call" | custom-call | flops 399999991808 | bytes 100000000 | tf_op jit(solution)/shard_map/pallas_call | solution.py:389
  393.3 20.8 %shard_map.223 = (f32[256,1536]{1,0:T(8,128)}, bf16[256,1536]{1,0:T(8,128)(2,1)S(1)}, bf16[256,1536]{1,0:T(8,128)(2,1)S(1)}, bf16[256,1536]{1,0:T(8,128)(2,1)S(1)}, f32[256,1536]{1,0:T(8,128)}) custom-call(bf16[256,1536]{1,0:T(8,128)(2,1)S(1)} %get-tuple-element.144.x, bf16[256,1536]{1,0:T(8,128)(2,1)S(1)} %fusion.39.normed, ...), custom_call_target="tpu_custom_call" | custom-call | flops 99999997952 | bytes 20000000 | tf_op jit(solution)/shard_map/pallas_call | solution.py:517
  417.9 30.3 %all-gather.2.cloned.1.call-done = bf16[1024,1536]{1,0:T(8,128)(2,1)} async-done(((bf16[256,1536]{1,0:T(8,128)(2,1)}), bf16[1024,1536]{1,0:T(8,128)(2,1)}) %all-gather.2.cloned.1.call-update) | async-done | bytes 3145744 | tf_op jit(solution)/shard_map/all_gather | solution.py:552
  449.6 130.7 %shard_map.224 = (f32[256,1536]{1,0:T(8,128)S(1)}, bf16[4,256,1536]{2,1,0:T(8,128)(2,1)}, bf16[4,3,192,1536]{3,2,1,0:T(8,128)(2,1)}, bf16[4,3,192,1536]{3,2,1,0:T(8,128)(2,1)}) custom-call(bf16[256,1536]{1,0:T(8,128)(2,1)S(1)} %copy-done.35, f32[2,4,256,128]{3,2,1,0:T(8,128)S(1)} %broadcast_in_dim.99.refs_1_, ...), custom_call_target="tpu_custom_call" | custom-call | flops 399999991808 | bytes 100000000 | tf_op jit(solution)/shard_map/pallas_call | solution.py:389
  581.5 24.4 %shard_map.225 = (f32[256,1536]{1,0:T(8,128)}, bf16[256,1536]{1,0:T(8,128)(2,1)S(1)}, bf16[1024,512]{1,0:T(8,128)(2,1)S(1)}, bf16[1536,1536]{1,0:T(8,128)(2,1)}, f32[1,1536]{1,0:T(1,128)S(1)}) custom-call(f32[256,1536]{1,0:T(8,128)} %get-tuple-element.142.grad, f32[256,1536]{1,0:T(8,128)} %copy-done.25, f32[256,1536]{1,0:T(8,128)} %get-tuple-element.69.hidden, ...), custom_call_target="tpu_custom_call" | custom-call | flops 99999997952 | bytes 20000000 | tf_op jit(solution)/shard_map/pallas_call | solution.py:517
  620.4 5.2 fusion.46
  628.4 4.4 broadcast_select_fusion.2
  637.4 6.3 broadcast_select_fusion.3
  643.7 4.5 fusion.51
  648.2 44.7 %reduce-scatter.2.cloned.1.call-done = bf16[256,1536]{1,0:T(8,128)(2,1)} async-done(((bf16[1024,1536]{1,0:T(8,128)(2,1)}), bf16[256,1536]{1,0:T(8,128)(2,1)}) %reduce-scatter.2.cloned.1.call-update) | async-done | bytes 786448 | tf_op jit(solution)/shard_map/reduce_scatter | solution.py:556
  695.6 6.2 reduce-precision_convert_fusion.8
  713.1 116.2 %shard_map.226 = (f32[256,1536]{1,0:T(8,128)S(1)}, bf16[4,3,192,1536]{3,2,1,0:T(8,128)(2,1)}, bf16[4,3,192,1536]{3,2,1,0:T(8,128)(2,1)}) custom-call(bf16[256,1536]{1,0:T(8,128)(2,1)S(1)} %fusion.45.refs_0_, f32[2,4,256,128]{3,2,1,0:T(8,128)S(1)} %copy-done.11, bf16[3,192,1536]{2,1,0:T(8,128)(2,1)S(1)} %copy-done.5, ...), custom_call_target="tpu_custom_call" | custom-call | flops 399999991808 | bytes 100000000 | tf_op jit(solution)/shard_map/pallas_call | solution.py:389
  830.8 19.2 %collective-permute-done.43 = bf16[1040,1536]{1,0:T(8,128)(2,1)} collective-permute-done((bf16[1040,1536]{1,0:T(8,128)(2,1)}, bf16[1040,1536]{1,0:T(8,128)(2,1)}, u32[]{:S(2)}, u32[]{:S(2)}) %collective-permute-start.43) | collective-permute-done | bytes 3194912 | tf_op jit(solution)/shard_map/ppermute | solution.py:42
  850.0 6.4 reduce-precision_convert_fusion.2
  863.4 24.4 %shard_map.227 = (f32[256,1536]{1,0:T(8,128)}, bf16[256,1536]{1,0:T(8,128)(2,1)S(1)}, bf16[1024,512]{1,0:T(8,128)(2,1)S(1)}, bf16[1536,1536]{1,0:T(8,128)(2,1)}, f32[1,1536]{1,0:T(1,128)S(1)}) custom-call(f32[256,1536]{1,0:T(8,128)} %convert_element_type.536.grad, f32[256,1536]{1,0:T(8,128)} %copy-done.24, f32[256,1536]{1,0:T(8,128)} %get-tuple-element.60.hidden, ...), custom_call_target="tpu_custom_call" | custom-call | flops 99999997952 | bytes 20000000 | tf_op jit(solution)/shard_map/pallas_call | solution.py:517
  893.2 4.7 reduce-precision_convert_fusion
  900.0 5.2 collective-permute-done.47
  947.9 28.2 %collective-permute-done.53 = bf16[464,1536]{1,0:T(8,128)(2,1)S(1)} collective-permute-done((bf16[464,1536]{1,0:T(8,128)(2,1)S(1)}, bf16[464,1536]{1,0:T(8,128)(2,1)S(1)}, u32[]{:S(2)}, u32[]{:S(2)}) %collective-permute-start.53) | collective-permute-done | bytes 1425440 | tf_op jit(solution)/shard_map/ppermute | solution.py:42
  976.1 30.0 %collective-permute-done.52 = bf16[464,1536]{1,0:T(8,128)(2,1)S(1)} collective-permute-done((bf16[464,1536]{1,0:T(8,128)(2,1)S(1)}, bf16[464,1536]{1,0:T(8,128)(2,1)S(1)}, u32[]{:S(2)}, u32[]{:S(2)}) %collective-permute-start.52) | collective-permute-done | bytes 1425440 | tf_op jit(solution)/shard_map/ppermute | solution.py:42
  1018.6 8.0 collective-permute-done.61
  1028.9 42.9 %all-reduce.5.cloned.1.call-done = bf16[464,1536]{1,0:T(8,128)(2,1)} async-done(((bf16[464,1536]{1,0:T(8,128)(2,1)}), bf16[464,1536]{1,0:T(8,128)(2,1)}) %all-reduce.5.cloned.1.call-update) | async-done | bytes 1425424 | tf_op jit(solution)/shard_map/psum | solution.py:732
  1072.0 16.8 %collective-permute-done.60 = bf16[1,192,1536]{2,1,0:T(8,128)(2,1)S(1)} collective-permute-done((bf16[1,192,1536]{2,1,0:T(8,128)(2,1)}, bf16[1,192,1536]{2,1,0:T(8,128)(2,1)S(1)}, u32[]{:S(2)}, u32[]{:S(2)}) %collective-permute-start.60) | collective-permute-done | bytes 589856 | tf_op jit(solution)/shard_map/ppermute | solution.py:42
  1114.9 8.4 collective-permute-done.56
  (509 shorter events, 251.7 us)
Async XLA Ops:
  7.2 440.9 %all-gather.2.cloned.1.call-start = ((), (), s32[]{:S(2)}) async-start(), calls=%async_computation.1 | async-start | bytes 3932160 | tf_op jit(solution)/shard_map/all_gather | solution.py:552
  19.3 71.6 %collective-permute-start.15 = (bf16[3,192,1536]{2,1,0:T(8,128)(2,1)}, bf16[3,192,1536]{2,1,0:T(8,128)(2,1)}, u32[]{:S(2)}, u32[]{:S(2)}) collective-permute-start(bf16[3,192,1536]{2,1,0:T(8,128)(2,1)} %dynamic-slice_bitcast_fusion), channel_id=1, source_target_pairs={{0,16},{16,0},{1,17},{17,1},{2,18},{18,2},{3,19},{19,3},{4,20},{20... | collective-permute-start | bytes 5308424 | tf_op jit(solution)/shard_map/ppermute | solution.py:27
  37.1 56.8 %collective-permute-start.4 = (bf16[256,512]{1,0:T(8,128)(2,1)}, bf16[256,512]{1,0:T(8,128)(2,1)S(1)}, u32[]{:S(2)}, u32[]{:S(2)}) collective-permute-start(bf16[256,512]{1,0:T(8,128)(2,1)} %copy.85), channel_id=1, source_target_pairs={{0,3},{1,2},{2,1},{3,0},{4,7},{5,6},{6,5},{7,4},{8,11},{9,10},{10,... | collective-permute-start | bytes 786440 | tf_op jit(solution)/shard_map/ppermute | solution.py:42
  90.9 144.5 %collective-permute-start.10 = (bf16[1536,1536]{1,0:T(8,128)(2,1)}, bf16[1536,1536]{1,0:T(8,128)(2,1)}, u32[]{:S(2)}, u32[]{:S(2)}) collective-permute-start(bf16[1536,1536]{1,0:T(8,128)(2,1)} %pad_maximum_fusion.mine), channel_id=1, source_target_pairs={{0,16},{16,0},{1,17},{17,1},{2,18},{18,2},{3,19},{19,3},{4,20},{20... | collective-permute-start | bytes 14155784 | tf_op jit(solution)/shard_map/ppermute | solution.py:27
  98.6 78.2 %collective-permute-start.17 = (bf16[3,192,1536]{2,1,0:T(8,128)(2,1)S(1)}, bf16[3,192,1536]{2,1,0:T(8,128)(2,1)}, u32[]{:S(2)}, u32[]{:S(2)}) collective-permute-start(bf16[3,192,1536]{2,1,0:T(8,128)(2,1)S(1)} %get-tuple-element.62.refs_2_), channel_id=1, source_target_pairs={{0,2},{1,3},{2,0},{3,1},{4,6},{5,7},{6,4},{7,5},{8,10},{9,11},{10,... | collective-permute-start | bytes 5308424 | tf_op jit(solution)/shard_map/ppermute | solution.py:42
  99.1 79.2 %collective-permute-start.18 = (bf16[3,192,1536]{2,1,0:T(8,128)(2,1)S(1)}, bf16[3,192,1536]{2,1,0:T(8,128)(2,1)}, u32[]{:S(2)}, u32[]{:S(2)}) collective-permute-start(bf16[3,192,1536]{2,1,0:T(8,128)(2,1)S(1)} %get-tuple-element.62.refs_2_), channel_id=1, source_target_pairs={{0,3},{1,2},{2,1},{3,0},{4,7},{5,6},{6,5},{7,4},{8,11},{9,10},{10,... | collective-permute-start | bytes 5308424 | tf_op jit(solution)/shard_map/ppermute | solution.py:42
  103.3 75.6 %collective-permute-start.14 = (f32[256,2,8]{0,2,1:T(8,128)S(1)}, f32[256,2,8]{0,2,1:T(8,128)S(1)}, u32[]{:S(2)}, u32[]{:S(2)}) collective-permute-start(f32[256,2,8]{0,2,1:T(8,128)S(1)} %get-tuple-element.238), channel_id=1, source_target_pairs={{0,12},{4,8},{8,4},{12,0},{1,13},{5,9},{9,5},{13,1},{2,14},{6,10},... | collective-permute-start | bytes 49160 | tf_op jit(solution)/shard_map/ppermute | solution.py:53
  193.0 64.7 %collective-permute-start.19 = (bf16[3,192,1536]{2,1,0:T(8,128)(2,1)S(1)}, bf16[3,192,1536]{2,1,0:T(8,128)(2,1)S(1)}, u32[]{:S(2)}, u32[]{:S(2)}) collective-permute-start(bf16[3,192,1536]{2,1,0:T(8,128)(2,1)S(1)} %get-tuple-element.62.refs_2_), channel_id=1, source_target_pairs={{0,16},{16,0},{1,17},{17,1},{2,18},{18,2},{3,19},{19,3},{4,20},{20... | collective-permute-start | bytes 5308424 | tf_op jit(solution)/shard_map/ppermute | solution.py:27
  207.7 174.4 %collective-permute-start.30 = (bf16[3,192,1536]{2,1,0:T(8,128)(2,1)}, bf16[3,192,1536]{2,1,0:T(8,128)(2,1)}, u32[]{:S(2)}, u32[]{:S(2)}) collective-permute-start(bf16[3,192,1536]{2,1,0:T(8,128)(2,1)} %get-tuple-element.67.refs_2_), channel_id=1, source_target_pairs={{0,1},{1,0},{2,3},{3,2},{4,5},{5,4},{6,7},{7,6},{8,9},{9,8},{10,11... | collective-permute-start | bytes 5308424 | tf_op jit(solution)/shard_map/ppermute | solution.py:42
  257.6 124.9 %collective-permute-start.31 = (bf16[3,192,1536]{2,1,0:T(8,128)(2,1)}, bf16[3,192,1536]{2,1,0:T(8,128)(2,1)}, u32[]{:S(2)}, u32[]{:S(2)}) collective-permute-start(bf16[3,192,1536]{2,1,0:T(8,128)(2,1)} %get-tuple-element.67.refs_2_), channel_id=1, source_target_pairs={{0,2},{1,3},{2,0},{3,1},{4,6},{5,7},{6,4},{7,5},{8,10},{9,11},{10,... | collective-permute-start | bytes 5308424 | tf_op jit(solution)/shard_map/ppermute | solution.py:42
  259.1 129.7 %collective-permute-start.32 = (bf16[3,192,1536]{2,1,0:T(8,128)(2,1)}, bf16[3,192,1536]{2,1,0:T(8,128)(2,1)}, u32[]{:S(2)}, u32[]{:S(2)}) collective-permute-start(bf16[3,192,1536]{2,1,0:T(8,128)(2,1)} %get-tuple-element.67.refs_2_), channel_id=1, source_target_pairs={{0,3},{1,2},{2,1},{3,0},{4,7},{5,6},{6,5},{7,4},{8,11},{9,10},{10,... | collective-permute-start | bytes 5308424 | tf_op jit(solution)/shard_map/ppermute | solution.py:42
  260.6 132.7 %collective-permute-start.29 = (bf16[1536,1536]{1,0:T(8,128)(2,1)}, bf16[1536,1536]{1,0:T(8,128)(2,1)}, u32[]{:S(2)}, u32[]{:S(2)}) collective-permute-start(bf16[1536,1536]{1,0:T(8,128)(2,1)} %constant_dynamic-update-slice_fusion.mine), channel_id=1, source_target_pairs={{0,16},{16,0},{1,17},{17,1},{2,18},{18,2},{3,19},{19,3},{4,20},{20... | collective-permute-start | bytes 14155784 | tf_op jit(solution)/shard_map/ppermute | solution.py:27
  387.2 305.7 %reduce-scatter.2.cloned.1.call-start = ((), (), s32[]{:S(2)}) async-start(), calls=%async_computation.2 | async-start | bytes 3932160 | tf_op jit(solution)/shard_map/reduce_scatter | solution.py:556
  388.7 59.4 %collective-permute-start.33 = (bf16[3,192,1536]{2,1,0:T(8,128)(2,1)}, bf16[3,192,1536]{2,1,0:T(8,128)(2,1)}, u32[]{:S(2)}, u32[]{:S(2)}) collective-permute-start(bf16[3,192,1536]{2,1,0:T(8,128)(2,1)} %get-tuple-element.67.refs_2_), channel_id=1, source_target_pairs={{0,16},{16,0},{1,17},{17,1},{2,18},{18,2},{3,19},{19,3},{4,20},{20... | collective-permute-start | bytes 5308424 | tf_op jit(solution)/shard_map/ppermute | solution.py:27
  388.8 59.3 %collective-permute-start.34 = (bf16[3,192,1536]{2,1,0:T(8,128)(2,1)}, bf16[3,192,1536]{2,1,0:T(8,128)(2,1)}, u32[]{:S(2)}, u32[]{:S(2)}) collective-permute-start(bf16[3,192,1536]{2,1,0:T(8,128)(2,1)} %collective-permute-done.30.refs_3_), channel_id=1, source_target_pairs={{0,16},{16,0},{1,17},{17,1},{2,18},{18,2},{3,19},{19,3},{4,20},{20... | collective-permute-start | bytes 5308424 | tf_op jit(solution)/shard_map/ppermute | solution.py:27
  390.7 57.4 %collective-permute-start.35 = (bf16[3,192,1536]{2,1,0:T(8,128)(2,1)}, bf16[3,192,1536]{2,1,0:T(8,128)(2,1)}, u32[]{:S(2)}, u32[]{:S(2)}) collective-permute-start(bf16[3,192,1536]{2,1,0:T(8,128)(2,1)} %collective-permute-done.31.refs_4_), channel_id=1, source_target_pairs={{0,16},{16,0},{1,17},{17,1},{2,18},{18,2},{3,19},{19,3},{4,20},{20... | collective-permute-start | bytes 5308424 | tf_op jit(solution)/shard_map/ppermute | solution.py:27
  392.1 56.1 %collective-permute-start.36 = (bf16[3,192,1536]{2,1,0:T(8,128)(2,1)}, bf16[3,192,1536]{2,1,0:T(8,128)(2,1)}, u32[]{:S(2)}, u32[]{:S(2)}) collective-permute-start(bf16[3,192,1536]{2,1,0:T(8,128)(2,1)} %collective-permute-done.32.refs_5_), channel_id=1, source_target_pairs={{0,16},{16,0},{1,17},{17,1},{2,18},{18,2},{3,19},{19,3},{4,20},{20... | collective-permute-start | bytes 5308424 | tf_op jit(solution)/shard_map/ppermute | solution.py:27
  609.5 86.1 %collective-permute-start.40 = (bf16[4,3,192,1536]{3,2,1,0:T(8,128)(2,1)}, bf16[4,3,192,1536]{3,2,1,0:T(8,128)(2,1)}, u32[]{:S(2)}, u32[]{:S(2)}) collective-permute-start(bf16[4,3,192,1536]{3,2,1,0:T(8,128)(2,1)} %get-tuple-element.77), channel_id=1, source_target_pairs={{0,16},{16,0},{1,17},{17,1},{2,18},{18,2},{3,19},{19,3},{4,20},{20... | collective-permute-start | bytes 21233672 | tf_op jit(solution)/shard_map/ppermute | solution.py:27
  634.7 373.4 %all-reduce.3.cloned.1.call-start = ((), (), s32[]{:S(2)}) async-start(), calls=%async_computation.3 | async-start | bytes 2850816 | tf_op jit(solution)/shard_map/psum | solution.py:725
  709.6 121.2 %collective-permute-start.44 = (bf16[1040,1536]{1,0:T(8,128)(2,1)}, bf16[1040,1536]{1,0:T(8,128)(2,1)}, u32[]{:S(2)}, u32[]{:S(2)}) collective-permute-start(bf16[1040,1536]{1,0:T(8,128)(2,1)} %pad_maximum_fusion.5), channel_id=1, source_target_pairs={{0,3},{1,2},{2,1},{3,0},{4,7},{5,6},{6,5},{7,4},{8,11},{9,10},{10,... | collective-permute-start | bytes 9584648 | tf_op jit(solution)/shard_map/ppermute | solution.py:42
  711.9 138.0 %collective-permute-start.43 = (bf16[1040,1536]{1,0:T(8,128)(2,1)}, bf16[1040,1536]{1,0:T(8,128)(2,1)}, u32[]{:S(2)}, u32[]{:S(2)}) collective-permute-start(bf16[1040,1536]{1,0:T(8,128)(2,1)} %pad_maximum_fusion.4), channel_id=1, source_target_pairs={{0,2},{1,3},{2,0},{3,1},{4,6},{5,7},{6,4},{7,5},{8,10},{9,11},{10,... | collective-permute-start | bytes 9584648 | tf_op jit(solution)/shard_map/ppermute | solution.py:42
  712.5 137.5 %collective-permute-start.42 = (bf16[1040,1536]{1,0:T(8,128)(2,1)}, bf16[1040,1536]{1,0:T(8,128)(2,1)}, u32[]{:S(2)}, u32[]{:S(2)}) collective-permute-start(bf16[1040,1536]{1,0:T(8,128)(2,1)} %pad_maximum_fusion.3), channel_id=1, source_target_pairs={{0,1},{1,0},{2,3},{3,2},{4,5},{5,4},{6,7},{7,6},{8,9},{9,8},{10,11... | collective-permute-start | bytes 9584648 | tf_op jit(solution)/shard_map/ppermute | solution.py:42
  830.8 102.7 %collective-permute-start.58 = (bf16[4,3,192,1536]{3,2,1,0:T(8,128)(2,1)}, bf16[4,3,192,1536]{3,2,1,0:T(8,128)(2,1)}, u32[]{:S(2)}, u32[]{:S(2)}) collective-permute-start(bf16[4,3,192,1536]{3,2,1,0:T(8,128)(2,1)} %get-tuple-element.104), channel_id=1, source_target_pairs={{0,16},{16,0},{1,17},{17,1},{2,18},{18,2},{3,19},{19,3},{4,20},{20... | collective-permute-start | bytes 21233672 | tf_op jit(solution)/shard_map/ppermute | solution.py:27
  863.3 60.7 %collective-permute-start.45 = (bf16[256,1536]{1,0:T(8,128)(2,1)}, bf16[256,1536]{1,0:T(8,128)(2,1)}, u32[]{:S(2)}, u32[]{:S(2)}) collective-permute-start(bf16[256,1536]{1,0:T(8,128)(2,1)} %broadcast_select_fusion.16), channel_id=1, source_target_pairs={{0,16},{16,0},{1,17},{17,1},{2,18},{18,2},{3,19},{19,3},{4,20},{20... | collective-permute-start | bytes 2359304 | tf_op jit(solution)/shard_map/ppermute | solution.py:27
  893.1 178.7 %all-reduce.5.cloned.1.call-start = ((), (), s32[]{:S(2)}) async-start(), calls=%async_computation.4 | async-start | bytes 2850816 | tf_op jit(solution)/shard_map/psum | solution.py:732
  942.8 63.3 %collective-permute-start.52 = (bf16[464,1536]{1,0:T(8,128)(2,1)S(1)}, bf16[464,1536]{1,0:T(8,128)(2,1)S(1)}, u32[]{:S(2)}, u32[]{:S(2)}) collective-permute-start(bf16[464,1536]{1,0:T(8,128)(2,1)S(1)} %get-tuple-element.157), channel_id=1, source_target_pairs={{0,2},{1,3},{2,0},{3,1},{4,6},{5,7},{6,4},{7,5},{8,10},{9,11},{10,... | collective-permute-start | bytes 4276232 | tf_op jit(solution)/shard_map/ppermute | solution.py:42
  944.0 62.0 %collective-permute-start.51 = (bf16[464,1536]{1,0:T(8,128)(2,1)S(1)}, bf16[464,1536]{1,0:T(8,128)(2,1)S(1)}, u32[]{:S(2)}, u32[]{:S(2)}) collective-permute-start(bf16[464,1536]{1,0:T(8,128)(2,1)S(1)} %get-tuple-element.155), channel_id=1, source_target_pairs={{0,1},{1,0},{2,3},{3,2},{4,5},{5,4},{6,7},{7,6},{8,9},{9,8},{10,11... | collective-permute-start | bytes 4276232 | tf_op jit(solution)/shard_map/ppermute | solution.py:42
  1013.0 77.2 %collective-permute-start.64 = (bf16[2,192,1536]{2,1,0:T(8,128)(2,1)}, bf16[2,192,1536]{2,1,0:T(8,128)(2,1)}, u32[]{:S(2)}, u32[]{:S(2)}) collective-permute-start(bf16[2,192,1536]{2,1,0:T(8,128)(2,1)} %slice_bitcast_fusion.5), channel_id=1, source_target_pairs={{0,3},{1,2},{2,1},{3,0},{4,7},{5,6},{6,5},{7,4},{8,11},{9,10},{10,... | collective-permute-start | bytes 3538952 | tf_op jit(solution)/shard_map/ppermute | solution.py:42
  1014.3 75.9 %collective-permute-start.63 = (bf16[2,192,1536]{2,1,0:T(8,128)(2,1)}, bf16[2,192,1536]{2,1,0:T(8,128)(2,1)}, u32[]{:S(2)}, u32[]{:S(2)}) collective-permute-start(bf16[2,192,1536]{2,1,0:T(8,128)(2,1)} %slice_bitcast_fusion.6), channel_id=1, source_target_pairs={{0,2},{1,3},{2,0},{3,1},{4,6},{5,7},{6,4},{7,5},{8,10},{9,11},{10,... | collective-permute-start | bytes 3538952 | tf_op jit(solution)/shard_map/ppermute | solution.py:42
  1015.7 74.5 %collective-permute-start.62 = (bf16[2,192,1536]{2,1,0:T(8,128)(2,1)}, bf16[2,192,1536]{2,1,0:T(8,128)(2,1)}, u32[]{:S(2)}, u32[]{:S(2)}) collective-permute-start(bf16[2,192,1536]{2,1,0:T(8,128)(2,1)} %slice_bitcast_fusion.7), channel_id=1, source_target_pairs={{0,1},{1,0},{2,3},{3,2},{4,5},{5,4},{6,7},{7,6},{8,9},{9,8},{10,11... | collective-permute-start | bytes 3538952 | tf_op jit(solution)/shard_map/ppermute | solution.py:42
  1017.4 71.4 %collective-permute-start.60 = (bf16[1,192,1536]{2,1,0:T(8,128)(2,1)}, bf16[1,192,1536]{2,1,0:T(8,128)(2,1)S(1)}, u32[]{:S(2)}, u32[]{:S(2)}) collective-permute-start(bf16[1,192,1536]{2,1,0:T(8,128)(2,1)} %slice_bitcast_fusion.11), channel_id=1, source_target_pairs={{0,2},{1,3},{2,0},{3,1},{4,6},{5,7},{6,4},{7,5},{8,10},{9,11},{10,... | collective-permute-start | bytes 1769480 | tf_op jit(solution)/shard_map/ppermute | solution.py:42
  1027.5 61.4 %collective-permute-start.59 = (bf16[1,192,1536]{2,1,0:T(8,128)(2,1)}, bf16[1,192,1536]{2,1,0:T(8,128)(2,1)S(1)}, u32[]{:S(2)}, u32[]{:S(2)}) collective-permute-start(bf16[1,192,1536]{2,1,0:T(8,128)(2,1)} %slice_bitcast_fusion.12), channel_id=1, source_target_pairs={{0,1},{1,0},{2,3},{3,2},{4,5},{5,4},{6,7},{7,6},{8,9},{9,8},{10,11... | collective-permute-start | bytes 1769480 | tf_op jit(solution)/shard_map/ppermute | solution.py:42
  (153 other events, 3162.8 us)
Sparse Core Ops, SparseCore 0:
  387.3 60.7 all-gather.1
  634.9 58.0 reduce-scatter.1
  893.2 63.5 all-reduce.2
  1008.3 63.4 all-reduce.4

commit v3 on v2

--- a/solution.py
+++ b/solution.py
@@ -122,10 +122,11 @@
     sub = rows // SUB
     me = lax.axis_index(D)
 
-    small = pieces[0].shape[1]
+    small = w.shape[1] // 8
     for i in range(3):
         for k, one in enumerate(pieces):
-            pltpu.make_async_copy(one.at[i], w.at[i, pl.ds(k * small, small)], w_sem.at[i]).start()
+            rows_at = pl.ds(one.shape[0] - (3 - i) * small, small)
+            pltpu.make_async_copy(one.at[rows_at], w.at[i, pl.ds(k * small, small)], w_sem.at[i]).start()
     loads = []
     if saved is not None:
         loads = [pltpu.make_async_copy(a, o, io_sem.at[i]) for i, (a, o) in enumerate(zip(saved, (gate, up, act, second)))]
@@ -369,9 +370,8 @@
                 left(b, s).wait_send()
 
 
-def experts(n, forward, backward, x, share, pieces, *more):
+def experts(n, forward, backward, x, share, small, pieces, *more):
     rows, width = x.shape
-    small = pieces[0].shape[1]
     hidden = small * 8
     shape = lambda *dims: jax.ShapeDtypeStruct(dims, BF)
     whole, wide = shape(n, rows, width), shape(n, rows, hidden)
@@ -524,7 +524,7 @@
     )(*operands)
 
 
-def keys_and_values(x, p, c):
+def keys_and_values(x, p, c, *before):
     rows = x.shape[0]
     xf = x.astype(F32)
     normed = low(xf * inverse_rms(xf) * p["ga"])
@@ -532,7 +532,7 @@
     cosine, sine = c["rope"]
     keys = rotate(kv[:, :GROUPS], cosine[:, None], sine[:, None])
     kv = low(jnp.concatenate([keys, kv[:, GROUPS:]], 1)).reshape(rows, -1)
-    return normed, jnp.concatenate(pieces_of(kv))
+    return normed, jnp.concatenate(pieces_of(after(kv, *before)))
 
 
 def attention_forward(x, normed, kv, p, c):
@@ -557,7 +557,7 @@
 
 
 def weights_of(p):
-    f = jnp.stack(p["pieces"])
+    f = jnp.stack([v[-3 * p["unit"] :].reshape(3, p["unit"], -1) for v in p["pieces"]])
     return tuple(f[:, i].reshape(-1, f.shape[-1]) for i in range(3))
 
 
@@ -567,7 +567,7 @@
 
 def mix_forward(mixer, p, n):
     if n <= SMALL:
-        y, tokens, act, gate, up = experts(n, True, False, mixer, p["wide"], p["pieces"])
+        y, tokens, act, gate, up = experts(n, True, False, mixer, p["wide"], p["unit"], p["pieces"])
         return y, dict(tokens=tokens, act=act, gate=gate, up=up)
     wg, wu, wd = weights_of(p)
     tokens = along(mixer)
@@ -580,7 +580,7 @@
 def mix_backward(grad, k, p, n):
     if n <= SMALL:
         saved = (k["gate"], k["up"], k["act"], k["tokens"])
-        return experts(n, False, True, grad, p["wide"], p["pieces"], *saved)
+        return experts(n, False, True, grad, p["wide"], p["unit"], p["pieces"], *saved)
     wg, wu, wd = weights_of(p)
     grads = along(grad)
     da = dot(grads, wd, (1,), (1,)) * share_of(p, wd.shape[0])
@@ -595,17 +595,16 @@
     return gm, gw[:4], gw[4:]
 
 
-def mix_both(mixer, grad, p, n):
+def mix_both(mixer, grad, p, n, grads):
     if n <= SMALL:
-        grads = along(grad).reshape(n, *grad.shape)
-        gm, part, keep, give = experts(n, True, True, mixer, p["wide"], p["pieces"], grads)
-        y = scatter_along(part).astype(F32)
-        return y, gm, keep, give
+        grads = grads.reshape(n, *grad.shape)
+        gm, part, keep, give = experts(n, True, True, mixer, p["wide"], p["unit"], p["pieces"], grads)
+        return part, gm, keep, give
     y, k = mix_forward(mixer, p, n)
     return (y,) + mix_backward(grad, k, p, n)
 
 
-def attention_backward(grad, grad_mixer, k, p, c, first):
+def attention_backward(grad, grad_mixer, k, p, c, first, early):
     rows, width = grad.shape
     cosine, sine = c["rope"]
     wide, length = (rows, HEADS * HEAD), c["bias"].shape[1]
@@ -616,8 +615,10 @@
         grad, grad_mixer, k["hidden"], p["gm"].reshape(1, -1), k["queries"], k["kv"], k["logs"], c["bias"],
         k["flat"], cosine, sine, p["mine"], p["other"],
     )
-    gkv = gkv.reshape(4, rows, -1)
+    gkv, early = lax.optimization_barrier((gkv.reshape(4, rows, -1), early))
+    part = summed([v[:1] for v in early]) if early else ()
     gkv = gkv[0].astype(F32) + sum(hop(gkv[r], r).astype(F32) for r in (1, 2, 3))
+    gkv, part = lax.optimization_barrier((gkv, part))
     gkv = gkv.reshape(rows, 2 * GROUPS, HEAD)
     cosine, sine = cosine[:, None], sine[:, None]
     gkv = jnp.concatenate([rotate(gkv[:, :GROUPS], cosine, -sine), gkv[:, GROUPS:]], 1)
@@ -638,7 +639,7 @@
 
     q, o = rows_of(gw_q, 0, g_ga), rows_of(gw_out, 1, g_gm[0])
     parts = over_sections(jnp.where(first, q, o), jnp.where(first, o, q))
-    return grad_hidden + more, parts
+    return grad_hidden + more, parts, part, early
 
 
 def on_device(
@@ -672,7 +673,7 @@
     def factors(own, l):
         share = own[:, l]
         share = lax.dynamic_slice_in_dim(share, lax.axis_index(D) * here, here, 1)
-        share = jnp.where(first, share, share[:, ::-1])
+        share = jnp.stack([jnp.where(first, share[:, i], share[:, 1 - i]) for i in range(2)], 1)
         return jnp.broadcast_to(share.T.reshape(here, -1, rows, 1), (here, share.shape[0] // rows, rows, HEAD)), share
 
     queries_at = at * rows + jnp.arange(rows)
@@ -687,55 +688,55 @@
     kv = both(first, jnp.concatenate([key_weight[0], value_weight[0]], 1))
     ga = both(first, attn_gain)
     gm = both(first, mixer_gain)
-    params = []
-    last = None
-    small = [dict(kv=kv[l], ga=ga[l], gm=gm[l]) for l in range(2)]
+    n = lax.axis_size(D)
+    small = [dict(kv=kv[l], ga=ga[l], gm=gm[l], unit=hidden) for l in range(2)]
+    for l, one in enumerate(small):
+        one["wide"], one["share"] = factors(shares, l)
+    grads = along(low(grad1)) if n <= SMALL else low(grad1)
+    ffn = [v.reshape(-1, width) for v in ffn]
+    high = w_out.shape[1]
+
     ahead = keys_and_values(x0, small[0], c)
-    for l in range(2):
-        own = attn[l] if last is None else after(attn[l], last)
-        got = pieces_of(own)
-        if last is None:
-            ffn = after(ffn, got, ahead)
-        mine = jnp.concatenate(got)
-        wide, share = factors(shares, l)
-        got = pieces_of(ffn[l] if last is None else after(ffn[l], last))
-        last = got
-        params.append(
-            dict(
-                small[l], mine=mine, other=partner(mine), share=share, wide=wide,
-                pieces=got + [partner(v) for v in got],
-            )
-        )
-    n = lax.axis_size(D)
-    hidden0, mixer, k0 = attention_forward(x0, *ahead, params[0], c)
-    y, kept = mix_forward(mixer, params[0], n)
+    got = pieces_of(attn[0])
+    late = after(ffn[0], got, ahead, grads)
+    mine = jnp.concatenate(got)
+    small[0].update(mine=mine, other=partner(mine))
+    hidden0, mixer, k0 = attention_forward(x0, *ahead, small[0], c)
+    got = pieces_of(late)
+    crossed = after(got, mixer)
+    small[0].update(pieces=got + [partner(v) for v in crossed])
+    more = pieces_of(after(jnp.concatenate([attn[1], ffn[1]]), got))
+    y, kept = mix_forward(mixer, small[0], n)
     y0 = low((hidden0 + y))
-    hidden1, mixer, k1 = attention_forward(y0, *keys_and_values(y0, params[1], c), params[1], c)
-    y, gm, keep, give = mix_both(mixer, low(grad1), params[1], n)
-    y1 = low(hidden1 + y)
+    other = [partner(v) for v in after(more, y)]
+    small[1].update(
+        mine=jnp.concatenate([v[:high] for v in more]), other=jnp.concatenate([v[:high] for v in other]),
+        pieces=more + other,
+    )
+    hidden1, mixer, k1 = attention_forward(y0, *keys_and_values(y0, small[1], c, other), small[1], c)
+    y, gm, keep, give = mix_both(mixer, low(grad1), small[1], n, grads)
     parts = over_sections(keep, give)
-    gx1, more = attention_backward(grad1, gm, k1, params[1], c, first)
+    gx1, more, _, _ = attention_backward(grad1, gm, k1, small[1], c, first, [])
     gb = low(gx1)
     rows_f = 3 * hidden
     both_parts = [jnp.concatenate([a.reshape(rows_f, width), b]) for a, b in zip(parts, more)]
     gb, both_parts = lax.optimization_barrier((gb, both_parts))
     got = summed(both_parts)
-    gm, keep, give = mix_backward(gb, kept, params[0], n)
-    gm, got, y1 = lax.optimization_barrier((gm, got, y1))
+    gm, keep, give = mix_backward(gb, kept, small[0], n)
+    gm, got, y = lax.optimization_barrier((gm, got, y))
+    y1 = low(hidden1 + (scatter_along(y).astype(F32) if n <= SMALL else y))
     f1, s1 = got[:rows_f].reshape(3, hidden, width), lax.psum(got[rows_f:], D)
     parts = over_sections(keep, give)
-    part_a = summed([v[:1] for v in parts])
-    gx0, more = attention_backward(gb.astype(F32), gm, k0, params[0], c, first)
+    gx0, more, part_a, parts = attention_backward(gb.astype(F32), gm, k0, small[0], c, first, parts)
     s0 = summed(more)
     part_b = summed(after([v[1:] for v in parts], s0))
     f0 = jnp.concatenate([part_a, part_b])
-    s0 = lax.psum(after(s0, s1), D)
+    s0 = lax.psum(after(s0, s1, y1), D)
 
     outs = jnp.stack(swap(first, y0, y1))
     input_grads = jnp.stack(swap(first, low(gx0), low(gx1))).astype(F32)
     f = jnp.stack(swap(first, f0, f1)).astype(F32)
     zero, one = swap(first, s0, s1)
-    high = w_out.shape[1]
     q, o = zero[:high].astype(F32), one[:high].astype(F32)
     less = jnp.stack(pieces_of(jnp.stack([zero[high:], one[high:]])))
     less = jnp.concatenate([lax.dynamic_index_in_dim(less, at ^ i, 0, False) for i in range(4)], 1).astype(F32)

time: 1150 us -> 1060 us (0.922)
  waiting for transfers between devices: 389 us -> 306 us
  other arithmetic: 112 us -> 130 us
    reduce_scatter x1, waiting for transfers between devices: 44.7 us -> 0.01 us  [scatter_along(): lax.psum_scatter(low(values.reshape(-1, values.shape[-1])), D, scatter_di...]
    all_gather x1, waiting for transfers between devices: 30.3 us -> 0.01 us  [along(): return lax.all_gather(low(values), D, axis=0, tiled=True)]
    ppermute x39 -> x36, waiting for transfers between devices: 265 us -> 238 us  [hop(): lax.ppermute(values, T, [(i, i ^ bit) for i in range(lax.axis_size(T))])]
    unnamed x236 -> x258, local copies, waits for them, and re-layouts: 38.3 us -> 23 us
    slice x5 -> x11, local copies, waits for them, and re-layouts: 4.93 us -> 17.4 us  [the longest x8 14 us: on_device(): v[:high]]
    ppermute x39 -> x36, starting transfers between devices: 50.1 us -> 42.8 us  [hop(): lax.ppermute(values, T, [(i, i ^ bit) for i in range(lax.axis_size(T))])]
    convert_element_type x20 -> x19, other arithmetic: 40.1 us -> 43.7 us  [low(): return lax.reduce_precision(values.astype(F32), 8, 7).astype(BF)]
  transfers between devices with their start and end apart: 70 -> 66, of which waited for: 27 -> 25; matrix products, arithmetic and copies ran while one was open for 15% -> 17% of each run, Pallas kernels for 26% -> 25%
where the time goes in v3:
time: 1060 us
  Pallas kernels  452 us (43%)
  waiting for transfers between devices  306 us (29%)
  other arithmetic  130 us (12%)
  local copies, waits for them, and re-layouts  72.9 us (7%)
  starting transfers between devices  55.4 us (5%)
  matrix products  25.1 us (2%)
  between operations  16 us (2%)
    pallas_call x3, Pallas kernels, experts(): pl.pallas_call(functools.partial(expert_kernel, n, forward, backward), ou...  353 us
    ppermute x36, waiting for transfers between devices, hop(): lax.ppermute(values, T, [(i, i ^ bit) for i in range(lax.axis_size(T))])  238 us
    pallas_call x4, Pallas kernels, local_call(): pl.pallas_call(body, out_shape=[jax.ShapeDtypeStruct(*o) for o in out], i...  99.7 us
    psum x1, waiting for transfers between devices, on_device(): s0 = lax.psum(after(s0, s1, y1), D)  52.4 us
    convert_element_type x19, other arithmetic, low(): return lax.reduce_precision(values.astype(F32), 8, 7).astype(BF)  43.7 us
    ppermute x36, starting transfers between devices, hop(): lax.ppermute(values, T, [(i, i ^ bit) for i in range(lax.axis_size(T))])  42.8 us
    dot_general x10, matrix products, dot(): lax.dot_general(a, b, ((ca, cb), ((), ())), preferred_element_type=F32)  25.1 us
    unnamed x258, local copies, waits for them, and re-layouts  23 us
  transfers between devices with their start and end apart: 66, of which 25 were waited for; matrix products, arithmetic and copies ran while one was open for 17% of the time, Pallas kernels for 25%

profile of v3, /device:TPU:0, one launch (start us, length us, event | category | flops | bytes accessed | tf_op | source)
XLA Modules:
  0.0 1058.0 jit_solution(1366995529434114645)
XLA Ops:
  24.7 24.9 %collective-permute-done.9 = bf16[384,1536]{1,0:T(8,128)(2,1)S(1)} collective-permute-done((bf16[384,1536]{1,0:T(8,128)(2,1)}, bf16[384,1536]{1,0:T(8,128)(2,1)S(1)}, u32[]{:S(2)}, u32[]{:S(2)}) %collective-permute-start.9) | collective-permute-done | bytes 1179680 | tf_op jit(solution)/shard_map/ppermute | solution.py:42
  49.6 25.1 %collective-permute-done.8 = bf16[384,1536]{1,0:T(8,128)(2,1)} collective-permute-done((bf16[384,1536]{1,0:T(8,128)(2,1)}, bf16[384,1536]{1,0:T(8,128)(2,1)}, u32[]{:S(2)}, u32[]{:S(2)}) %collective-permute-start.8) | collective-permute-done | bytes 1179680 | tf_op jit(solution)/shard_map/ppermute | solution.py:42
  75.1 4.8 pad_maximum_fusion.mine
  104.1 5.3 collective-permute-done.3
  117.4 20.8 %shard_map.221 = (f32[256,1536]{1,0:T(8,128)}, bf16[256,1536]{1,0:T(8,128)(2,1)S(1)}, bf16[256,1536]{1,0:T(8,128)(2,1)S(1)}, bf16[256,1536]{1,0:T(8,128)(2,1)S(1)}, f32[256,1536]{1,0:T(8,128)}) custom-call(bf16[256,1536]{1,0:T(8,128)(2,1)S(1)} %get-tuple-element.176.x, bf16[256,1536]{1,0:T(8,128)(2,1)S(1)} %fusion.33.normed, ...), custom_call_target="tpu_custom_call" | custom-call | flops 99999997952 | bytes 20000000 | tf_op jit(solution)/shard_map/pallas_call | solution.py:517
  140.9 12.5 %collective-permute-done.16.refs_3_ = bf16[576,1536]{1,0:T(8,128)(2,1)} collective-permute-done((bf16[576,1536]{1,0:T(8,128)(2,1)S(1)}, bf16[576,1536]{1,0:T(8,128)(2,1)}, u32[]{:S(2)}, u32[]{:S(2)}) %collective-permute-start.16) | collective-permute-done | bytes 1769504 | tf_op jit(solution)/shard_map/ppermute | solution.py:42
  153.3 38.2 %collective-permute-done.17.refs_4_ = bf16[576,1536]{1,0:T(8,128)(2,1)} collective-permute-done((bf16[576,1536]{1,0:T(8,128)(2,1)S(1)}, bf16[576,1536]{1,0:T(8,128)(2,1)}, u32[]{:S(2)}, u32[]{:S(2)}) %collective-permute-start.17) | collective-permute-done | bytes 1769504 | tf_op jit(solution)/shard_map/ppermute | solution.py:42
  198.9 3.8 collective-permute-done.13
  214.8 107.6 %shard_map.222 = (f32[256,1536]{1,0:T(8,128)S(1)}, bf16[4,256,1536]{2,1,0:T(8,128)(2,1)}, bf16[4,256,1536]{2,1,0:T(8,128)(2,1)}, bf16[4,256,1536]{2,1,0:T(8,128)(2,1)}, bf16[4,256,1536]{2,1,0:T(8,128)(2,1)}) custom-call(bf16[256,1536]{1,0:T(8,128)(2,1)S(1)} %copy-done.31, f32[2,4,256,128]{3,2,1,0:T(8,128)S(1)} %broadcast_in_dim.97.refs_1_, ...), custom_call_target="tpu_custom_call" | custom-call | flops 399999991808 | bytes 100000000 | tf_op jit(solution)/shard_map/pallas_call | solution.py:389
  323.6 12.6 %collective-permute-done.24.refs_4_ = bf16[960,1536]{1,0:T(8,128)(2,1)} collective-permute-done((bf16[960,1536]{1,0:T(8,128)(2,1)}, bf16[960,1536]{1,0:T(8,128)(2,1)}, u32[]{:S(2)}, u32[]{:S(2)}) %collective-permute-start.24) | collective-permute-done | bytes 2949152 | tf_op jit(solution)/shard_map/ppermute | solution.py:42
  370.8 21.1 %shard_map.223 = (f32[256,1536]{1,0:T(8,128)}, bf16[256,1536]{1,0:T(8,128)(2,1)S(1)}, bf16[256,1536]{1,0:T(8,128)(2,1)S(1)}, bf16[256,1536]{1,0:T(8,128)(2,1)S(1)}, f32[256,1536]{1,0:T(8,128)}) custom-call(bf16[256,1536]{1,0:T(8,128)(2,1)S(1)} %get-tuple-element.172.x, bf16[256,1536]{1,0:T(8,128)(2,1)S(1)} %fusion.43.normed, ...), custom_call_target="tpu_custom_call" | custom-call | flops 99999997952 | bytes 20000000 | tf_op jit(solution)/shard_map/pallas_call | solution.py:517
  392.3 131.0 %shard_map.224 = (f32[256,1536]{1,0:T(8,128)S(1)}, bf16[4,256,1536]{2,1,0:T(8,128)(2,1)}, bf16[4,3,192,1536]{3,2,1,0:T(8,128)(2,1)}, bf16[4,3,192,1536]{3,2,1,0:T(8,128)(2,1)}) custom-call(bf16[256,1536]{1,0:T(8,128)(2,1)S(1)} %get-tuple-element.89.refs_0_, f32[2,4,256,128]{3,2,1,0:T(8,128)S(1)} %broadcast_in_dim.99.refs_1_, ...), custom_call_target="tpu_custom_call" | custom-call | flops 399999991808 | bytes 100000000 | tf_op jit(solution)/shard_map/pallas_call | solution.py:389
  524.5 32.9 %shard_map.225 = (f32[256,1536]{1,0:T(8,128)}, bf16[256,1536]{1,0:T(8,128)(2,1)S(1)}, bf16[1024,512]{1,0:T(8,128)(2,1)S(1)}, bf16[1536,1536]{1,0:T(8,128)(2,1)}, f32[1,1536]{1,0:T(1,128)S(1)}) custom-call(f32[256,1536]{1,0:T(8,128)} %get-tuple-element.174.grad, f32[256,1536]{1,0:T(8,128)} %copy-done.25, f32[256,1536]{1,0:T(8,128)} %get-tuple-element.88.hidden, ...), custom_call_target="tpu_custom_call" | custom-call | flops 99999997952 | bytes 20000000 | tf_op jit(solution)/shard_map/pallas_call | solution.py:517
  576.7 4.1 fusion.50
  587.7 7.1 collective-permute-done.37
  598.2 4.1 reduce-precision_convert_fusion.8
  613.3 114.1 %shard_map.226 = (f32[256,1536]{1,0:T(8,128)S(1)}, bf16[4,3,192,1536]{3,2,1,0:T(8,128)(2,1)}, bf16[4,3,192,1536]{3,2,1,0:T(8,128)(2,1)}) custom-call(bf16[256,1536]{1,0:T(8,128)(2,1)S(1)} %fusion.49.refs_0_, f32[2,4,256,128]{3,2,1,0:T(8,128)S(1)} %copy-done.15, bf16[576,1536]{1,0:T(8,128)(2,1)S(1)} %bitcast.245, ...), custom_call_target="tpu_custom_call" | custom-call | flops 399999991808 | bytes 100000000 | tf_op jit(solution)/shard_map/pallas_call | solution.py:389
  729.0 21.7 %collective-permute-done.39 = bf16[1040,1536]{1,0:T(8,128)(2,1)} collective-permute-done((bf16[1040,1536]{1,0:T(8,128)(2,1)}, bf16[1040,1536]{1,0:T(8,128)(2,1)}, u32[]{:S(2)}, u32[]{:S(2)}) %collective-permute-start.39) | collective-permute-done | bytes 3194912 | tf_op jit(solution)/shard_map/ppermute | solution.py:42
  750.7 8.1 reduce-precision_convert_fusion.2
  758.8 24.8 %shard_map.227 = (f32[256,1536]{1,0:T(8,128)}, bf16[256,1536]{1,0:T(8,128)(2,1)S(1)}, bf16[1024,512]{1,0:T(8,128)(2,1)S(1)}, bf16[1536,1536]{1,0:T(8,128)(2,1)}, f32[1,1536]{1,0:T(1,128)S(1)}) custom-call(f32[256,1536]{1,0:T(8,128)} %convert_element_type.551.grad, f32[256,1536]{1,0:T(8,128)} %copy-done.24, f32[256,1536]{1,0:T(8,128)} %get-tuple-element.74.hidden, ...), custom_call_target="tpu_custom_call" | custom-call | flops 99999997952 | bytes 20000000 | tf_op jit(solution)/shard_map/pallas_call | solution.py:517
  783.7 6.2 fusion.31
  808.0 11.4 %collective-permute-done.48 = bf16[1,192,1536]{2,1,0:T(8,128)(2,1)S(1)} collective-permute-done((bf16[1,192,1536]{2,1,0:T(8,128)(2,1)S(1)}, bf16[1,192,1536]{2,1,0:T(8,128)(2,1)S(1)}, u32[]{:S(2)}, u32[]{:S(2)}) %collective-permute-start.48) | collective-permute-done | bytes 589856 | tf_op jit(solution)/shard_map/ppermute | solution.py:42
  819.4 11.6 %collective-permute-done.47 = bf16[1,192,1536]{2,1,0:T(8,128)(2,1)S(1)} collective-permute-done((bf16[1,192,1536]{2,1,0:T(8,128)(2,1)S(1)}, bf16[1,192,1536]{2,1,0:T(8,128)(2,1)S(1)}, u32[]{:S(2)}, u32[]{:S(2)}) %collective-permute-start.47) | collective-permute-done | bytes 589856 | tf_op jit(solution)/shard_map/ppermute | solution.py:42
  836.2 4.5 fusion.40
  844.0 4.5 broadcast_select_fusion
  863.0 5.7 broadcast_select_fusion.1
  868.7 5.9 fusion.57
  883.3 26.7 %collective-permute-done.53 = bf16[464,1536]{1,0:T(8,128)(2,1)} collective-permute-done((bf16[464,1536]{1,0:T(8,128)(2,1)}, bf16[464,1536]{1,0:T(8,128)(2,1)}, u32[]{:S(2)}, u32[]{:S(2)}) %collective-permute-start.53) | collective-permute-done | bytes 1425440 | tf_op jit(solution)/shard_map/ppermute | solution.py:42
  910.0 29.6 %collective-permute-done.52 = bf16[464,1536]{1,0:T(8,128)(2,1)} collective-permute-done((bf16[464,1536]{1,0:T(8,128)(2,1)}, bf16[464,1536]{1,0:T(8,128)(2,1)}, u32[]{:S(2)}, u32[]{:S(2)}) %collective-permute-start.52) | collective-permute-done | bytes 1425440 | tf_op jit(solution)/shard_map/ppermute | solution.py:42
  939.6 5.1 fusion.9
  953.8 52.4 %all-reduce.5.cloned.1.call-done = bf16[464,1536]{1,0:T(8,128)(2,1)} async-done(((bf16[464,1536]{1,0:T(8,128)(2,1)}), bf16[464,1536]{1,0:T(8,128)(2,1)}) %all-reduce.5.cloned.1.call-update) | async-done | bytes 1425424 | tf_op jit(solution)/shard_map/psum | solution.py:734
  1033.8 8.5 collective-permute-done.56
  (533 shorter events, 245.2 us)
Async XLA Ops:
  7.2 104.6 %all-gather.2.cloned.1.call-start = ((), (), s32[]{:S(2)}) async-start(), calls=%async_computation.1 | async-start | bytes 3932160 | tf_op jit(solution)/shard_map/all_gather | solution.py:552
  10.9 74.9 %collective-permute-start = (f32[1,1536]{1,0:T(1,128)S(1)}, f32[1,1536]{1,0:T(1,128)S(1)}, u32[]{:S(2)}, u32[]{:S(2)}) collective-permute-start(f32[1,1536]{1,0:T(1,128)S(1)} %copy-done.111), channel_id=1, source_target_pairs={{0,16},{16,0},{1,17},{17,1},{2,18},{18,2},{3,19},{19,3},{4,20},{20... | collective-permute-start | bytes 18440 | tf_op jit(solution)/shard_map/ppermute | solution.py:27
  12.2 74.8 %collective-permute-start.1 = (bf16[1536,512]{1,0:T(8,128)(2,1)}, bf16[1536,512]{1,0:T(8,128)(2,1)}, u32[]{:S(2)}, u32[]{:S(2)}) collective-permute-start(bf16[1536,512]{1,0:T(8,128)(2,1)} %pad_maximum_fusion.11), channel_id=1, source_target_pairs={{0,16},{16,0},{1,17},{17,1},{2,18},{18,2},{3,19},{19,3},{4,20},{20... | collective-permute-start | bytes 4718600 | tf_op jit(solution)/shard_map/ppermute | solution.py:27
  15.7 864.3 %reduce-scatter.2.cloned.1.call-start = ((), (), s32[]{:S(2)}) async-start(), calls=%async_computation.2 | async-start | bytes 3932160 | tf_op jit(solution)/shard_map/reduce_scatter | solution.py:556
  19.1 30.5 %collective-permute-start.9 = (bf16[384,1536]{1,0:T(8,128)(2,1)}, bf16[384,1536]{1,0:T(8,128)(2,1)S(1)}, u32[]{:S(2)}, u32[]{:S(2)}) collective-permute-start(bf16[384,1536]{1,0:T(8,128)(2,1)} %get-tuple-element.204), channel_id=1, source_target_pairs={{0,3},{1,2},{2,1},{3,0},{4,7},{5,6},{6,5},{7,4},{8,11},{9,10},{10,... | collective-permute-start | bytes 3538952 | tf_op jit(solution)/shard_map/ppermute | solution.py:42
  22.5 52.2 %collective-permute-start.8 = (bf16[384,1536]{1,0:T(8,128)(2,1)}, bf16[384,1536]{1,0:T(8,128)(2,1)}, u32[]{:S(2)}, u32[]{:S(2)}) collective-permute-start(bf16[384,1536]{1,0:T(8,128)(2,1)} %get-tuple-element.204), channel_id=1, source_target_pairs={{0,2},{1,3},{2,0},{3,1},{4,6},{5,7},{6,4},{7,5},{8,10},{9,11},{10,... | collective-permute-start | bytes 3538952 | tf_op jit(solution)/shard_map/ppermute | solution.py:42
  23.0 52.0 %collective-permute-start.7 = (bf16[384,1536]{1,0:T(8,128)(2,1)}, bf16[384,1536]{1,0:T(8,128)(2,1)}, u32[]{:S(2)}, u32[]{:S(2)}) collective-permute-start(bf16[384,1536]{1,0:T(8,128)(2,1)} %get-tuple-element.204), channel_id=1, source_target_pairs={{0,1},{1,0},{2,3},{3,2},{4,5},{5,4},{6,7},{7,6},{8,9},{9,8},{10,11... | collective-permute-start | bytes 3538952 | tf_op jit(solution)/shard_map/ppermute | solution.py:42
  49.6 37.4 %collective-permute-start.5 = (f32[1,1536]{1,0:T(1,128)S(1)}, f32[1,1536]{1,0:T(1,128)S(1)}, u32[]{:S(2)}, u32[]{:S(2)}) collective-permute-start(f32[1,1536]{1,0:T(1,128)S(1)} %copy-done.112), channel_id=1, source_target_pairs={{0,16},{16,0},{1,17},{17,1},{2,18},{18,2},{3,19},{19,3},{4,20},{20... | collective-permute-start | bytes 18440 | tf_op jit(solution)/shard_map/ppermute | solution.py:27
  74.8 117.8 %collective-permute-start.11 = (f32[256,8]{0,1:T(8,128)S(1)}, f32[256,8]{0,1:T(8,128)S(1)}, u32[]{:S(2)}, u32[]{:S(2)}) collective-permute-start(f32[256,8]{0,1:T(8,128)S(1)} %fusion.85), channel_id=1, source_target_pairs={{0,16},{16,0},{1,17},{17,1},{2,18},{18,2},{3,19},{19,3},{4,20},{20... | collective-permute-start | bytes 24584 | tf_op jit(solution)/shard_map/ppermute | solution.py:27
  79.9 35.4 %collective-permute-start.10 = (bf16[1536,1536]{1,0:T(8,128)(2,1)}, bf16[1536,1536]{1,0:T(8,128)(2,1)}, u32[]{:S(2)}, u32[]{:S(2)}) collective-permute-start(bf16[1536,1536]{1,0:T(8,128)(2,1)} %pad_maximum_fusion.mine), channel_id=1, source_target_pairs={{0,16},{16,0},{1,17},{17,1},{2,18},{18,2},{3,19},{19,3},{4,20},{20... | collective-permute-start | bytes 14155784 | tf_op jit(solution)/shard_map/ppermute | solution.py:27
  111.8 41.6 %collective-permute-start.16 = (bf16[576,1536]{1,0:T(8,128)(2,1)S(1)}, bf16[576,1536]{1,0:T(8,128)(2,1)}, u32[]{:S(2)}, u32[]{:S(2)}) collective-permute-start(bf16[576,1536]{1,0:T(8,128)(2,1)S(1)} %bitcast.240), channel_id=1, source_target_pairs={{0,1},{1,0},{2,3},{3,2},{4,5},{5,4},{6,7},{7,6},{8,9},{9,8},{10,11... | collective-permute-start | bytes 5308424 | tf_op jit(solution)/shard_map/ppermute | solution.py:42
  113.2 78.3 %collective-permute-start.17 = (bf16[576,1536]{1,0:T(8,128)(2,1)S(1)}, bf16[576,1536]{1,0:T(8,128)(2,1)}, u32[]{:S(2)}, u32[]{:S(2)}) collective-permute-start(bf16[576,1536]{1,0:T(8,128)(2,1)S(1)} %bitcast.241), channel_id=1, source_target_pairs={{0,2},{1,3},{2,0},{3,1},{4,6},{5,7},{6,4},{7,5},{8,10},{9,11},{10,... | collective-permute-start | bytes 5308424 | tf_op jit(solution)/shard_map/ppermute | solution.py:42
  113.8 77.7 %collective-permute-start.18 = (bf16[576,1536]{1,0:T(8,128)(2,1)S(1)}, bf16[576,1536]{1,0:T(8,128)(2,1)}, u32[]{:S(2)}, u32[]{:S(2)}) collective-permute-start(bf16[576,1536]{1,0:T(8,128)(2,1)S(1)} %bitcast.242), channel_id=1, source_target_pairs={{0,3},{1,2},{2,1},{3,0},{4,7},{5,6},{6,5},{7,4},{8,11},{9,10},{10,... | collective-permute-start | bytes 5308424 | tf_op jit(solution)/shard_map/ppermute | solution.py:42
  210.9 112.6 %collective-permute-start.23 = (bf16[960,1536]{1,0:T(8,128)(2,1)}, bf16[960,1536]{1,0:T(8,128)(2,1)}, u32[]{:S(2)}, u32[]{:S(2)}) collective-permute-start(bf16[960,1536]{1,0:T(8,128)(2,1)} %pad_maximum_fusion.8.refs_2_), channel_id=1, source_target_pairs={{0,1},{1,0},{2,3},{3,2},{4,5},{5,4},{6,7},{7,6},{8,9},{9,8},{10,11... | collective-permute-start | bytes 8847368 | tf_op jit(solution)/shard_map/ppermute | solution.py:42
  211.6 124.6 %collective-permute-start.24 = (bf16[960,1536]{1,0:T(8,128)(2,1)}, bf16[960,1536]{1,0:T(8,128)(2,1)}, u32[]{:S(2)}, u32[]{:S(2)}) collective-permute-start(bf16[960,1536]{1,0:T(8,128)(2,1)} %pad_maximum_fusion.8.refs_2_), channel_id=1, source_target_pairs={{0,2},{1,3},{2,0},{3,1},{4,6},{5,7},{6,4},{7,5},{8,10},{9,11},{10,... | collective-permute-start | bytes 8847368 | tf_op jit(solution)/shard_map/ppermute | solution.py:42
  213.0 124.2 %collective-permute-start.25 = (bf16[960,1536]{1,0:T(8,128)(2,1)}, bf16[960,1536]{1,0:T(8,128)(2,1)}, u32[]{:S(2)}, u32[]{:S(2)}) collective-permute-start(bf16[960,1536]{1,0:T(8,128)(2,1)} %pad_maximum_fusion.8.refs_2_), channel_id=1, source_target_pairs={{0,3},{1,2},{2,1},{3,0},{4,7},{5,6},{6,5},{7,4},{8,11},{9,10},{10,... | collective-permute-start | bytes 8847368 | tf_op jit(solution)/shard_map/ppermute | solution.py:42
  561.0 37.2 %collective-permute-start.36 = (bf16[4,3,192,1536]{3,2,1,0:T(8,128)(2,1)}, bf16[4,3,192,1536]{3,2,1,0:T(8,128)(2,1)}, u32[]{:S(2)}, u32[]{:S(2)}) collective-permute-start(bf16[4,3,192,1536]{3,2,1,0:T(8,128)(2,1)} %get-tuple-element.98), channel_id=1, source_target_pairs={{0,16},{16,0},{1,17},{17,1},{2,18},{18,2},{3,19},{19,3},{4,20},{20... | collective-permute-start | bytes 21233672 | tf_op jit(solution)/shard_map/ppermute | solution.py:27
  609.8 119.2 %collective-permute-start.40 = (bf16[1040,1536]{1,0:T(8,128)(2,1)}, bf16[1040,1536]{1,0:T(8,128)(2,1)}, u32[]{:S(2)}, u32[]{:S(2)}) collective-permute-start(bf16[1040,1536]{1,0:T(8,128)(2,1)} %pad_maximum_fusion.7), channel_id=1, source_target_pairs={{0,3},{1,2},{2,1},{3,0},{4,7},{5,6},{6,5},{7,4},{8,11},{9,10},{10,... | collective-permute-start | bytes 9584648 | tf_op jit(solution)/shard_map/ppermute | solution.py:42
  611.2 139.5 %collective-permute-start.39 = (bf16[1040,1536]{1,0:T(8,128)(2,1)}, bf16[1040,1536]{1,0:T(8,128)(2,1)}, u32[]{:S(2)}, u32[]{:S(2)}) collective-permute-start(bf16[1040,1536]{1,0:T(8,128)(2,1)} %pad_maximum_fusion.6), channel_id=1, source_target_pairs={{0,2},{1,3},{2,0},{3,1},{4,6},{5,7},{6,4},{7,5},{8,10},{9,11},{10,... | collective-permute-start | bytes 9584648 | tf_op jit(solution)/shard_map/ppermute | solution.py:42
  612.0 138.6 %collective-permute-start.38 = (bf16[1040,1536]{1,0:T(8,128)(2,1)}, bf16[1040,1536]{1,0:T(8,128)(2,1)}, u32[]{:S(2)}, u32[]{:S(2)}) collective-permute-start(bf16[1040,1536]{1,0:T(8,128)(2,1)} %pad_maximum_fusion.5), channel_id=1, source_target_pairs={{0,1},{1,0},{2,3},{3,2},{4,5},{5,4},{6,7},{7,6},{8,9},{9,8},{10,11... | collective-permute-start | bytes 9584648 | tf_op jit(solution)/shard_map/ppermute | solution.py:42
  728.9 54.7 %collective-permute-start.42 = (bf16[4,3,192,1536]{3,2,1,0:T(8,128)(2,1)}, bf16[4,3,192,1536]{3,2,1,0:T(8,128)(2,1)}, u32[]{:S(2)}, u32[]{:S(2)}) collective-permute-start(bf16[4,3,192,1536]{3,2,1,0:T(8,128)(2,1)} %get-tuple-element.121), channel_id=1, source_target_pairs={{0,16},{16,0},{1,17},{17,1},{2,18},{18,2},{3,19},{19,3},{4,20},{20... | collective-permute-start | bytes 21233672 | tf_op jit(solution)/shard_map/ppermute | solution.py:27
  794.1 150.6 %all-reduce.3.cloned.1.call-start = ((), (), s32[]{:S(2)}) async-start(), calls=%async_computation.3 | async-start | bytes 2850816 | tf_op jit(solution)/shard_map/psum | solution.py:728
  800.1 30.9 %collective-permute-start.47 = (bf16[1,192,1536]{2,1,0:T(8,128)(2,1)S(1)}, bf16[1,192,1536]{2,1,0:T(8,128)(2,1)S(1)}, u32[]{:S(2)}, u32[]{:S(2)}) collective-permute-start(bf16[1,192,1536]{2,1,0:T(8,128)(2,1)S(1)} %slice.381), channel_id=1, source_target_pairs={{0,2},{1,3},{2,0},{3,1},{4,6},{5,7},{6,4},{7,5},{8,10},{9,11},{10,... | collective-permute-start | bytes 1769480 | tf_op jit(solution)/shard_map/ppermute | solution.py:42
  855.6 150.6 %all-reduce.5.cloned.1.call-start = ((), (), s32[]{:S(2)}) async-start(), calls=%async_computation.4 | async-start | bytes 2850816 | tf_op jit(solution)/shard_map/psum | solution.py:734
  874.7 35.4 %collective-permute-start.53 = (bf16[464,1536]{1,0:T(8,128)(2,1)}, bf16[464,1536]{1,0:T(8,128)(2,1)}, u32[]{:S(2)}, u32[]{:S(2)}) collective-permute-start(bf16[464,1536]{1,0:T(8,128)(2,1)} %get-tuple-element.186), channel_id=1, source_target_pairs={{0,3},{1,2},{2,1},{3,0},{4,7},{5,6},{6,5},{7,4},{8,11},{9,10},{10,... | collective-permute-start | bytes 4276232 | tf_op jit(solution)/shard_map/ppermute | solution.py:42
  876.2 63.4 %collective-permute-start.52 = (bf16[464,1536]{1,0:T(8,128)(2,1)}, bf16[464,1536]{1,0:T(8,128)(2,1)}, u32[]{:S(2)}, u32[]{:S(2)}) collective-permute-start(bf16[464,1536]{1,0:T(8,128)(2,1)} %get-tuple-element.187), channel_id=1, source_target_pairs={{0,2},{1,3},{2,0},{3,1},{4,6},{5,7},{6,4},{7,5},{8,10},{9,11},{10,... | collective-permute-start | bytes 4276232 | tf_op jit(solution)/shard_map/ppermute | solution.py:42
  877.0 62.6 %collective-permute-start.51 = (bf16[464,1536]{1,0:T(8,128)(2,1)}, bf16[464,1536]{1,0:T(8,128)(2,1)}, u32[]{:S(2)}, u32[]{:S(2)}) collective-permute-start(bf16[464,1536]{1,0:T(8,128)(2,1)} %get-tuple-element.185), channel_id=1, source_target_pairs={{0,1},{1,0},{2,3},{3,2},{4,5},{5,4},{6,7},{7,6},{8,9},{9,8},{10,11... | collective-permute-start | bytes 4276232 | tf_op jit(solution)/shard_map/ppermute | solution.py:42
  880.0 64.8 %collective-permute-start.49 = (bf16[256,1536]{1,0:T(8,128)(2,1)}, bf16[256,1536]{1,0:T(8,128)(2,1)}, u32[]{:S(2)}, u32[]{:S(2)}) collective-permute-start(bf16[256,1536]{1,0:T(8,128)(2,1)} %get-tuple-element.165), channel_id=1, source_target_pairs={{0,16},{16,0},{1,17},{17,1},{2,18},{18,2},{3,19},{19,3},{4,20},{20... | collective-permute-start | bytes 2359304 | tf_op jit(solution)/shard_map/ppermute | solution.py:27
  882.8 68.9 %collective-permute-start.41 = (bf16[256,1536]{1,0:T(8,128)(2,1)}, bf16[256,1536]{1,0:T(8,128)(2,1)}, u32[]{:S(2)}, u32[]{:S(2)}) collective-permute-start(bf16[256,1536]{1,0:T(8,128)(2,1)} %get-tuple-element.167), channel_id=1, source_target_pairs={{0,16},{16,0},{1,17},{17,1},{2,18},{18,2},{3,19},{19,3},{4,20},{20... | collective-permute-start | bytes 2359304 | tf_op jit(solution)/shard_map/ppermute | solution.py:27
  948.1 60.9 %collective-permute-start.60 = (bf16[2,192,1536]{2,1,0:T(8,128)(2,1)}, bf16[2,192,1536]{2,1,0:T(8,128)(2,1)}, u32[]{:S(2)}, u32[]{:S(2)}) collective-permute-start(bf16[2,192,1536]{2,1,0:T(8,128)(2,1)} %slice.413), channel_id=1, source_target_pairs={{0,3},{1,2},{2,1},{3,0},{4,7},{5,6},{6,5},{7,4},{8,11},{9,10},{10,... | collective-permute-start | bytes 3538952 | tf_op jit(solution)/shard_map/ppermute | solution.py:42
  949.7 59.4 %collective-permute-start.59 = (bf16[2,192,1536]{2,1,0:T(8,128)(2,1)}, bf16[2,192,1536]{2,1,0:T(8,128)(2,1)}, u32[]{:S(2)}, u32[]{:S(2)}) collective-permute-start(bf16[2,192,1536]{2,1,0:T(8,128)(2,1)} %slice.412), channel_id=1, source_target_pairs={{0,2},{1,3},{2,0},{3,1},{4,6},{5,7},{6,4},{7,5},{8,10},{9,11},{10,... | collective-permute-start | bytes 3538952 | tf_op jit(solution)/shard_map/ppermute | solution.py:42
  950.5 58.6 %collective-permute-start.58 = (bf16[2,192,1536]{2,1,0:T(8,128)(2,1)}, bf16[2,192,1536]{2,1,0:T(8,128)(2,1)}, u32[]{:S(2)}, u32[]{:S(2)}) collective-permute-start(bf16[2,192,1536]{2,1,0:T(8,128)(2,1)} %slice.411), channel_id=1, source_target_pairs={{0,1},{1,0},{2,3},{3,2},{4,5},{5,4},{6,7},{7,6},{8,9},{9,8},{10,11... | collective-permute-start | bytes 3538952 | tf_op jit(solution)/shard_map/ppermute | solution.py:42
  (160 other events, 2651.7 us)
Sparse Core Ops, SparseCore 0:
  15.8 65.8 all-gather.1
  794.2 57.5 reduce-scatter.1
  855.7 62.9 all-reduce.2
  944.9 61.2 all-reduce.4

commit v4 on v3

--- a/solution.py
+++ b/solution.py
@@ -604,7 +604,7 @@
     return (y,) + mix_backward(grad, k, p, n)
 
 
-def attention_backward(grad, grad_mixer, k, p, c, first, early):
+def attention_backward(grad, grad_mixer, k, p, c, first):
     rows, width = grad.shape
     cosine, sine = c["rope"]
     wide, length = (rows, HEADS * HEAD), c["bias"].shape[1]
@@ -615,10 +615,8 @@
         grad, grad_mixer, k["hidden"], p["gm"].reshape(1, -1), k["queries"], k["kv"], k["logs"], c["bias"],
         k["flat"], cosine, sine, p["mine"], p["other"],
     )
-    gkv, early = lax.optimization_barrier((gkv.reshape(4, rows, -1), early))
-    part = summed([v[:1] for v in early]) if early else ()
+    gkv = gkv.reshape(4, rows, -1)
     gkv = gkv[0].astype(F32) + sum(hop(gkv[r], r).astype(F32) for r in (1, 2, 3))
-    gkv, part = lax.optimization_barrier((gkv, part))
     gkv = gkv.reshape(rows, 2 * GROUPS, HEAD)
     cosine, sine = cosine[:, None], sine[:, None]
     gkv = jnp.concatenate([rotate(gkv[:, :GROUPS], cosine, -sine), gkv[:, GROUPS:]], 1)
@@ -639,7 +637,7 @@
 
     q, o = rows_of(gw_q, 0, g_ga), rows_of(gw_out, 1, g_gm[0])
     parts = over_sections(jnp.where(first, q, o), jnp.where(first, o, q))
-    return grad_hidden + more, parts, part, early
+    return grad_hidden + more, parts
 
 
 def on_device(
@@ -716,7 +714,7 @@
     hidden1, mixer, k1 = attention_forward(y0, *keys_and_values(y0, small[1], c, other), small[1], c)
     y, gm, keep, give = mix_both(mixer, low(grad1), small[1], n, grads)
     parts = over_sections(keep, give)
-    gx1, more, _, _ = attention_backward(grad1, gm, k1, small[1], c, first, [])
+    gx1, more = attention_backward(grad1, gm, k1, small[1], c, first)
     gb = low(gx1)
     rows_f = 3 * hidden
     both_parts = [jnp.concatenate([a.reshape(rows_f, width), b]) for a, b in zip(parts, more)]
@@ -727,10 +725,9 @@
     y1 = low(hidden1 + (scatter_along(y).astype(F32) if n <= SMALL else y))
     f1, s1 = got[:rows_f].reshape(3, hidden, width), lax.psum(got[rows_f:], D)
     parts = over_sections(keep, give)
-    gx0, more, part_a, parts = attention_backward(gb.astype(F32), gm, k0, small[0], c, first, parts)
+    gx0, more = attention_backward(gb.astype(F32), gm, k0, small[0], c, first)
     s0 = summed(more)
-    part_b = summed(after([v[1:] for v in parts], s0))
-    f0 = jnp.concatenate([part_a, part_b])
+    f0 = summed(after(parts, s0))
     s0 = lax.psum(after(s0, s1, y1), D)
 
     outs = jnp.stack(swap(first, y0, y1))

time: 1060 us -> 1050 us (level)
    unnamed x258 -> x238, local copies, waits for them, and re-layouts: 23 us -> 28.4 us
    ppermute x36 -> x33, waiting for transfers between devices: 238 us -> 243 us  [hop(): lax.ppermute(values, T, [(i, i ^ bit) for i in range(lax.axis_size(T))])]
    convert_element_type x19 -> x17, other arithmetic: 43.7 us -> 39.7 us  [low(): return lax.reduce_precision(values.astype(F32), 8, 7).astype(BF)]
    ppermute x36 -> x33, starting transfers between devices: 42.8 us -> 39.2 us  [hop(): lax.ppermute(values, T, [(i, i ^ bit) for i in range(lax.axis_size(T))])]
  transfers between devices with their start and end apart: 66 -> 63, of which waited for: 25 -> 26; matrix products, arithmetic and copies ran while one was open for 17% -> 17% of each run, Pallas kernels for 25% -> 26%
where the time goes in v4:
time: 1050 us; the launch traced here: 1040 us
  Pallas kernels  443 us (42%)
  waiting for transfers between devices  313 us (30%)
  other arithmetic  131 us (12%)
  local copies, waits for them, and re-layouts  63.4 us (6%)
  starting transfers between devices  50.5 us (5%)
  matrix products  24 us (2%)
  between operations  16.1 us (2%)
    pallas_call x3, Pallas kernels, experts(): pl.pallas_call(functools.partial(expert_kernel, n, forward, backward), ou...  352 us
    ppermute x33, waiting for transfers between devices, hop(): lax.ppermute(values, T, [(i, i ^ bit) for i in range(lax.axis_size(T))])  243 us
    pallas_call x4, Pallas kernels, local_call(): pl.pallas_call(body, out_shape=[jax.ShapeDtypeStruct(*o) for o in out], i...  90.5 us
    psum x1, waiting for transfers between devices, on_device(): s0 = lax.psum(after(s0, s1, y1), D)  53.2 us
    convert_element_type x17, other arithmetic, low(): return lax.reduce_precision(values.astype(F32), 8, 7).astype(BF)  39.7 us
    ppermute x33, starting transfers between devices, hop(): lax.ppermute(values, T, [(i, i ^ bit) for i in range(lax.axis_size(T))])  39.2 us
    unnamed x238, local copies, waits for them, and re-layouts  28.4 us
    dot_general x10, matrix products, dot(): lax.dot_general(a, b, ((ca, cb), ((), ())), preferred_element_type=F32)  24 us
  transfers between devices with their start and end apart: 63, of which 26 were waited for; matrix products, arithmetic and copies ran while one was open for 17% of the time, Pallas kernels for 26%

profile of v4, /device:TPU:0, one launch (start us, length us, event | category | flops | bytes accessed | tf_op | source)
XLA Modules:
  0.0 1040.5 jit_solution(8521080487805592241)
XLA Ops:
  24.7 24.9 %collective-permute-done.9 = bf16[384,1536]{1,0:T(8,128)(2,1)S(1)} collective-permute-done((bf16[384,1536]{1,0:T(8,128)(2,1)}, bf16[384,1536]{1,0:T(8,128)(2,1)S(1)}, u32[]{:S(2)}, u32[]{:S(2)}) %collective-permute-start.9) | collective-permute-done | bytes 1179680 | tf_op jit(solution)/shard_map/ppermute | solution.py:42
  49.6 25.1 %collective-permute-done.8 = bf16[384,1536]{1,0:T(8,128)(2,1)} collective-permute-done((bf16[384,1536]{1,0:T(8,128)(2,1)}, bf16[384,1536]{1,0:T(8,128)(2,1)}, u32[]{:S(2)}, u32[]{:S(2)}) %collective-permute-start.8) | collective-permute-done | bytes 1179680 | tf_op jit(solution)/shard_map/ppermute | solution.py:42
  75.0 4.9 pad_maximum_fusion.mine
  104.3 5.3 collective-permute-done.3
  117.6 20.8 %shard_map.221 = (f32[256,1536]{1,0:T(8,128)}, bf16[256,1536]{1,0:T(8,128)(2,1)S(1)}, bf16[256,1536]{1,0:T(8,128)(2,1)S(1)}, bf16[256,1536]{1,0:T(8,128)(2,1)S(1)}, f32[256,1536]{1,0:T(8,128)}) custom-call(bf16[256,1536]{1,0:T(8,128)(2,1)S(1)} %get-tuple-element.164.x, bf16[256,1536]{1,0:T(8,128)(2,1)S(1)} %fusion.33.normed, ...), custom_call_target="tpu_custom_call" | custom-call | flops 99999997952 | bytes 20000000 | tf_op jit(solution)/shard_map/pallas_call | solution.py:517
  141.0 12.4 %collective-permute-done.16.refs_3_ = bf16[576,1536]{1,0:T(8,128)(2,1)} collective-permute-done((bf16[576,1536]{1,0:T(8,128)(2,1)S(1)}, bf16[576,1536]{1,0:T(8,128)(2,1)}, u32[]{:S(2)}, u32[]{:S(2)}) %collective-permute-start.16) | collective-permute-done | bytes 1769504 | tf_op jit(solution)/shard_map/ppermute | solution.py:42
  153.5 38.2 %collective-permute-done.17.refs_4_ = bf16[576,1536]{1,0:T(8,128)(2,1)} collective-permute-done((bf16[576,1536]{1,0:T(8,128)(2,1)S(1)}, bf16[576,1536]{1,0:T(8,128)(2,1)}, u32[]{:S(2)}, u32[]{:S(2)}) %collective-permute-start.17) | collective-permute-done | bytes 1769504 | tf_op jit(solution)/shard_map/ppermute | solution.py:42
  215.0 107.3 %shard_map.222 = (f32[256,1536]{1,0:T(8,128)S(1)}, bf16[4,256,1536]{2,1,0:T(8,128)(2,1)}, bf16[4,256,1536]{2,1,0:T(8,128)(2,1)}, bf16[4,256,1536]{2,1,0:T(8,128)(2,1)}, bf16[4,256,1536]{2,1,0:T(8,128)(2,1)}) custom-call(bf16[256,1536]{1,0:T(8,128)(2,1)S(1)} %copy-done.31, f32[2,4,256,128]{3,2,1,0:T(8,128)S(1)} %broadcast_in_dim.97.refs_1_, ...), custom_call_target="tpu_custom_call" | custom-call | flops 399999991808 | bytes 100000000 | tf_op jit(solution)/shard_map/pallas_call | solution.py:389
  323.4 13.9 %collective-permute-done.24.refs_4_ = bf16[960,1536]{1,0:T(8,128)(2,1)} collective-permute-done((bf16[960,1536]{1,0:T(8,128)(2,1)}, bf16[960,1536]{1,0:T(8,128)(2,1)}, u32[]{:S(2)}, u32[]{:S(2)}) %collective-permute-start.24) | collective-permute-done | bytes 2949152 | tf_op jit(solution)/shard_map/ppermute | solution.py:42
  370.9 20.7 %shard_map.223 = (f32[256,1536]{1,0:T(8,128)}, bf16[256,1536]{1,0:T(8,128)(2,1)S(1)}, bf16[256,1536]{1,0:T(8,128)(2,1)S(1)}, bf16[256,1536]{1,0:T(8,128)(2,1)S(1)}, f32[256,1536]{1,0:T(8,128)}) custom-call(bf16[256,1536]{1,0:T(8,128)(2,1)S(1)} %get-tuple-element.160.x, bf16[256,1536]{1,0:T(8,128)(2,1)S(1)} %fusion.43.normed, ...), custom_call_target="tpu_custom_call" | custom-call | flops 99999997952 | bytes 20000000 | tf_op jit(solution)/shard_map/pallas_call | solution.py:517
  392.0 131.1 %shard_map.224 = (f32[256,1536]{1,0:T(8,128)S(1)}, bf16[4,256,1536]{2,1,0:T(8,128)(2,1)}, bf16[4,3,192,1536]{3,2,1,0:T(8,128)(2,1)}, bf16[4,3,192,1536]{3,2,1,0:T(8,128)(2,1)}) custom-call(bf16[256,1536]{1,0:T(8,128)(2,1)S(1)} %get-tuple-element.82.refs_0_, f32[2,4,256,128]{3,2,1,0:T(8,128)S(1)} %broadcast_in_dim.99.refs_1_, ...), custom_call_target="tpu_custom_call" | custom-call | flops 399999991808 | bytes 100000000 | tf_op jit(solution)/shard_map/pallas_call | solution.py:389
  524.3 24.4 %shard_map.225 = (f32[256,1536]{1,0:T(8,128)}, bf16[256,1536]{1,0:T(8,128)(2,1)S(1)}, bf16[1024,512]{1,0:T(8,128)(2,1)S(1)}, bf16[1536,1536]{1,0:T(8,128)(2,1)}, f32[1,1536]{1,0:T(1,128)S(1)}) custom-call(f32[256,1536]{1,0:T(8,128)} %get-tuple-element.162.grad, f32[256,1536]{1,0:T(8,128)} %copy-done.25, f32[256,1536]{1,0:T(8,128)} %get-tuple-element.81.hidden, ...), custom_call_target="tpu_custom_call" | custom-call | flops 99999997952 | bytes 20000000 | tf_op jit(solution)/shard_map/pallas_call | solution.py:517
  569.9 4.3 broadcast_select_fusion.2
  576.6 7.3 collective-permute-done.37
  587.4 4.2 reduce-precision_convert_fusion.9
  602.7 113.7 %shard_map.226 = (f32[256,1536]{1,0:T(8,128)S(1)}, bf16[4,3,192,1536]{3,2,1,0:T(8,128)(2,1)}, bf16[4,3,192,1536]{3,2,1,0:T(8,128)(2,1)}) custom-call(bf16[256,1536]{1,0:T(8,128)(2,1)S(1)} %fusion.49.refs_0_, f32[2,4,256,128]{3,2,1,0:T(8,128)S(1)} %copy-done.13, bf16[576,1536]{1,0:T(8,128)(2,1)S(1)} %bitcast.223, ...), custom_call_target="tpu_custom_call" | custom-call | flops 399999991808 | bytes 100000000 | tf_op jit(solution)/shard_map/pallas_call | solution.py:389
  717.9 22.2 %collective-permute-done.39 = bf16[1040,1536]{1,0:T(8,128)(2,1)} collective-permute-done((bf16[1040,1536]{1,0:T(8,128)(2,1)}, bf16[1040,1536]{1,0:T(8,128)(2,1)}, u32[]{:S(2)}, u32[]{:S(2)}) %collective-permute-start.39) | collective-permute-done | bytes 3194912 | tf_op jit(solution)/shard_map/ppermute | solution.py:42
  740.1 8.0 reduce-precision_convert_fusion.2
  754.1 24.6 %shard_map.227 = (f32[256,1536]{1,0:T(8,128)}, bf16[256,1536]{1,0:T(8,128)(2,1)S(1)}, bf16[1024,512]{1,0:T(8,128)(2,1)S(1)}, bf16[1536,1536]{1,0:T(8,128)(2,1)}, f32[1,1536]{1,0:T(1,128)S(1)}) custom-call(f32[256,1536]{1,0:T(8,128)} %convert_element_type.529.grad, f32[256,1536]{1,0:T(8,128)} %copy-done.24, f32[256,1536]{1,0:T(8,128)} %get-tuple-element.67.hidden, ...), custom_call_target="tpu_custom_call" | custom-call | flops 99999997952 | bytes 20000000 | tf_op jit(solution)/shard_map/pallas_call | solution.py:517
  788.9 4.6 collective-permute-done.43
  797.5 4.5 fusion.40
  804.8 4.4 broadcast_select_fusion
  817.3 7.0 broadcast_select_fusion.1
  824.3 5.9 fusion.57
  833.8 6.1 fusion.31
  842.5 23.1 %collective-permute-done.49 = bf16[464,1536]{1,0:T(8,128)(2,1)} collective-permute-done((bf16[464,1536]{1,0:T(8,128)(2,1)}, bf16[464,1536]{1,0:T(8,128)(2,1)}, u32[]{:S(2)}, u32[]{:S(2)}) %collective-permute-start.49) | collective-permute-done | bytes 1425440 | tf_op jit(solution)/shard_map/ppermute | solution.py:42
  865.6 29.6 %collective-permute-done.48 = bf16[464,1536]{1,0:T(8,128)(2,1)} collective-permute-done((bf16[464,1536]{1,0:T(8,128)(2,1)}, bf16[464,1536]{1,0:T(8,128)(2,1)}, u32[]{:S(2)}, u32[]{:S(2)}) %collective-permute-start.48) | collective-permute-done | bytes 1425440 | tf_op jit(solution)/shard_map/ppermute | solution.py:42
  895.2 5.1 fusion.9
  908.8 53.2 %all-reduce.5.cloned.1.call-done = bf16[464,1536]{1,0:T(8,128)(2,1)} async-done(((bf16[464,1536]{1,0:T(8,128)(2,1)}), bf16[464,1536]{1,0:T(8,128)(2,1)}) %all-reduce.5.cloned.1.call-update) | async-done | bytes 1425424 | tf_op jit(solution)/shard_map/psum | solution.py:731
  966.2 17.4 %collective-permute-done.56 = bf16[3,192,1536]{2,1,0:T(8,128)(2,1)} collective-permute-done((bf16[3,192,1536]{2,1,0:T(8,128)(2,1)}, bf16[3,192,1536]{2,1,0:T(8,128)(2,1)}, u32[]{:S(2)}, u32[]{:S(2)}) %collective-permute-start.56) | collective-permute-done | bytes 1769504 | tf_op jit(solution)/shard_map/ppermute | solution.py:42
  983.6 5.7 broadcast_select_fusion.4
  1006.0 10.1 collective-permute-done.52
  (498 shorter events, 234.3 us)
Async XLA Ops:
  7.2 104.7 %all-gather.2.cloned.1.call-start = ((), (), s32[]{:S(2)}) async-start(), calls=%async_computation.1 | async-start | bytes 3932160 | tf_op jit(solution)/shard_map/all_gather | solution.py:552
  10.9 74.9 %collective-permute-start = (f32[1,1536]{1,0:T(1,128)S(1)}, f32[1,1536]{1,0:T(1,128)S(1)}, u32[]{:S(2)}, u32[]{:S(2)}) collective-permute-start(f32[1,1536]{1,0:T(1,128)S(1)} %copy-done.101), channel_id=1, source_target_pairs={{0,16},{16,0},{1,17},{17,1},{2,18},{18,2},{3,19},{19,3},{4,20},{20... | collective-permute-start | bytes 18440 | tf_op jit(solution)/shard_map/ppermute | solution.py:27
  12.2 74.8 %collective-permute-start.1 = (bf16[1536,512]{1,0:T(8,128)(2,1)}, bf16[1536,512]{1,0:T(8,128)(2,1)}, u32[]{:S(2)}, u32[]{:S(2)}) collective-permute-start(bf16[1536,512]{1,0:T(8,128)(2,1)} %pad_maximum_fusion.10), channel_id=1, source_target_pairs={{0,16},{16,0},{1,17},{17,1},{2,18},{18,2},{3,19},{19,3},{4,20},{20... | collective-permute-start | bytes 4718600 | tf_op jit(solution)/shard_map/ppermute | solution.py:27
  15.7 824.2 %reduce-scatter.2.cloned.1.call-start = ((), (), s32[]{:S(2)}) async-start(), calls=%async_computation.2 | async-start | bytes 3932160 | tf_op jit(solution)/shard_map/reduce_scatter | solution.py:556
  19.0 30.5 %collective-permute-start.9 = (bf16[384,1536]{1,0:T(8,128)(2,1)}, bf16[384,1536]{1,0:T(8,128)(2,1)S(1)}, u32[]{:S(2)}, u32[]{:S(2)}) collective-permute-start(bf16[384,1536]{1,0:T(8,128)(2,1)} %get-tuple-element.192), channel_id=1, source_target_pairs={{0,3},{1,2},{2,1},{3,0},{4,7},{5,6},{6,5},{7,4},{8,11},{9,10},{10,... | collective-permute-start | bytes 3538952 | tf_op jit(solution)/shard_map/ppermute | solution.py:42
  22.5 52.2 %collective-permute-start.8 = (bf16[384,1536]{1,0:T(8,128)(2,1)}, bf16[384,1536]{1,0:T(8,128)(2,1)}, u32[]{:S(2)}, u32[]{:S(2)}) collective-permute-start(bf16[384,1536]{1,0:T(8,128)(2,1)} %get-tuple-element.192), channel_id=1, source_target_pairs={{0,2},{1,3},{2,0},{3,1},{4,6},{5,7},{6,4},{7,5},{8,10},{9,11},{10,... | collective-permute-start | bytes 3538952 | tf_op jit(solution)/shard_map/ppermute | solution.py:42
  23.0 52.0 %collective-permute-start.7 = (bf16[384,1536]{1,0:T(8,128)(2,1)}, bf16[384,1536]{1,0:T(8,128)(2,1)}, u32[]{:S(2)}, u32[]{:S(2)}) collective-permute-start(bf16[384,1536]{1,0:T(8,128)(2,1)} %get-tuple-element.192), channel_id=1, source_target_pairs={{0,1},{1,0},{2,3},{3,2},{4,5},{5,4},{6,7},{7,6},{8,9},{9,8},{10,11... | collective-permute-start | bytes 3538952 | tf_op jit(solution)/shard_map/ppermute | solution.py:42
  49.5 37.4 %collective-permute-start.5 = (f32[1,1536]{1,0:T(1,128)S(1)}, f32[1,1536]{1,0:T(1,128)S(1)}, u32[]{:S(2)}, u32[]{:S(2)}) collective-permute-start(f32[1,1536]{1,0:T(1,128)S(1)} %copy-done.102), channel_id=1, source_target_pairs={{0,16},{16,0},{1,17},{17,1},{2,18},{18,2},{3,19},{19,3},{4,20},{20... | collective-permute-start | bytes 18440 | tf_op jit(solution)/shard_map/ppermute | solution.py:27
  74.7 118.0 %collective-permute-start.11 = (f32[256,8]{0,1:T(8,128)S(1)}, f32[256,8]{0,1:T(8,128)S(1)}, u32[]{:S(2)}, u32[]{:S(2)}) collective-permute-start(f32[256,8]{0,1:T(8,128)S(1)} %fusion.85), channel_id=1, source_target_pairs={{0,16},{16,0},{1,17},{17,1},{2,18},{18,2},{3,19},{19,3},{4,20},{20... | collective-permute-start | bytes 24584 | tf_op jit(solution)/shard_map/ppermute | solution.py:27
  79.9 35.6 %collective-permute-start.10 = (bf16[1536,1536]{1,0:T(8,128)(2,1)}, bf16[1536,1536]{1,0:T(8,128)(2,1)}, u32[]{:S(2)}, u32[]{:S(2)}) collective-permute-start(bf16[1536,1536]{1,0:T(8,128)(2,1)} %pad_maximum_fusion.mine), channel_id=1, source_target_pairs={{0,16},{16,0},{1,17},{17,1},{2,18},{18,2},{3,19},{19,3},{4,20},{20... | collective-permute-start | bytes 14155784 | tf_op jit(solution)/shard_map/ppermute | solution.py:27
  111.9 41.6 %collective-permute-start.16 = (bf16[576,1536]{1,0:T(8,128)(2,1)S(1)}, bf16[576,1536]{1,0:T(8,128)(2,1)}, u32[]{:S(2)}, u32[]{:S(2)}) collective-permute-start(bf16[576,1536]{1,0:T(8,128)(2,1)S(1)} %bitcast.218), channel_id=1, source_target_pairs={{0,1},{1,0},{2,3},{3,2},{4,5},{5,4},{6,7},{7,6},{8,9},{9,8},{10,11... | collective-permute-start | bytes 5308424 | tf_op jit(solution)/shard_map/ppermute | solution.py:42
  113.3 78.3 %collective-permute-start.17 = (bf16[576,1536]{1,0:T(8,128)(2,1)S(1)}, bf16[576,1536]{1,0:T(8,128)(2,1)}, u32[]{:S(2)}, u32[]{:S(2)}) collective-permute-start(bf16[576,1536]{1,0:T(8,128)(2,1)S(1)} %bitcast.219), channel_id=1, source_target_pairs={{0,2},{1,3},{2,0},{3,1},{4,6},{5,7},{6,4},{7,5},{8,10},{9,11},{10,... | collective-permute-start | bytes 5308424 | tf_op jit(solution)/shard_map/ppermute | solution.py:42
  113.9 77.7 %collective-permute-start.18 = (bf16[576,1536]{1,0:T(8,128)(2,1)S(1)}, bf16[576,1536]{1,0:T(8,128)(2,1)}, u32[]{:S(2)}, u32[]{:S(2)}) collective-permute-start(bf16[576,1536]{1,0:T(8,128)(2,1)S(1)} %bitcast.220), channel_id=1, source_target_pairs={{0,3},{1,2},{2,1},{3,0},{4,7},{5,6},{6,5},{7,4},{8,11},{9,10},{10,... | collective-permute-start | bytes 5308424 | tf_op jit(solution)/shard_map/ppermute | solution.py:42
  211.1 112.3 %collective-permute-start.23 = (bf16[960,1536]{1,0:T(8,128)(2,1)}, bf16[960,1536]{1,0:T(8,128)(2,1)}, u32[]{:S(2)}, u32[]{:S(2)}) collective-permute-start(bf16[960,1536]{1,0:T(8,128)(2,1)} %pad_maximum_fusion.8.refs_2_), channel_id=1, source_target_pairs={{0,1},{1,0},{2,3},{3,2},{4,5},{5,4},{6,7},{7,6},{8,9},{9,8},{10,11... | collective-permute-start | bytes 8847368 | tf_op jit(solution)/shard_map/ppermute | solution.py:42
  211.7 125.7 %collective-permute-start.24 = (bf16[960,1536]{1,0:T(8,128)(2,1)}, bf16[960,1536]{1,0:T(8,128)(2,1)}, u32[]{:S(2)}, u32[]{:S(2)}) collective-permute-start(bf16[960,1536]{1,0:T(8,128)(2,1)} %pad_maximum_fusion.8.refs_2_), channel_id=1, source_target_pairs={{0,2},{1,3},{2,0},{3,1},{4,6},{5,7},{6,4},{7,5},{8,10},{9,11},{10,... | collective-permute-start | bytes 8847368 | tf_op jit(solution)/shard_map/ppermute | solution.py:42
  213.2 124.2 %collective-permute-start.25 = (bf16[960,1536]{1,0:T(8,128)(2,1)}, bf16[960,1536]{1,0:T(8,128)(2,1)}, u32[]{:S(2)}, u32[]{:S(2)}) collective-permute-start(bf16[960,1536]{1,0:T(8,128)(2,1)} %pad_maximum_fusion.8.refs_2_), channel_id=1, source_target_pairs={{0,3},{1,2},{2,1},{3,0},{4,7},{5,6},{6,5},{7,4},{8,11},{9,10},{10,... | collective-permute-start | bytes 8847368 | tf_op jit(solution)/shard_map/ppermute | solution.py:42
  552.3 35.0 %collective-permute-start.36 = (bf16[4,3,192,1536]{3,2,1,0:T(8,128)(2,1)}, bf16[4,3,192,1536]{3,2,1,0:T(8,128)(2,1)}, u32[]{:S(2)}, u32[]{:S(2)}) collective-permute-start(bf16[4,3,192,1536]{3,2,1,0:T(8,128)(2,1)} %get-tuple-element.91), channel_id=1, source_target_pairs={{0,16},{16,0},{1,17},{17,1},{2,18},{18,2},{3,19},{19,3},{4,20},{20... | collective-permute-start | bytes 21233672 | tf_op jit(solution)/shard_map/ppermute | solution.py:27
  599.2 118.7 %collective-permute-start.40 = (bf16[1040,1536]{1,0:T(8,128)(2,1)}, bf16[1040,1536]{1,0:T(8,128)(2,1)}, u32[]{:S(2)}, u32[]{:S(2)}) collective-permute-start(bf16[1040,1536]{1,0:T(8,128)(2,1)} %pad_maximum_fusion.7), channel_id=1, source_target_pairs={{0,3},{1,2},{2,1},{3,0},{4,7},{5,6},{6,5},{7,4},{8,11},{9,10},{10,... | collective-permute-start | bytes 9584648 | tf_op jit(solution)/shard_map/ppermute | solution.py:42
  600.7 139.4 %collective-permute-start.39 = (bf16[1040,1536]{1,0:T(8,128)(2,1)}, bf16[1040,1536]{1,0:T(8,128)(2,1)}, u32[]{:S(2)}, u32[]{:S(2)}) collective-permute-start(bf16[1040,1536]{1,0:T(8,128)(2,1)} %pad_maximum_fusion.6), channel_id=1, source_target_pairs={{0,2},{1,3},{2,0},{3,1},{4,6},{5,7},{6,4},{7,5},{8,10},{9,11},{10,... | collective-permute-start | bytes 9584648 | tf_op jit(solution)/shard_map/ppermute | solution.py:42
  601.4 138.7 %collective-permute-start.38 = (bf16[1040,1536]{1,0:T(8,128)(2,1)}, bf16[1040,1536]{1,0:T(8,128)(2,1)}, u32[]{:S(2)}, u32[]{:S(2)}) collective-permute-start(bf16[1040,1536]{1,0:T(8,128)(2,1)} %pad_maximum_fusion.5), channel_id=1, source_target_pairs={{0,1},{1,0},{2,3},{3,2},{4,5},{5,4},{6,7},{7,6},{8,9},{9,8},{10,11... | collective-permute-start | bytes 9584648 | tf_op jit(solution)/shard_map/ppermute | solution.py:42
  717.9 115.8 %collective-permute-start.54 = (bf16[4,3,192,1536]{3,2,1,0:T(8,128)(2,1)}, bf16[4,3,192,1536]{3,2,1,0:T(8,128)(2,1)}, u32[]{:S(2)}, u32[]{:S(2)}) collective-permute-start(bf16[4,3,192,1536]{3,2,1,0:T(8,128)(2,1)} %get-tuple-element.118), channel_id=1, source_target_pairs={{0,16},{16,0},{1,17},{17,1},{2,18},{18,2},{3,19},{19,3},{4,20},{20... | collective-permute-start | bytes 21233672 | tf_op jit(solution)/shard_map/ppermute | solution.py:27
  750.0 150.3 %all-reduce.3.cloned.1.call-start = ((), (), s32[]{:S(2)}) async-start(), calls=%async_computation.3 | async-start | bytes 2850816 | tf_op jit(solution)/shard_map/psum | solution.py:726
  813.4 148.6 %all-reduce.5.cloned.1.call-start = ((), (), s32[]{:S(2)}) async-start(), calls=%async_computation.4 | async-start | bytes 2850816 | tf_op jit(solution)/shard_map/psum | solution.py:731
  817.2 84.8 %collective-permute-start.45 = (bf16[256,1536]{1,0:T(8,128)(2,1)}, bf16[256,1536]{1,0:T(8,128)(2,1)}, u32[]{:S(2)}, u32[]{:S(2)}) collective-permute-start(bf16[256,1536]{1,0:T(8,128)(2,1)} %get-tuple-element.153), channel_id=1, source_target_pairs={{0,16},{16,0},{1,17},{17,1},{2,18},{18,2},{3,19},{19,3},{4,20},{20... | collective-permute-start | bytes 2359304 | tf_op jit(solution)/shard_map/ppermute | solution.py:27
  830.2 35.4 %collective-permute-start.49 = (bf16[464,1536]{1,0:T(8,128)(2,1)}, bf16[464,1536]{1,0:T(8,128)(2,1)}, u32[]{:S(2)}, u32[]{:S(2)}) collective-permute-start(bf16[464,1536]{1,0:T(8,128)(2,1)} %get-tuple-element.174), channel_id=1, source_target_pairs={{0,3},{1,2},{2,1},{3,0},{4,7},{5,6},{6,5},{7,4},{8,11},{9,10},{10,... | collective-permute-start | bytes 4276232 | tf_op jit(solution)/shard_map/ppermute | solution.py:42
  832.0 63.1 %collective-permute-start.48 = (bf16[464,1536]{1,0:T(8,128)(2,1)}, bf16[464,1536]{1,0:T(8,128)(2,1)}, u32[]{:S(2)}, u32[]{:S(2)}) collective-permute-start(bf16[464,1536]{1,0:T(8,128)(2,1)} %get-tuple-element.175), channel_id=1, source_target_pairs={{0,2},{1,3},{2,0},{3,1},{4,6},{5,7},{6,4},{7,5},{8,10},{9,11},{10,... | collective-permute-start | bytes 4276232 | tf_op jit(solution)/shard_map/ppermute | solution.py:42
  832.8 62.4 %collective-permute-start.47 = (bf16[464,1536]{1,0:T(8,128)(2,1)}, bf16[464,1536]{1,0:T(8,128)(2,1)}, u32[]{:S(2)}, u32[]{:S(2)}) collective-permute-start(bf16[464,1536]{1,0:T(8,128)(2,1)} %get-tuple-element.173), channel_id=1, source_target_pairs={{0,1},{1,0},{2,3},{3,2},{4,5},{5,4},{6,7},{7,6},{8,9},{9,8},{10,11... | collective-permute-start | bytes 4276232 | tf_op jit(solution)/shard_map/ppermute | solution.py:42
  903.3 60.3 %collective-permute-start.41 = (bf16[256,1536]{1,0:T(8,128)(2,1)}, bf16[256,1536]{1,0:T(8,128)(2,1)}, u32[]{:S(2)}, u32[]{:S(2)}) collective-permute-start(bf16[256,1536]{1,0:T(8,128)(2,1)} %get-tuple-element.155), channel_id=1, source_target_pairs={{0,16},{16,0},{1,17},{17,1},{2,18},{18,2},{3,19},{19,3},{4,20},{20... | collective-permute-start | bytes 2359304 | tf_op jit(solution)/shard_map/ppermute | solution.py:27
  903.4 62.8 %collective-permute-start.57 = (bf16[3,192,1536]{2,1,0:T(8,128)(2,1)}, bf16[3,192,1536]{2,1,0:T(8,128)(2,1)}, u32[]{:S(2)}, u32[]{:S(2)}) collective-permute-start(bf16[3,192,1536]{2,1,0:T(8,128)(2,1)} %get-tuple-element.122), channel_id=1, source_target_pairs={{0,3},{1,2},{2,1},{3,0},{4,7},{5,6},{6,5},{7,4},{8,11},{9,10},{10,... | collective-permute-start | bytes 5308424 | tf_op jit(solution)/shard_map/ppermute | solution.py:42
  905.2 78.3 %collective-permute-start.56 = (bf16[3,192,1536]{2,1,0:T(8,128)(2,1)}, bf16[3,192,1536]{2,1,0:T(8,128)(2,1)}, u32[]{:S(2)}, u32[]{:S(2)}) collective-permute-start(bf16[3,192,1536]{2,1,0:T(8,128)(2,1)} %get-tuple-element.121), channel_id=1, source_target_pairs={{0,2},{1,3},{2,0},{3,1},{4,6},{5,7},{6,4},{7,5},{8,10},{9,11},{10,... | collective-permute-start | bytes 5308424 | tf_op jit(solution)/shard_map/ppermute | solution.py:42
  906.0 77.6 %collective-permute-start.55 = (bf16[3,192,1536]{2,1,0:T(8,128)(2,1)}, bf16[3,192,1536]{2,1,0:T(8,128)(2,1)}, u32[]{:S(2)}, u32[]{:S(2)}) collective-permute-start(bf16[3,192,1536]{2,1,0:T(8,128)(2,1)} %get-tuple-element.120), channel_id=1, source_target_pairs={{0,1},{1,0},{2,3},{3,2},{4,5},{5,4},{6,7},{7,6},{8,9},{9,8},{10,11... | collective-permute-start | bytes 5308424 | tf_op jit(solution)/shard_map/ppermute | solution.py:42
  989.3 37.9 %collective-permute-start.58 = (bf16[3,192,1536]{2,1,0:T(8,128)(2,1)}, bf16[3,192,1536]{2,1,0:T(8,128)(2,1)}, u32[]{:S(2)}, u32[]{:S(2)}) collective-permute-start(bf16[3,192,1536]{2,1,0:T(8,128)(2,1)} %get-tuple-element.151), channel_id=1, source_target_pairs={{0,16},{16,0},{1,17},{17,1},{2,18},{18,2},{3,19},{19,3},{4,20},{20... | collective-permute-start | bytes 5308424 | tf_op jit(solution)/shard_map/ppermute | solution.py:27
  (147 other events, 2392.2 us)
Sparse Core Ops, SparseCore 0:
  15.8 65.8 all-gather.1
  750.2 57.4 reduce-scatter.1
  813.5 61.4 all-reduce.2
  900.5 61.4 all-reduce.4

commit v5 on v4

--- a/solution.py
+++ b/solution.py
@@ -696,7 +696,7 @@
 
     ahead = keys_and_values(x0, small[0], c)
     got = pieces_of(attn[0])
-    late = after(ffn[0], got, ahead, grads)
+    late = after(ffn[0], got, ahead, grads, shares)
     mine = jnp.concatenate(got)
     small[0].update(mine=mine, other=partner(mine))
     hidden0, mixer, k0 = attention_forward(x0, *ahead, small[0], c)

time: 1050 us -> 1040 us (level)
    unnamed x238 -> x254, local copies, waits for them, and re-layouts: 28.4 us -> 30.1 us
  transfers between devices with their start and end apart: 63 -> 63, of which waited for: 26 -> 28; matrix products, arithmetic and copies ran while one was open for 17% -> 17% of each run, Pallas kernels for 26% -> 26%
where the time goes in v5:
time: 1040 us; the launch traced here: 1030 us
  Pallas kernels  448 us (43%)
  waiting for transfers between devices  304 us (29%)
  other arithmetic  127 us (12%)
  local copies, waits for them, and re-layouts  64.3 us (6%)
  starting transfers between devices  49.6 us (5%)
  matrix products  22.4 us (2%)
  between operations  16.2 us (2%)
    pallas_call x3, Pallas kernels, experts(): pl.pallas_call(functools.partial(expert_kernel, n, forward, backward), ou...  358 us
    ppermute x33, waiting for transfers between devices, hop(): lax.ppermute(values, T, [(i, i ^ bit) for i in range(lax.axis_size(T))])  235 us
    pallas_call x4, Pallas kernels, local_call(): pl.pallas_call(body, out_shape=[jax.ShapeDtypeStruct(*o) for o in out], i...  90.5 us
    psum x1, waiting for transfers between devices, on_device(): s0 = lax.psum(after(s0, s1, y1), D)  53.2 us
    convert_element_type x17, other arithmetic, low(): return lax.reduce_precision(values.astype(F32), 8, 7).astype(BF)  39.7 us
    ppermute x33, starting transfers between devices, hop(): lax.ppermute(values, T, [(i, i ^ bit) for i in range(lax.axis_size(T))])  38.9 us
    unnamed x254, local copies, waits for them, and re-layouts  30.1 us
    dot_general x10, matrix products, dot(): lax.dot_general(a, b, ((ca, cb), ((), ())), preferred_element_type=F32)  22.4 us
  transfers between devices with their start and end apart: 63, of which 28 were waited for; matrix products, arithmetic and copies ran while one was open for 17% of the time, Pallas kernels for 26%

profile of v5, /device:TPU:0, one launch (start us, length us, event | category | flops | bytes accessed | tf_op | source)
XLA Modules:
  0.0 1031.4 jit_solution(8999457277095521957)
XLA Ops:
  25.1 24.2 %collective-permute-done.9 = bf16[384,1536]{1,0:T(8,128)(2,1)S(1)} collective-permute-done((bf16[384,1536]{1,0:T(8,128)(2,1)S(1)}, bf16[384,1536]{1,0:T(8,128)(2,1)S(1)}, u32[]{:S(2)}, u32[]{:S(2)}) %collective-permute-start.9) | collective-permute-done | bytes 1179680 | tf_op jit(solution)/shard_map/ppermute | solution.py:42
  49.3 24.9 %collective-permute-done.8 = bf16[384,1536]{1,0:T(8,128)(2,1)S(1)} collective-permute-done((bf16[384,1536]{1,0:T(8,128)(2,1)S(1)}, bf16[384,1536]{1,0:T(8,128)(2,1)S(1)}, u32[]{:S(2)}, u32[]{:S(2)}) %collective-permute-start.8) | collective-permute-done | bytes 1179680 | tf_op jit(solution)/shard_map/ppermute | solution.py:42
  82.2 3.9 collective-permute-start.14
  108.6 4.1 collective-permute-done.3
  120.4 20.8 %shard_map.221 = (f32[256,1536]{1,0:T(8,128)}, bf16[256,1536]{1,0:T(8,128)(2,1)S(1)}, bf16[256,1536]{1,0:T(8,128)(2,1)S(1)}, bf16[256,1536]{1,0:T(8,128)(2,1)S(1)}, f32[256,1536]{1,0:T(8,128)}) custom-call(bf16[256,1536]{1,0:T(8,128)(2,1)S(1)} %get-tuple-element.164.x, bf16[256,1536]{1,0:T(8,128)(2,1)S(1)} %fusion.33.normed, ...), custom_call_target="tpu_custom_call" | custom-call | flops 99999997952 | bytes 20000000 | tf_op jit(solution)/shard_map/pallas_call | solution.py:517
  143.9 12.4 %collective-permute-done.16.refs_3_ = bf16[576,1536]{1,0:T(8,128)(2,1)} collective-permute-done((bf16[576,1536]{1,0:T(8,128)(2,1)S(1)}, bf16[576,1536]{1,0:T(8,128)(2,1)}, u32[]{:S(2)}, u32[]{:S(2)}) %collective-permute-start.16) | collective-permute-done | bytes 1769504 | tf_op jit(solution)/shard_map/ppermute | solution.py:42
  156.4 38.1 %collective-permute-done.17.refs_4_ = bf16[576,1536]{1,0:T(8,128)(2,1)} collective-permute-done((bf16[576,1536]{1,0:T(8,128)(2,1)S(1)}, bf16[576,1536]{1,0:T(8,128)(2,1)}, u32[]{:S(2)}, u32[]{:S(2)}) %collective-permute-start.17) | collective-permute-done | bytes 1769504 | tf_op jit(solution)/shard_map/ppermute | solution.py:42
  206.5 113.9 %shard_map.222 = (f32[256,1536]{1,0:T(8,128)S(1)}, bf16[4,256,1536]{2,1,0:T(8,128)(2,1)}, bf16[4,256,1536]{2,1,0:T(8,128)(2,1)}, bf16[4,256,1536]{2,1,0:T(8,128)(2,1)}, bf16[4,256,1536]{2,1,0:T(8,128)(2,1)}) custom-call(bf16[256,1536]{1,0:T(8,128)(2,1)S(1)} %copy-done.31, f32[2,4,256,128]{3,2,1,0:T(8,128)S(1)} %broadcast_in_dim.97.refs_1_, ...), custom_call_target="tpu_custom_call" | custom-call | flops 399999991808 | bytes 100000000 | tf_op jit(solution)/shard_map/pallas_call | solution.py:389
  321.5 8.7 collective-permute-done.24.refs_4_
  363.1 20.7 %shard_map.223 = (f32[256,1536]{1,0:T(8,128)}, bf16[256,1536]{1,0:T(8,128)(2,1)S(1)}, bf16[256,1536]{1,0:T(8,128)(2,1)S(1)}, bf16[256,1536]{1,0:T(8,128)(2,1)S(1)}, f32[256,1536]{1,0:T(8,128)}) custom-call(bf16[256,1536]{1,0:T(8,128)(2,1)S(1)} %get-tuple-element.160.x, bf16[256,1536]{1,0:T(8,128)(2,1)S(1)} %fusion.43.normed, ...), custom_call_target="tpu_custom_call" | custom-call | flops 99999997952 | bytes 20000000 | tf_op jit(solution)/shard_map/pallas_call | solution.py:517
  384.2 130.0 %shard_map.224 = (f32[256,1536]{1,0:T(8,128)S(1)}, bf16[4,256,1536]{2,1,0:T(8,128)(2,1)}, bf16[4,3,192,1536]{3,2,1,0:T(8,128)(2,1)}, bf16[4,3,192,1536]{3,2,1,0:T(8,128)(2,1)}) custom-call(bf16[256,1536]{1,0:T(8,128)(2,1)S(1)} %get-tuple-element.82.refs_0_, f32[2,4,256,128]{3,2,1,0:T(8,128)S(1)} %broadcast_in_dim.99.refs_1_, ...), custom_call_target="tpu_custom_call" | custom-call | flops 399999991808 | bytes 100000000 | tf_op jit(solution)/shard_map/pallas_call | solution.py:389
  515.3 24.4 %shard_map.225 = (f32[256,1536]{1,0:T(8,128)}, bf16[256,1536]{1,0:T(8,128)(2,1)S(1)}, bf16[1024,512]{1,0:T(8,128)(2,1)S(1)}, bf16[1536,1536]{1,0:T(8,128)(2,1)}, f32[1,1536]{1,0:T(1,128)S(1)}) custom-call(f32[256,1536]{1,0:T(8,128)} %get-tuple-element.162.grad, f32[256,1536]{1,0:T(8,128)} %copy-done.25, f32[256,1536]{1,0:T(8,128)} %get-tuple-element.81.hidden, ...), custom_call_target="tpu_custom_call" | custom-call | flops 99999997952 | bytes 20000000 | tf_op jit(solution)/shard_map/pallas_call | solution.py:517
  560.9 4.3 broadcast_select_fusion.2
  567.6 7.3 collective-permute-done.37
  578.3 4.2 reduce-precision_convert_fusion.9
  593.7 113.7 %shard_map.226 = (f32[256,1536]{1,0:T(8,128)S(1)}, bf16[4,3,192,1536]{3,2,1,0:T(8,128)(2,1)}, bf16[4,3,192,1536]{3,2,1,0:T(8,128)(2,1)}) custom-call(bf16[256,1536]{1,0:T(8,128)(2,1)S(1)} %fusion.49.refs_0_, f32[2,4,256,128]{3,2,1,0:T(8,128)S(1)} %copy-done.13, bf16[576,1536]{1,0:T(8,128)(2,1)S(1)} %bitcast.223, ...), custom_call_target="tpu_custom_call" | custom-call | flops 399999991808 | bytes 100000000 | tf_op jit(solution)/shard_map/pallas_call | solution.py:389
  708.8 22.2 %collective-permute-done.39 = bf16[1040,1536]{1,0:T(8,128)(2,1)} collective-permute-done((bf16[1040,1536]{1,0:T(8,128)(2,1)}, bf16[1040,1536]{1,0:T(8,128)(2,1)}, u32[]{:S(2)}, u32[]{:S(2)}) %collective-permute-start.39) | collective-permute-done | bytes 3194912 | tf_op jit(solution)/shard_map/ppermute | solution.py:42
  731.0 8.0 reduce-precision_convert_fusion.2
  745.0 24.6 %shard_map.227 = (f32[256,1536]{1,0:T(8,128)}, bf16[256,1536]{1,0:T(8,128)(2,1)S(1)}, bf16[1024,512]{1,0:T(8,128)(2,1)S(1)}, bf16[1536,1536]{1,0:T(8,128)(2,1)}, f32[1,1536]{1,0:T(1,128)S(1)}) custom-call(f32[256,1536]{1,0:T(8,128)} %convert_element_type.529.grad, f32[256,1536]{1,0:T(8,128)} %copy-done.24, f32[256,1536]{1,0:T(8,128)} %get-tuple-element.67.hidden, ...), custom_call_target="tpu_custom_call" | custom-call | flops 99999997952 | bytes 20000000 | tf_op jit(solution)/shard_map/pallas_call | solution.py:517
  779.8 4.7 collective-permute-done.43
  795.0 4.4 broadcast_select_fusion
  808.1 7.0 broadcast_select_fusion.1
  815.2 5.9 fusion.57
  824.7 6.1 fusion.31
  833.4 23.1 %collective-permute-done.49 = bf16[464,1536]{1,0:T(8,128)(2,1)} collective-permute-done((bf16[464,1536]{1,0:T(8,128)(2,1)}, bf16[464,1536]{1,0:T(8,128)(2,1)}, u32[]{:S(2)}, u32[]{:S(2)}) %collective-permute-start.49) | collective-permute-done | bytes 1425440 | tf_op jit(solution)/shard_map/ppermute | solution.py:42
  856.5 29.6 %collective-permute-done.48 = bf16[464,1536]{1,0:T(8,128)(2,1)} collective-permute-done((bf16[464,1536]{1,0:T(8,128)(2,1)}, bf16[464,1536]{1,0:T(8,128)(2,1)}, u32[]{:S(2)}, u32[]{:S(2)}) %collective-permute-start.48) | collective-permute-done | bytes 1425440 | tf_op jit(solution)/shard_map/ppermute | solution.py:42
  886.1 5.1 fusion.9
  899.7 53.2 %all-reduce.5.cloned.1.call-done = bf16[464,1536]{1,0:T(8,128)(2,1)} async-done(((bf16[464,1536]{1,0:T(8,128)(2,1)}), bf16[464,1536]{1,0:T(8,128)(2,1)}) %all-reduce.5.cloned.1.call-update) | async-done | bytes 1425424 | tf_op jit(solution)/shard_map/psum | solution.py:731
  957.1 17.4 %collective-permute-done.56 = bf16[3,192,1536]{2,1,0:T(8,128)(2,1)} collective-permute-done((bf16[3,192,1536]{2,1,0:T(8,128)(2,1)}, bf16[3,192,1536]{2,1,0:T(8,128)(2,1)}, u32[]{:S(2)}, u32[]{:S(2)}) %collective-permute-start.56) | collective-permute-done | bytes 1769504 | tf_op jit(solution)/shard_map/ppermute | solution.py:42
  974.5 5.7 broadcast_select_fusion.4
  993.0 3.9 collective-permute-done.53
  996.8 10.1 collective-permute-done.52
  (514 shorter events, 228.7 us)
Async XLA Ops:
  7.2 107.6 %all-gather.2.cloned.1.call-start = ((), (), s32[]{:S(2)}) async-start(), calls=%async_computation.1 | async-start | bytes 3932160 | tf_op jit(solution)/shard_map/all_gather | solution.py:552
  7.2 74.1 %collective-permute-start = (f32[1,1536]{1,0:T(1,128)}, f32[1,1536]{1,0:T(1,128)S(1)}, u32[]{:S(2)}, u32[]{:S(2)}) collective-permute-start(f32[1,1536]{1,0:T(1,128)} %param.19), channel_id=1, source_target_pairs={{0,16},{16,0},{1,17},{17,1},{2,18},{18,2},{3,19},{19,3},{4,20},{20... | collective-permute-start | bytes 18440 | tf_op jit(solution)/shard_map/ppermute | solution.py:27
  12.2 79.2 %collective-permute-start.1 = (bf16[1536,512]{1,0:T(8,128)(2,1)}, bf16[1536,512]{1,0:T(8,128)(2,1)}, u32[]{:S(2)}, u32[]{:S(2)}) collective-permute-start(bf16[1536,512]{1,0:T(8,128)(2,1)} %pad_maximum_fusion.10), channel_id=1, source_target_pairs={{0,16},{16,0},{1,17},{17,1},{2,18},{18,2},{3,19},{19,3},{4,20},{20... | collective-permute-start | bytes 4718600 | tf_op jit(solution)/shard_map/ppermute | solution.py:27
  15.7 815.1 %reduce-scatter.2.cloned.1.call-start = ((), (), s32[]{:S(2)}) async-start(), calls=%async_computation.2 | async-start | bytes 3932160 | tf_op jit(solution)/shard_map/reduce_scatter | solution.py:556
  18.9 30.4 %collective-permute-start.9 = (bf16[384,1536]{1,0:T(8,128)(2,1)S(1)}, bf16[384,1536]{1,0:T(8,128)(2,1)S(1)}, u32[]{:S(2)}, u32[]{:S(2)}) collective-permute-start(bf16[384,1536]{1,0:T(8,128)(2,1)S(1)} %get-tuple-element.192), channel_id=1, source_target_pairs={{0,3},{1,2},{2,1},{3,0},{4,7},{5,6},{6,5},{7,4},{8,11},{9,10},{10,... | collective-permute-start | bytes 3538952 | tf_op jit(solution)/shard_map/ppermute | solution.py:42
  22.4 51.8 %collective-permute-start.8 = (bf16[384,1536]{1,0:T(8,128)(2,1)S(1)}, bf16[384,1536]{1,0:T(8,128)(2,1)S(1)}, u32[]{:S(2)}, u32[]{:S(2)}) collective-permute-start(bf16[384,1536]{1,0:T(8,128)(2,1)S(1)} %get-tuple-element.192), channel_id=1, source_target_pairs={{0,2},{1,3},{2,0},{3,1},{4,6},{5,7},{6,4},{7,5},{8,10},{9,11},{10,... | collective-permute-start | bytes 3538952 | tf_op jit(solution)/shard_map/ppermute | solution.py:42
  22.9 51.6 %collective-permute-start.7 = (bf16[384,1536]{1,0:T(8,128)(2,1)S(1)}, bf16[384,1536]{1,0:T(8,128)(2,1)S(1)}, u32[]{:S(2)}, u32[]{:S(2)}) collective-permute-start(bf16[384,1536]{1,0:T(8,128)(2,1)S(1)} %get-tuple-element.192), channel_id=1, source_target_pairs={{0,1},{1,0},{2,3},{3,2},{4,5},{5,4},{6,7},{7,6},{8,9},{9,8},{10,11... | collective-permute-start | bytes 3538952 | tf_op jit(solution)/shard_map/ppermute | solution.py:42
  49.3 36.8 %collective-permute-start.5 = (f32[1,1536]{1,0:T(1,128)S(1)}, f32[1,1536]{1,0:T(1,128)S(1)}, u32[]{:S(2)}, u32[]{:S(2)}) collective-permute-start(f32[1,1536]{1,0:T(1,128)S(1)} %copy-done.110), channel_id=1, source_target_pairs={{0,16},{16,0},{1,17},{17,1},{2,18},{18,2},{3,19},{19,3},{4,20},{20... | collective-permute-start | bytes 18440 | tf_op jit(solution)/shard_map/ppermute | solution.py:27
  77.2 41.1 %collective-permute-start.10 = (bf16[1536,1536]{1,0:T(8,128)(2,1)}, bf16[1536,1536]{1,0:T(8,128)(2,1)}, u32[]{:S(2)}, u32[]{:S(2)}) collective-permute-start(bf16[1536,1536]{1,0:T(8,128)(2,1)} %pad_maximum_fusion.mine), channel_id=1, source_target_pairs={{0,16},{16,0},{1,17},{17,1},{2,18},{18,2},{3,19},{19,3},{4,20},{20... | collective-permute-start | bytes 14155784 | tf_op jit(solution)/shard_map/ppermute | solution.py:27
  114.8 41.6 %collective-permute-start.16 = (bf16[576,1536]{1,0:T(8,128)(2,1)S(1)}, bf16[576,1536]{1,0:T(8,128)(2,1)}, u32[]{:S(2)}, u32[]{:S(2)}) collective-permute-start(bf16[576,1536]{1,0:T(8,128)(2,1)S(1)} %bitcast.218), channel_id=1, source_target_pairs={{0,1},{1,0},{2,3},{3,2},{4,5},{5,4},{6,7},{7,6},{8,9},{9,8},{10,11... | collective-permute-start | bytes 5308424 | tf_op jit(solution)/shard_map/ppermute | solution.py:42
  116.2 78.3 %collective-permute-start.17 = (bf16[576,1536]{1,0:T(8,128)(2,1)S(1)}, bf16[576,1536]{1,0:T(8,128)(2,1)}, u32[]{:S(2)}, u32[]{:S(2)}) collective-permute-start(bf16[576,1536]{1,0:T(8,128)(2,1)S(1)} %bitcast.219), channel_id=1, source_target_pairs={{0,2},{1,3},{2,0},{3,1},{4,6},{5,7},{6,4},{7,5},{8,10},{9,11},{10,... | collective-permute-start | bytes 5308424 | tf_op jit(solution)/shard_map/ppermute | solution.py:42
  117.0 77.5 %collective-permute-start.18 = (bf16[576,1536]{1,0:T(8,128)(2,1)S(1)}, bf16[576,1536]{1,0:T(8,128)(2,1)}, u32[]{:S(2)}, u32[]{:S(2)}) collective-permute-start(bf16[576,1536]{1,0:T(8,128)(2,1)S(1)} %bitcast.220), channel_id=1, source_target_pairs={{0,3},{1,2},{2,1},{3,0},{4,7},{5,6},{6,5},{7,4},{8,11},{9,10},{10,... | collective-permute-start | bytes 5308424 | tf_op jit(solution)/shard_map/ppermute | solution.py:42
  199.8 121.7 %collective-permute-start.23 = (bf16[960,1536]{1,0:T(8,128)(2,1)}, bf16[960,1536]{1,0:T(8,128)(2,1)}, u32[]{:S(2)}, u32[]{:S(2)}) collective-permute-start(bf16[960,1536]{1,0:T(8,128)(2,1)} %pad_maximum_fusion.8.refs_2_), channel_id=1, source_target_pairs={{0,1},{1,0},{2,3},{3,2},{4,5},{5,4},{6,7},{7,6},{8,9},{9,8},{10,11... | collective-permute-start | bytes 8847368 | tf_op jit(solution)/shard_map/ppermute | solution.py:42
  200.8 129.4 %collective-permute-start.24 = (bf16[960,1536]{1,0:T(8,128)(2,1)}, bf16[960,1536]{1,0:T(8,128)(2,1)}, u32[]{:S(2)}, u32[]{:S(2)}) collective-permute-start(bf16[960,1536]{1,0:T(8,128)(2,1)} %pad_maximum_fusion.8.refs_2_), channel_id=1, source_target_pairs={{0,2},{1,3},{2,0},{3,1},{4,6},{5,7},{6,4},{7,5},{8,10},{9,11},{10,... | collective-permute-start | bytes 8847368 | tf_op jit(solution)/shard_map/ppermute | solution.py:42
  201.9 128.3 %collective-permute-start.25 = (bf16[960,1536]{1,0:T(8,128)(2,1)}, bf16[960,1536]{1,0:T(8,128)(2,1)}, u32[]{:S(2)}, u32[]{:S(2)}) collective-permute-start(bf16[960,1536]{1,0:T(8,128)(2,1)} %pad_maximum_fusion.8.refs_2_), channel_id=1, source_target_pairs={{0,3},{1,2},{2,1},{3,0},{4,7},{5,6},{6,5},{7,4},{8,11},{9,10},{10,... | collective-permute-start | bytes 8847368 | tf_op jit(solution)/shard_map/ppermute | solution.py:42
  543.3 35.0 %collective-permute-start.36 = (bf16[4,3,192,1536]{3,2,1,0:T(8,128)(2,1)}, bf16[4,3,192,1536]{3,2,1,0:T(8,128)(2,1)}, u32[]{:S(2)}, u32[]{:S(2)}) collective-permute-start(bf16[4,3,192,1536]{3,2,1,0:T(8,128)(2,1)} %get-tuple-element.91), channel_id=1, source_target_pairs={{0,16},{16,0},{1,17},{17,1},{2,18},{18,2},{3,19},{19,3},{4,20},{20... | collective-permute-start | bytes 21233672 | tf_op jit(solution)/shard_map/ppermute | solution.py:27
  590.2 118.7 %collective-permute-start.40 = (bf16[1040,1536]{1,0:T(8,128)(2,1)}, bf16[1040,1536]{1,0:T(8,128)(2,1)}, u32[]{:S(2)}, u32[]{:S(2)}) collective-permute-start(bf16[1040,1536]{1,0:T(8,128)(2,1)} %pad_maximum_fusion.7), channel_id=1, source_target_pairs={{0,3},{1,2},{2,1},{3,0},{4,7},{5,6},{6,5},{7,4},{8,11},{9,10},{10,... | collective-permute-start | bytes 9584648 | tf_op jit(solution)/shard_map/ppermute | solution.py:42
  591.5 139.5 %collective-permute-start.39 = (bf16[1040,1536]{1,0:T(8,128)(2,1)}, bf16[1040,1536]{1,0:T(8,128)(2,1)}, u32[]{:S(2)}, u32[]{:S(2)}) collective-permute-start(bf16[1040,1536]{1,0:T(8,128)(2,1)} %pad_maximum_fusion.6), channel_id=1, source_target_pairs={{0,2},{1,3},{2,0},{3,1},{4,6},{5,7},{6,4},{7,5},{8,10},{9,11},{10,... | collective-permute-start | bytes 9584648 | tf_op jit(solution)/shard_map/ppermute | solution.py:42
  592.9 138.1 %collective-permute-start.38 = (bf16[1040,1536]{1,0:T(8,128)(2,1)}, bf16[1040,1536]{1,0:T(8,128)(2,1)}, u32[]{:S(2)}, u32[]{:S(2)}) collective-permute-start(bf16[1040,1536]{1,0:T(8,128)(2,1)} %pad_maximum_fusion.5), channel_id=1, source_target_pairs={{0,1},{1,0},{2,3},{3,2},{4,5},{5,4},{6,7},{7,6},{8,9},{9,8},{10,11... | collective-permute-start | bytes 9584648 | tf_op jit(solution)/shard_map/ppermute | solution.py:42
  708.8 115.8 %collective-permute-start.54 = (bf16[4,3,192,1536]{3,2,1,0:T(8,128)(2,1)}, bf16[4,3,192,1536]{3,2,1,0:T(8,128)(2,1)}, u32[]{:S(2)}, u32[]{:S(2)}) collective-permute-start(bf16[4,3,192,1536]{3,2,1,0:T(8,128)(2,1)} %get-tuple-element.118), channel_id=1, source_target_pairs={{0,16},{16,0},{1,17},{17,1},{2,18},{18,2},{3,19},{19,3},{4,20},{20... | collective-permute-start | bytes 21233672 | tf_op jit(solution)/shard_map/ppermute | solution.py:27
  741.0 150.2 %all-reduce.3.cloned.1.call-start = ((), (), s32[]{:S(2)}) async-start(), calls=%async_computation.3 | async-start | bytes 2850816 | tf_op jit(solution)/shard_map/psum | solution.py:726
  804.4 148.5 %all-reduce.5.cloned.1.call-start = ((), (), s32[]{:S(2)}) async-start(), calls=%async_computation.4 | async-start | bytes 2850816 | tf_op jit(solution)/shard_map/psum | solution.py:731
  808.1 84.8 %collective-permute-start.45 = (bf16[256,1536]{1,0:T(8,128)(2,1)}, bf16[256,1536]{1,0:T(8,128)(2,1)}, u32[]{:S(2)}, u32[]{:S(2)}) collective-permute-start(bf16[256,1536]{1,0:T(8,128)(2,1)} %get-tuple-element.153), channel_id=1, source_target_pairs={{0,16},{16,0},{1,17},{17,1},{2,18},{18,2},{3,19},{19,3},{4,20},{20... | collective-permute-start | bytes 2359304 | tf_op jit(solution)/shard_map/ppermute | solution.py:27
  821.1 35.4 %collective-permute-start.49 = (bf16[464,1536]{1,0:T(8,128)(2,1)}, bf16[464,1536]{1,0:T(8,128)(2,1)}, u32[]{:S(2)}, u32[]{:S(2)}) collective-permute-start(bf16[464,1536]{1,0:T(8,128)(2,1)} %get-tuple-element.174), channel_id=1, source_target_pairs={{0,3},{1,2},{2,1},{3,0},{4,7},{5,6},{6,5},{7,4},{8,11},{9,10},{10,... | collective-permute-start | bytes 4276232 | tf_op jit(solution)/shard_map/ppermute | solution.py:42
  822.9 63.2 %collective-permute-start.48 = (bf16[464,1536]{1,0:T(8,128)(2,1)}, bf16[464,1536]{1,0:T(8,128)(2,1)}, u32[]{:S(2)}, u32[]{:S(2)}) collective-permute-start(bf16[464,1536]{1,0:T(8,128)(2,1)} %get-tuple-element.175), channel_id=1, source_target_pairs={{0,2},{1,3},{2,0},{3,1},{4,6},{5,7},{6,4},{7,5},{8,10},{9,11},{10,... | collective-permute-start | bytes 4276232 | tf_op jit(solution)/shard_map/ppermute | solution.py:42
  823.8 62.2 %collective-permute-start.47 = (bf16[464,1536]{1,0:T(8,128)(2,1)}, bf16[464,1536]{1,0:T(8,128)(2,1)}, u32[]{:S(2)}, u32[]{:S(2)}) collective-permute-start(bf16[464,1536]{1,0:T(8,128)(2,1)} %get-tuple-element.173), channel_id=1, source_target_pairs={{0,1},{1,0},{2,3},{3,2},{4,5},{5,4},{6,7},{7,6},{8,9},{9,8},{10,11... | collective-permute-start | bytes 4276232 | tf_op jit(solution)/shard_map/ppermute | solution.py:42
  894.2 60.3 %collective-permute-start.41 = (bf16[256,1536]{1,0:T(8,128)(2,1)}, bf16[256,1536]{1,0:T(8,128)(2,1)}, u32[]{:S(2)}, u32[]{:S(2)}) collective-permute-start(bf16[256,1536]{1,0:T(8,128)(2,1)} %get-tuple-element.155), channel_id=1, source_target_pairs={{0,16},{16,0},{1,17},{17,1},{2,18},{18,2},{3,19},{19,3},{4,20},{20... | collective-permute-start | bytes 2359304 | tf_op jit(solution)/shard_map/ppermute | solution.py:27
  894.3 62.8 %collective-permute-start.57 = (bf16[3,192,1536]{2,1,0:T(8,128)(2,1)}, bf16[3,192,1536]{2,1,0:T(8,128)(2,1)}, u32[]{:S(2)}, u32[]{:S(2)}) collective-permute-start(bf16[3,192,1536]{2,1,0:T(8,128)(2,1)} %get-tuple-element.122), channel_id=1, source_target_pairs={{0,3},{1,2},{2,1},{3,0},{4,7},{5,6},{6,5},{7,4},{8,11},{9,10},{10,... | collective-permute-start | bytes 5308424 | tf_op jit(solution)/shard_map/ppermute | solution.py:42
  896.1 78.3 %collective-permute-start.56 = (bf16[3,192,1536]{2,1,0:T(8,128)(2,1)}, bf16[3,192,1536]{2,1,0:T(8,128)(2,1)}, u32[]{:S(2)}, u32[]{:S(2)}) collective-permute-start(bf16[3,192,1536]{2,1,0:T(8,128)(2,1)} %get-tuple-element.121), channel_id=1, source_target_pairs={{0,2},{1,3},{2,0},{3,1},{4,6},{5,7},{6,4},{7,5},{8,10},{9,11},{10,... | collective-permute-start | bytes 5308424 | tf_op jit(solution)/shard_map/ppermute | solution.py:42
  897.1 77.4 %collective-permute-start.55 = (bf16[3,192,1536]{2,1,0:T(8,128)(2,1)}, bf16[3,192,1536]{2,1,0:T(8,128)(2,1)}, u32[]{:S(2)}, u32[]{:S(2)}) collective-permute-start(bf16[3,192,1536]{2,1,0:T(8,128)(2,1)} %get-tuple-element.120), channel_id=1, source_target_pairs={{0,1},{1,0},{2,3},{3,2},{4,5},{5,4},{6,7},{7,6},{8,9},{9,8},{10,11... | collective-permute-start | bytes 5308424 | tf_op jit(solution)/shard_map/ppermute | solution.py:42
  954.4 25.8 %collective-permute-start.50 = (bf16[464,1536]{1,0:T(8,128)(2,1)S(1)}, bf16[464,1536]{1,0:T(8,128)(2,1)S(1)}, u32[]{:S(2)}, u32[]{:S(2)}) collective-permute-start(bf16[464,1536]{1,0:T(8,128)(2,1)S(1)} %broadcast_select_fusion.10), channel_id=1, source_target_pairs={{0,16},{16,0},{1,17},{17,1},{2,18},{18,2},{3,19},{19,3},{4,20},{20... | collective-permute-start | bytes 4276232 | tf_op jit(solution)/shard_map/ppermute | solution.py:27
  980.2 38.0 %collective-permute-start.58 = (bf16[3,192,1536]{2,1,0:T(8,128)(2,1)}, bf16[3,192,1536]{2,1,0:T(8,128)(2,1)}, u32[]{:S(2)}, u32[]{:S(2)}) collective-permute-start(bf16[3,192,1536]{2,1,0:T(8,128)(2,1)} %get-tuple-element.151), channel_id=1, source_target_pairs={{0,16},{16,0},{1,17},{17,1},{2,18},{18,2},{3,19},{19,3},{4,20},{20... | collective-permute-start | bytes 5308424 | tf_op jit(solution)/shard_map/ppermute | solution.py:27
  (155 other events, 2470.4 us)
Sparse Core Ops, SparseCore 0:
  15.8 65.9 all-gather.1
  741.1 57.3 reduce-scatter.1
  804.5 61.4 all-reduce.2
  891.3 61.4 all-reduce.4
